TPU v7x, 128 devices: a whole 4x4x4 slice. The times are simulated.
128 devices in a mesh: ctx: 32 (over z, y_lo, x), wsh: 4 (over y_hi, core).
Axes of the slice: x: 4, y: 4 (y_hi: 2, y_lo: 2; y = y_hi * 2 + y_lo), z: 4, core: 2. Of those that a mesh axis runs over, the one named last changes fastest.
Arguments:
- tokens: bfloat16 [4, 8192, 768], P('wsh', 'ctx'), may hold values from -6 to 6
- cotangent: bfloat16 [4, 8192, 768], P('wsh', 'ctx'), may hold values from -6 to 6
- pairing: int32 [32], replicated, may hold values from 0 to 31, each once
- first_gain: bfloat16 [768], P('wsh'), may hold values from 0.5 to 1.5
- first_shift: bfloat16 [768], P('wsh'), may hold values from -4 to 4
- qkv_weight: bfloat16 [768, 2304], P('wsh'), may hold values from -0.3125 to 0.3125
- qkv_bias: bfloat16 [2304], P('wsh'), may hold values from -4 to 4
- dense_weight: bfloat16 [768, 768], P('wsh'), may hold values from -1.25 to 1.25
- second_gain: bfloat16 [768], P('wsh'), may hold values from 0.5 to 1.5
- second_shift: bfloat16 [768], P('wsh'), may hold values from -4 to 4
- up_weight: bfloat16 [768, 3072], P('wsh'), may hold values from -0.21875 to 0.21875
- up_bias: bfloat16 [3072], P('wsh'), may hold values from -6 to 6
- down_weight: bfloat16 [3072, 768], P('wsh'), may hold values from -0.109375 to 0.109375
- out_bias: bfloat16 [768], P('wsh'), may hold values from -6 to 6
Outputs:
- layer_output: bfloat16 [4, 8192, 768], P('wsh', 'ctx')
- input_grad: bfloat16 [4, 8192, 768], P('wsh', 'ctx')
- first_gain_grad: float32 [768], P('wsh')
- first_shift_grad: float32 [768], P('wsh')
- qkv_weight_grad: float32 [768, 2304], P('wsh')
- qkv_bias_grad: float32 [2304], P('wsh')
- dense_weight_grad: float32 [768, 768], P('wsh')
- second_gain_grad: float32 [768], P('wsh')
- second_shift_grad: float32 [768], P('wsh')
- up_weight_grad: float32 [768, 3072], P('wsh')
- up_bias_grad: float32 [3072], P('wsh')
- down_weight_grad: float32 [3072, 768], P('wsh')
- out_bias_grad: float32 [768], P('wsh')
All inputs are finite; a program needn't handle non-finite values.
Results may differ from a plain program's by a relative error of at most 0.03.
Values may be sent and summed in bfloat16 or wider, within the bound.
A program may use at most 320 MiB of HBM per device.

v0:
```python
import jax
import jax.numpy as jnp
from jax import lax
from jax.sharding import PartitionSpec as P

D = 768
HEADS = 12
HD = 64
ROT = 16
TOK_DEV = 256
BLK = 128


def for_sending(array):

    def short(part):
        return part.astype(jnp.bfloat16) if part.dtype == jnp.float32 else part

    return jax.tree.map(short, array)


def layer_norm(values, norm_gain, norm_shift):
    row_mean = jnp.mean(values, -1, keepdims=True)
    centered = values - row_mean
    row_var = jnp.mean(centered * centered, -1, keepdims=True)
    return centered * lax.rsqrt(row_var + 1e-05) * norm_gain + norm_shift


def rotate(tensor, cosine, sine_table):
    half_dims = ROT // 2
    lower_part = tensor[..., :half_dims]
    upper_part = tensor[..., half_dims:ROT]
    turned = jnp.concatenate([-upper_part, lower_part], -1)
    moved = tensor[..., :ROT] * cosine + turned * sine_table
    return jnp.concatenate([moved, tensor[..., ROT:]], -1)


def rotary_tables(positions):
    half_dims = ROT // 2
    exponents = jnp.arange(half_dims).astype(jnp.float32) * 2.0 / ROT
    inverse = 10000.0 ** (-exponents)
    angles = positions.astype(jnp.float32)[:, None] * inverse[None, :]
    angles = jnp.concatenate([angles, angles], -1)[:, None, :]
    return (jnp.cos(angles), jnp.sin(angles))


def contract(left_side, right_side, left_dim, right_dim):
    return lax.dot_general(
        left_side,
        right_side,
        (((left_dim,), (right_dim,)), ((), ())),
        preferred_element_type=jnp.float32,
    )


def gelu_exact(values):
    return jax.nn.gelu(values, approximate=False)


def on_device(
    tokens,
    cotangent,
    pairing,
    first_gain,
    first_shift,
    qkv_weight,
    qkv_bias,
    dense_weight,
    second_gain,
    second_shift,
    up_weight,
    up_bias,
    down_weight,
    out_bias,
):
    total_blocks = 2 * lax.axis_size("ctx")
    group_size = max(1, min(512 // BLK, total_blocks))
    tile_rows = group_size * BLK
    offsets = jnp.arange(BLK, dtype=jnp.int32)
    ctx_index = lax.axis_index("ctx")
    seq_of_layout = jnp.stack([pairing, total_blocks - 1 - pairing], 1).reshape(-1)
    layout_of_seq = (
        jnp.zeros((total_blocks,), jnp.int32)
        .at[seq_of_layout]
        .set(jnp.arange(total_blocks, dtype=jnp.int32))
    )
    own_blocks = lax.dynamic_slice(seq_of_layout, (2 * ctx_index,), (2,))
    local_pos = (own_blocks[:, None] * BLK + offsets[None, :]).reshape(-1)
    cosine, sine_table = rotary_tables(local_pos)
    query_scale = HD ** (-0.5)

    def turn_queries(tensor):
        return rotate(tensor, cosine, sine_table) * query_scale

    def turn_keys(tensor):
        return rotate(tensor, cosine, sine_table)

    shards = (
        first_gain,
        first_shift,
        qkv_weight,
        qkv_bias,
        dense_weight,
        second_gain,
        second_shift,
        up_weight,
        up_bias,
        down_weight,
        out_bias,
    )
    gathered = (
        lax.all_gather(shards[0], "wsh", axis=0, tiled=True),
        lax.all_gather(shards[1], "wsh", axis=0, tiled=True),
        lax.all_gather(shards[2], "wsh", axis=0, tiled=True),
        lax.all_gather(shards[3], "wsh", axis=0, tiled=True),
        lax.all_gather(shards[4], "wsh", axis=0, tiled=True),
        lax.all_gather(shards[5], "wsh", axis=0, tiled=True),
        lax.all_gather(shards[6], "wsh", axis=0, tiled=True),
        lax.all_gather(shards[7], "wsh", axis=0, tiled=True),
        lax.all_gather(shards[8], "wsh", axis=0, tiled=True),
        lax.all_gather(shards[9], "wsh", axis=0, tiled=True),
        lax.all_gather(shards[10], "wsh", axis=0, tiled=True),
    )
    (
        gain_one,
        shift_one,
        qkv_matrix,
        qkv_offset,
        dense_matrix,
        gain_two,
        shift_two,
        up_matrix,
        up_offset,
        down_matrix,
        out_offset,
    ) = gathered
    inputs = tokens[0].astype(jnp.float32)
    normed_one = layer_norm(
        inputs, gain_one.astype(jnp.float32), shift_one.astype(jnp.float32)
    ).astype(jnp.bfloat16)
    mixed_rows = jnp.dot(
        normed_one, qkv_matrix, preferred_element_type=jnp.float32
    ) + qkv_offset.astype(jnp.float32)
    query_raw = mixed_rows[:, :D].reshape(TOK_DEV, HEADS, HD)
    key_raw = mixed_rows[:, D : 2 * D].reshape(TOK_DEV, HEADS, HD)
    queries = turn_queries(query_raw).astype(jnp.bfloat16)
    key_rows = turn_keys(key_raw).astype(jnp.bfloat16)
    value_rows = mixed_rows[:, 2 * D :].astype(jnp.bfloat16)
    all_keys, all_values = (
        lax.all_gather(key_rows.reshape(TOK_DEV, D), "ctx", axis=0, tiled=True),
        lax.all_gather(value_rows, "ctx", axis=0, tiled=True),
    )
    key_stack = all_keys.reshape(total_blocks, BLK, HEADS, HD)
    value_stack = all_values.reshape(total_blocks, BLK, HEADS, HD)

    def pick_tile(tile_index):
        wanted = tile_index * group_size + jnp.arange(group_size, dtype=jnp.int32)
        chosen = layout_of_seq[jnp.minimum(wanted, total_blocks - 1)]
        tile_pos = (wanted[:, None] * BLK + offsets[None, :]).reshape(-1)
        return (wanted, chosen, tile_pos)

    query_blocks = queries.reshape(2, BLK, HEADS, HD)
    pos_blocks = local_pos.reshape(2, BLK)
    tile_totals = (own_blocks + group_size) // group_size
    log_totals = []
    attended_parts = []
    for slot_index in range(2):
        attend_query_block = query_blocks[slot_index]
        attend_query_pos = pos_blocks[slot_index]
        tile_total = tile_totals[slot_index]

        def tile_scores(tile_index):
            wanted, chosen, key_pos = pick_tile(tile_index)
            key_tile = key_stack[chosen].reshape(tile_rows, HEADS, HD)
            allowed = key_pos[None, :] <= attend_query_pos[:, None]
            scores = jnp.einsum(
                "qhd,khd->hqk", attend_query_block, key_tile, preferred_element_type=jnp.float32
            )
            return (scores, allowed, chosen)

        def stats_step(tile_index, running):
            row_max, row_total = running
            scores, allowed, chosen = tile_scores(tile_index)
            scores = jnp.where(allowed[None], scores, -jnp.inf)
            new_max = jnp.maximum(row_max, jnp.max(scores, -1))
            row_total = row_total * jnp.exp(row_max - new_max) + jnp.sum(
                jnp.exp(scores - new_max[..., None]), -1
            )
            return (new_max, row_total)

        initial = (
            jnp.full((HEADS, BLK), -jnp.inf, jnp.float32),
            jnp.zeros((HEADS, BLK), jnp.float32),
        )
        row_max, row_total = lax.fori_loop(0, tile_total, stats_step, initial)
        log_total = row_max + jnp.log(row_total)

        def value_step(tile_index, accumulated):
            scores, allowed, chosen = tile_scores(tile_index)
            value_tile = value_stack[chosen].reshape(tile_rows, HEADS, HD)
            weights_tile = jnp.where(
                allowed[None], jnp.exp(scores - log_total[..., None]), 0.0
            ).astype(jnp.bfloat16)
            return accumulated + jnp.einsum(
                "hqk,khd->qhd", weights_tile, value_tile, preferred_element_type=jnp.float32
            )

        attended = lax.fori_loop(
            0, tile_total, value_step, jnp.zeros((BLK, HEADS, HD), jnp.float32)
        )
        log_total, attended = (log_total, attended)
        log_totals.append(log_total)
        attended_parts.append(attended)
    attended_full = jnp.concatenate(attended_parts, 0)
    attended_low = attended_full.reshape(TOK_DEV, D).astype(jnp.bfloat16)
    attention_out = jnp.dot(attended_low, dense_matrix, preferred_element_type=jnp.float32)
    normed_two = layer_norm(
        inputs, gain_two.astype(jnp.float32), shift_two.astype(jnp.float32)
    ).astype(jnp.bfloat16)
    upper_rows = jnp.dot(
        normed_two, up_matrix, preferred_element_type=jnp.float32
    ) + up_offset.astype(jnp.float32)
    activated = gelu_exact(upper_rows).astype(jnp.bfloat16)
    mlp_out = jnp.dot(activated, down_matrix, preferred_element_type=jnp.float32)
    result_rows = inputs + attention_out + mlp_out + out_offset.astype(jnp.float32)
    layer_output = result_rows.astype(jnp.bfloat16)[None]
    (
        gain_one,
        shift_one,
        qkv_matrix,
        qkv_offset,
        dense_matrix,
        gain_two,
        shift_two,
        up_matrix,
        up_offset,
        down_matrix,
        out_offset,
    ) = gathered
    grad_rows = cotangent[0]
    grad_float = grad_rows.astype(jnp.float32)
    out_offset_grad = jnp.sum(grad_float, 0)
    dense_grad = contract(attended_low, grad_rows, 0, 0)
    down_grad = contract(activated, grad_rows, 0, 0)
    grad_attended = contract(grad_rows, dense_matrix, 1, 1).astype(jnp.bfloat16)
    grad_activated = contract(grad_rows, down_matrix, 1, 1)
    gelu_back = jax.vjp(gelu_exact, upper_rows)[1]
    grad_upper = gelu_back(grad_activated)[0].astype(jnp.bfloat16)
    up_grad = contract(normed_two, grad_upper, 0, 0)
    up_offset_grad = jnp.sum(grad_upper.astype(jnp.float32), 0)
    grad_normed_two = contract(grad_upper, up_matrix, 1, 1)
    grad_heads = grad_attended.reshape(TOK_DEV, HEADS, HD)
    delta_rows = jnp.sum(grad_heads.astype(jnp.float32) * attended_full, -1)
    grad_blocks = grad_heads.reshape(2, BLK, HEADS, HD)
    delta_blocks = delta_rows.reshape(2, BLK, HEADS)

    def grad_tiles(query_block, query_pos, grad_block, log_total, delta_block):

        def tile_step(tile_index, running):
            wanted, chosen, key_pos = pick_tile(tile_index)
            key_tile = key_stack[chosen].reshape(tile_rows, HEADS, HD)
            value_tile = value_stack[chosen].reshape(tile_rows, HEADS, HD)
            allowed = key_pos[None, :] <= query_pos[:, None]
            scores = jnp.einsum(
                "qhd,khd->hqk", query_block, key_tile, preferred_element_type=jnp.float32
            )
            probs_tile = jnp.where(allowed[None], jnp.exp(scores - log_total[..., None]), 0.0)
            grad_probs = jnp.einsum(
                "qhd,khd->hqk", grad_block, value_tile, preferred_element_type=jnp.float32
            )
            grad_scores = (probs_tile * (grad_probs - delta_block[..., None])).astype(jnp.bfloat16)
            grad_query = running[0] + jnp.einsum(
                "hqk,khd->qhd", grad_scores, key_tile, preferred_element_type=jnp.float32
            )
            key_part = jnp.einsum(
                "hqk,qhd->khd", grad_scores, query_block, preferred_element_type=jnp.float32
            )
            value_part = jnp.einsum(
                "hqk,qhd->khd",
                probs_tile.astype(jnp.bfloat16),
                grad_block,
                preferred_element_type=jnp.float32,
            )
            key_grads = running[1].at[chosen].add(key_part.reshape(group_size, BLK, D))
            value_grads = running[2].at[chosen].add(value_part.reshape(group_size, BLK, D))
            return (grad_query, key_grads, value_grads)

        return tile_step

    zero_query = jnp.zeros((BLK, HEADS, HD), jnp.float32)
    grad_query_parts = []
    running = (
        zero_query,
        jnp.zeros((total_blocks, BLK, D), jnp.float32),
        jnp.zeros((total_blocks, BLK, D), jnp.float32),
    )
    for slot_index in range(2):
        tile_step = grad_tiles(
            query_blocks[slot_index],
            pos_blocks[slot_index],
            grad_blocks[slot_index],
            log_totals[slot_index],
            delta_blocks[slot_index].T,
        )
        running = lax.fori_loop(0, tile_totals[slot_index], tile_step, (zero_query,) + running[1:])
        grad_query_parts.append(running[0])
    grad_keys, grad_values = (
        lax.psum_scatter(
            running[1].reshape(-1, D).astype(jnp.bfloat16), "ctx", scatter_dimension=0, tiled=True
        ).astype(jnp.float32),
        lax.psum_scatter(
            running[2].reshape(-1, D).astype(jnp.bfloat16), "ctx", scatter_dimension=0, tiled=True
        ).astype(jnp.float32),
    )
    grad_keys = grad_keys.reshape(TOK_DEV, HEADS, HD)
    grad_queries = jnp.concatenate(grad_query_parts, 0)
    grad_query_raw = jax.vjp(turn_queries, query_raw)[1](grad_queries)[0]
    grad_key_raw = jax.vjp(turn_keys, key_raw)[1](grad_keys)[0]
    grad_mixed = jnp.concatenate(
        [grad_query_raw.reshape(TOK_DEV, D), grad_key_raw.reshape(TOK_DEV, D), grad_values], 1
    ).astype(jnp.bfloat16)
    qkv_grad = contract(normed_one, grad_mixed, 0, 0)
    qkv_offset_grad = jnp.sum(grad_mixed.astype(jnp.float32), 0)
    grad_normed_one = contract(grad_mixed, qkv_matrix, 1, 1)
    norm_back_one = jax.vjp(
        layer_norm, inputs, gain_one.astype(jnp.float32), shift_one.astype(jnp.float32)
    )[1]
    grad_in_one, gain_one_grad, shift_one_grad = norm_back_one(grad_normed_one)
    norm_back_two = jax.vjp(
        layer_norm, inputs, gain_two.astype(jnp.float32), shift_two.astype(jnp.float32)
    )[1]
    grad_in_two, gain_two_grad, shift_two_grad = norm_back_two(grad_normed_two)
    input_grad = (grad_float + grad_in_one + grad_in_two).astype(jnp.bfloat16)[None]
    grad_parts = (
        lax.psum_scatter(
            gain_one_grad.astype(jnp.bfloat16), "wsh", scatter_dimension=0, tiled=True
        ).astype(jnp.float32),
        lax.psum_scatter(
            shift_one_grad.astype(jnp.bfloat16), "wsh", scatter_dimension=0, tiled=True
        ).astype(jnp.float32),
        lax.psum_scatter(
            qkv_grad.astype(jnp.bfloat16), "wsh", scatter_dimension=0, tiled=True
        ).astype(jnp.float32),
        lax.psum_scatter(
            qkv_offset_grad.astype(jnp.bfloat16), "wsh", scatter_dimension=0, tiled=True
        ).astype(jnp.float32),
        lax.psum_scatter(
            dense_grad.astype(jnp.bfloat16), "wsh", scatter_dimension=0, tiled=True
        ).astype(jnp.float32),
        lax.psum_scatter(
            gain_two_grad.astype(jnp.bfloat16), "wsh", scatter_dimension=0, tiled=True
        ).astype(jnp.float32),
        lax.psum_scatter(
            shift_two_grad.astype(jnp.bfloat16), "wsh", scatter_dimension=0, tiled=True
        ).astype(jnp.float32),
        lax.psum_scatter(
            up_grad.astype(jnp.bfloat16), "wsh", scatter_dimension=0, tiled=True
        ).astype(jnp.float32),
        lax.psum_scatter(
            up_offset_grad.astype(jnp.bfloat16), "wsh", scatter_dimension=0, tiled=True
        ).astype(jnp.float32),
        lax.psum_scatter(
            down_grad.astype(jnp.bfloat16), "wsh", scatter_dimension=0, tiled=True
        ).astype(jnp.float32),
        lax.psum_scatter(
            out_offset_grad.astype(jnp.bfloat16), "wsh", scatter_dimension=0, tiled=True
        ).astype(jnp.float32),
    )
    grad_sums = jax.tree.map(
        lambda part: part.astype(jnp.float32), lax.psum(for_sending(tuple(grad_parts)), "ctx")
    )
    return (layer_output, input_grad) + tuple(grad_sums)


def solution(mesh):
    placed = (
        P("wsh", "ctx", None),
        P("wsh", "ctx", None),
        P(),
        P("wsh"),
        P("wsh"),
        P("wsh", None),
        P("wsh"),
        P("wsh", None),
        P("wsh"),
        P("wsh"),
        P("wsh", None),
        P("wsh"),
        P("wsh", None),
        P("wsh"),
    )
    return jax.shard_map(
        on_device,
        mesh=mesh,
        in_specs=placed,
        out_specs=(
            P("wsh", "ctx", None),
            P("wsh", "ctx", None),
            P("wsh"),
            P("wsh"),
            P("wsh", None),
            P("wsh"),
            P("wsh", None),
            P("wsh"),
            P("wsh"),
            P("wsh", None),
            P("wsh"),
            P("wsh", None),
            P("wsh"),
        ),
        check_vma=False,
    )
```

profile of v0, /device:TPU:0, one launch (start us, length us, event | category | flops | bytes accessed | tf_op | source)
XLA Modules:
  0.0 2364.2 jit_solution(4793230479721488543)
XLA Ops:
  18.5 17.2 all-reduce.24
  37.1 10.1 all-gather.8.cloned.1.call-done
  58.2 11.7 all-gather.14.cloned.1.call-done
  73.7 204.0 %all-gather.12.cloned.1.call-done = bf16[8192,768]{0,1:T(8,128)(2,1)} async-done(((bf16[256,768]{0,1:T(8,128)(2,1)}), bf16[8192,768]{0,1:T(8,128)(2,1)}) %all-gather.12.cloned.1.call-update) | async-done | bytes 12582928 | tf_op jit(solution)/shard_map/all_gather | solution.py:150
  277.7 11.4 copy.159
  289.2 28.6 %copy.138 = bf16[64,128,12,64]{3,2,1,0:T(8,128)(2,1)} copy(bf16[64,128,12,64]{1,0,3,2:T(8,128)(2,1)} %bitcast.466) | data formatting | bytes 25165824
  317.8 31.2 %while.78 = (s32[]{:T(128)}, f32[12,128]{1,0:T(8,128)S(1)}, f32[12,128]{1,0:T(8,128)S(1)}, s32[]{:T(128)}, s32[1,128]{1,0:T(1,128)S(1)}, /*index=5*/s32[64]{0:T(...) while((s32[]{:T(128)}, f32[12,128]{1,0:T(8,128)S(1)}, ...), condition=%wide.region_6.7_spmd.clone, body=%wide.region_3.6_spmd.clone.sunk | while | flops 104666664 | bytes 9136937 | solution.py:195
  349.5 107.3 %all-gather.10.cloned.1.call-done = bf16[8192,768]{1,0:T(8,128)(2,1)} async-done(((bf16[256,768]{1,0:T(8,128)(2,1)}), bf16[8192,768]{1,0:T(8,128)(2,1)}) %all-gather.10.cloned.1.call-update) | async-done | bytes 12582928 | tf_op jit(solution)/shard_map/all_gather | solution.py:151
  456.9 38.2 %reshape.1063 = bf16[64,128,12,64]{3,2,1,0:T(8,128)(2,1)} reshape(bf16[8192,768]{1,0:T(8,128)(2,1)} %all-gather.10.cloned.1.call-done) | data formatting | bytes 25165824
  495.9 68.6 %while.79 = (s32[]{:T(128)}, f32[128,12,64]{0,2,1:T(8,128)}, s32[]{:T(128)}, s32[64]{0:T(128)S(1)}, bf16[64,128,12,64]{3,2,1,0:T(8,128)(2,1)}, /*index=5*/s32[1,...) while((s32[]{:T(128)}, f32[128,12,64]{0,2,1:T(8,128)}, ...), condition=%wide.region_8.9_spmd.clone, body=%wide.region_7.8_spmd.clone.sunk | while | flops 203852336 | bytes 5851969 | solution.py:208
  514.9 3.9 fusion.266
  526.1 4.0 fusion.266
  566.5 57.3 %while.80 = (s32[]{:T(128)}, f32[12,128]{1,0:T(8,128)S(1)}, f32[12,128]{1,0:T(8,128)S(1)}, s32[]{:T(128)}, s32[1,128]{1,0:T(1,128)S(1)}, /*index=5*/s32[64]{0:T(...) while((s32[]{:T(128)}, f32[12,128]{1,0:T(8,128)S(1)}, ...), condition=%wide.region_12.13_spmd.clone, body=%wide.region_9.12_spmd.clone.sunk | while | flops 104666664 | bytes 9136937 | solution.py:195
  624.6 125.3 %while.81 = (s32[]{:T(128)}, f32[128,12,64]{0,2,1:T(8,128)}, s32[]{:T(128)}, s32[64]{0:T(128)S(1)}, bf16[64,128,12,64]{3,2,1,0:T(8,128)(2,1)}, /*index=5*/s32[1,...) while((s32[]{:T(128)}, f32[128,12,64]{0,2,1:T(8,128)}, ...), condition=%wide.region_14.15_spmd.clone, body=%wide.region_13.14_spmd.clone.sunk | while | flops 203852336 | bytes 5851969 | solution.py:208
  632.0 3.9 fusion.278
  643.4 3.9 fusion.278
  654.7 3.9 fusion.278
  677.4 3.9 fusion.278
  688.7 3.9 fusion.278
  700.0 3.9 fusion.278
  711.4 3.9 fusion.278
  722.7 3.9 fusion.278
  734.1 3.9 fusion.278
  745.4 3.9 fusion.278
  754.9 11.4 broadcast.823
  766.3 11.4 broadcast.823.clone
  778.5 223.5 %while.82 = (s32[]{:T(128)}, f32[128,12,64]{0,2,1:T(8,128)}, f32[64,128,768]{2,1,0:T(8,128)}, f32[64,128,768]{2,1,0:T(8,128)}, s32[]{:T(128)}, /*index=5*/s32[64...) while((s32[]{:T(128)}, f32[128,12,64]{0,2,1:T(8,128)}, ...), condition=%wide.region_19.20_spmd.clone, body=%wide.region_16.19_spmd.clone.sunk | while | flops 510560800 | bytes 54754472 | solution.py:305
  802.7 4.2 scatter_fusion
  839.8 4.3 scatter_fusion
  876.8 4.3 scatter_fusion
  914.0 4.2 scatter_fusion
  951.0 4.3 scatter_fusion
  988.2 4.2 scatter_fusion
  1002.8 400.9 %while.83 = (s32[]{:T(128)}, f32[128,12,64]{0,2,1:T(8,128)}, f32[64,128,768]{2,1,0:T(8,128)}, f32[64,128,768]{2,1,0:T(8,128)}, s32[]{:T(128)}, /*index=5*/s32[64...) while((s32[]{:T(128)}, f32[128,12,64]{0,2,1:T(8,128)}, ...), condition=%wide.region_23.24_spmd.clone, body=%wide.region_20.23_spmd.clone.sunk | while | flops 510560800 | bytes 55565536 | solution.py:305
  1026.2 4.2 scatter_fusion.2
  1062.5 4.3 scatter_fusion.2
  1098.9 4.3 scatter_fusion.2
  1135.3 4.2 scatter_fusion.2
  1171.7 4.3 scatter_fusion.2
  1208.1 4.2 scatter_fusion.2
  1244.5 4.3 scatter_fusion.2
  1280.8 4.3 scatter_fusion.2
  1317.2 4.2 scatter_fusion.2
  1353.6 4.2 scatter_fusion.2
  1390.0 4.2 scatter_fusion.2
  1403.7 13.4 convert_element_type.234
  1417.1 16.8 copy.149
  1434.0 13.4 convert_element_type.236
  1447.3 16.7 copy.150
  1464.7 7.2 all-gather
  1472.0 11.5 multiply_convert_fusion
  1483.4 7.0 fusion.159
  1502.5 137.9 %reduce-scatter.7.cloned.1.call-done = bf16[256,768]{0,1:T(8,128)(2,1)} async-done(((bf16[8192,768]{0,1:T(8,128)(2,1)}), bf16[256,768]{0,1:T(8,128)(2,1)}) %reduce-scatter.7.cloned.1.call-update) | async-done | bytes 393232 | tf_op jit(solution)/shard_map/reduce_scatter | solution.py:308
  1643.8 187.2 %reduce-scatter.9.cloned.1.call-done = bf16[256,768]{0,1:T(8,128)(2,1)} async-done(((bf16[8192,768]{0,1:T(8,128)(2,1)}), bf16[256,768]{0,1:T(8,128)(2,1)}) %reduce-scatter.9.cloned.1.call-update) | async-done | bytes 393232 | tf_op jit(solution)/shard_map/reduce_scatter | solution.py:311
  1831.0 4.1 convolution_convert_fusion.2
  1835.3 50.3 %reduce-scatter.15.cloned.1.call-done = bf16[192,3072]{1,0:T(8,128)(2,1)} async-done(((bf16[768,3072]{1,0:T(8,128)(2,1)}), bf16[192,3072]{1,0:T(8,128)(2,1)}) %reduce-scatter.15.cloned.1.call-update) | async-done | bytes 1179664 | tf_op jit(solution)/shard_map/reduce_scatter | solution.py:356
  1885.7 56.9 %reduce-scatter.17.cloned.1.call-done = bf16[768,768]{1,0:T(8,128)(2,1)} async-done(((bf16[3072,768]{1,0:T(8,128)(2,1)}), bf16[768,768]{1,0:T(8,128)(2,1)}) %reduce-scatter.17.cloned.1.call-update) | async-done | bytes 1179664 | tf_op jit(solution)/shard_map/reduce_scatter | solution.py:362
  1942.5 35.3 %reduce-scatter.13.cloned.1.call-done = bf16[192,768]{1,0:T(8,128)(2,1)} async-done(((bf16[768,768]{1,0:T(8,128)(2,1)}), bf16[192,768]{1,0:T(8,128)(2,1)}) %reduce-scatter.13.cloned.1.call-update) | async-done | bytes 294928 | tf_op jit(solution)/shard_map/reduce_scatter | solution.py:347
  1977.9 49.5 %reduce-scatter.11.cloned.1.call-done = bf16[192,2304]{1,0:T(8,128)(2,1)} async-done(((bf16[768,2304]{1,0:T(8,128)(2,1)}), bf16[192,2304]{1,0:T(8,128)(2,1)}) %reduce-scatter.11.cloned.1.call-update) | async-done | bytes 884752 | tf_op jit(solution)/shard_map/reduce_scatter | solution.py:341
  2032.0 4.2 fusion.163
  2036.2 4.8 fusion.162
  2046.9 14.9 all-reduce.23
  2070.9 84.9 %all-reduce.21 = (bf16[192]{0:T(256)(128)(2,1)}, bf16[192]{0:T(256)(128)(2,1)}, bf16[576]{0:T(1024)(128)(2,1)}, bf16[192]{0:T(256)(128)(2,1)}, bf16[192]{0:T(256...) all-reduce(bf16[192]{0:T(256)(128)(2,1)} %dynamic-slice.7, ...), channel_id=1, replica_groups=mesh['ctx'=32,'wsh'=4] {'ctx'}, use_global_device_ids=true, to_apply=%region_32.33 | all-reduce | flops 2304 | bytes 9216 | tf_op jit(solution)/shard_map/psum | solution.py:370
  2170.3 180.1 %all-reduce.27.cloned.1.call-done = (bf16[192,2304]{1,0:T(8,128)(2,1)}, bf16[192,768]{1,0:T(8,128)(2,1)}, bf16[192,3072]{1,0:T(8,128)(2,1)}, bf16[768,768]{1,0:T(8,128)(2,1)}) async-done(((bf16[192,2304]{1,0:T(8,128)(2,1)}, bf16[192,768]{1,0:T(8,128)(2,1)}, bf16[192,3072]{1,0:T(8,128)(2,1)}, bf16[768,768]{1,0:T(8,128)(2,1)}), (bf16[192,2304]{1,0:T(8,128)(2,1)}, bf16[192,768]{1,0:T(8,128)(2,1)}, ...) | async-done | bytes 3538960 | tf_op jit(solution)/shard_map/psum | solution.py:370
  (1246 shorter events, 838.6 us)
Async XLA Ops:
  7.2 40.0 %all-gather.8.cloned.1.call-start = ((), (), s32[]{:S(2)}) async-start(), calls=%async_computation.6 | async-start | bytes 4423680 | tf_op jit(solution)/shard_map/all_gather | solution.py:114
  7.9 62.0 %all-gather.14.cloned.1.call-start = ((), (), s32[]{:S(2)}) async-start(), calls=%async_computation.9 | async-start | bytes 1474560 | tf_op jit(solution)/shard_map/all_gather | solution.py:116
  8.7 269.1 %all-gather.12.cloned.1.call-start = ((), (), s32[]{:S(2)}) async-start(), calls=%async_computation.8 | async-start | bytes 12976128 | tf_op jit(solution)/shard_map/all_gather | solution.py:150
  12.5 38.0 %copy-start.42 = (f32[256]{0:T(256)}, f32[256]{0:T(256)S(1)}, u32[]{:S(2)}) copy-start(f32[256]{0:T(256)S(1)} %broadcast_multiply_fusion.1) | copy-start | bytes 3076
  35.7 14.8 copy-start.40
  35.7 14.8 copy-start.52
  35.8 16.8 copy-start.29
  35.8 16.8 copy-start.31
  37.1 13.5 copy-start.50
  37.1 13.5 copy-start.44
  52.5 17.3 copy-start.9
  53.5 403.4 %all-gather.10.cloned.1.call-start = ((), (), s32[]{:S(2)}) async-start(), calls=%async_computation.7 | async-start | bytes 12976128 | tf_op jit(solution)/shard_map/all_gather | solution.py:151
  55.5 1416.4 %all-gather.16.cloned.1.call-start = ((), (), s32[]{:S(2)}) async-start(), calls=%async_computation.10 | async-start | bytes 5898240 | tf_op jit(solution)/shard_map/all_gather | solution.py:119
  56.1 1427.4 %all-gather.18.cloned.1.call-start = ((), (), s32[]{:S(2)}) async-start(), calls=%async_computation.11 | async-start | bytes 5898240 | tf_op jit(solution)/shard_map/all_gather | solution.py:121
  56.6 1583.8 %reduce-scatter.7.cloned.1.call-start = ((), (), s32[]{:S(2)}) async-start(), calls=%async_computation.12 | async-start | bytes 12976128 | tf_op jit(solution)/shard_map/reduce_scatter | solution.py:308
  349.5 146.3 %copy-start.35 = (s32[1,128]{1,0:T(1,128)S(1)}, s32[1,128]{1,0:T(1,128)}, u32[]{:S(2)}) copy-start(s32[1,128]{1,0:T(1,128)} %copy-done.34) | copy-start | bytes 1540
  750.0 16.3 copy-start.26
  750.0 16.3 copy-start.33
  797.4 5.3 copy-start.37
  834.5 5.3 copy-start.37
  871.6 5.3 copy-start.37
  908.7 5.3 copy-start.37
  945.7 5.3 copy-start.37
  982.9 5.3 copy-start.37
  1004.3 4.5 copy-start.38
  1020.9 5.3 copy-start.39
  1040.6 4.5 copy-start.38
  1057.3 5.3 copy-start.39
  1093.6 5.3 copy-start.39
  1113.4 4.5 copy-start.38
  1130.0 5.3 copy-start.39
  1166.4 5.3 copy-start.39
  1202.8 5.3 copy-start.39
  1239.2 5.3 copy-start.39
  1275.5 5.3 copy-start.39
  1295.3 4.5 copy-start.38
  1311.9 5.3 copy-start.39
  1348.3 5.3 copy-start.39
  1368.1 4.5 copy-start.38
  1384.7 5.3 copy-start.39
  1433.9 397.0 %reduce-scatter.9.cloned.1.call-start = ((), (), s32[]{:S(2)}) async-start(), calls=%async_computation.13 | async-start | bytes 12976128 | tf_op jit(solution)/shard_map/reduce_scatter | solution.py:311
  1464.0 7.9 copy-start.8
  1464.0 7.9 copy-start.43
  1464.0 7.9 copy-start.45
  1464.1 421.6 %reduce-scatter.15.cloned.1.call-start = ((), (), s32[]{:S(2)}) async-start(), calls=%async_computation.16 | async-start | bytes 5898240 | tf_op jit(solution)/shard_map/reduce_scatter | solution.py:356
  1471.9 11.5 copy-start.10
  1495.4 447.2 %reduce-scatter.17.cloned.1.call-start = ((), (), s32[]{:S(2)}) async-start(), calls=%async_computation.17 | async-start | bytes 5898240 | tf_op jit(solution)/shard_map/reduce_scatter | solution.py:362
  1499.0 478.9 %reduce-scatter.13.cloned.1.call-start = ((), (), s32[]{:S(2)}) async-start(), calls=%async_computation.15 | async-start | bytes 1474560 | tf_op jit(solution)/shard_map/reduce_scatter | solution.py:347
  1501.5 141.1 %copy-start.30 = (f32[256,16]{0,1:T(8,128)S(1)}, f32[256,16]{0,1:T(8,128)}, u32[]{:S(2)}) copy-start(f32[256,16]{0,1:T(8,128)} %copy-done.29) | copy-start | bytes 49156
  1501.5 141.1 %copy-start.32 = (f32[256,16]{0,1:T(8,128)S(1)}, f32[256,16]{0,1:T(8,128)}, u32[]{:S(2)}) copy-start(f32[256,16]{0,1:T(8,128)} %copy-done.31) | copy-start | bytes 49156
  1501.5 525.9 %reduce-scatter.11.cloned.1.call-start = ((), (), s32[]{:S(2)}) async-start(), calls=%async_computation.14 | async-start | bytes 4423680 | tf_op jit(solution)/shard_map/reduce_scatter | solution.py:341
  1502.5 141.1 %slice-start = ((f32[256,12,64]{0,2,1:T(8,128)}), f32[256,12,48]{0,2,1:T(8,128)S(1)}, s32[]{:S(2)}) async-start(f32[256,12,64]{0,2,1:T(8,128)} %copy-done.15), calls=%async_computation.19 | async-start | bytes 1179648 | tf_op jit(solution)/shard_map/transpose(jvp())/split | solution.py:35
  1641.5 189.4 %copy-start.41 = (f32[768]{0:T(1024)S(1)}, f32[768]{0:T(1024)}, u32[]{:S(2)}) copy-start(f32[768]{0:T(1024)} %copy-done.40) | copy-start | bytes 9220
  1643.7 397.4 %copy-start.17 = (bf16[256,12,64]{0,2,1:T(8,128)(2,1)}, bf16[256,12,64]{0,2,1:T(8,128)(2,1)S(1)}, u32[]{:S(2)}) copy-start(bf16[256,12,64]{0,2,1:T(8,128)(2,1)S(1)} %add_convert_fusion.3) | copy-start | bytes 1179652
  1643.8 191.2 %copy-start.18 = (bf16[256,12,64]{0,2,1:T(8,128)(2,1)}, bf16[256,12,64]{0,2,1:T(8,128)(2,1)S(1)}, u32[]{:S(2)}) copy-start(bf16[256,12,64]{0,2,1:T(8,128)(2,1)S(1)} %add_convert_fusion.2) | copy-start | bytes 1179652
  1835.0 195.6 %copy-start.57 = (bf16[192]{0:T(256)(128)(2,1)S(1)}, bf16[192]{0:T(256)(128)(2,1)}, u32[]{:S(2)}) copy-start(bf16[192]{0:T(256)(128)(2,1)} %param.39) | copy-start | bytes 1156
  1835.0 515.3 %all-reduce.27.cloned.1.call-start = ((), (), s32[]{:S(2)}) async-start(), calls=%async_computation.18 | async-start | bytes 7077888 | tf_op jit(solution)/shard_map/psum | solution.py:370
  2036.2 4.8 copy-start.19
  2036.2 4.8 copy-start.25
  2036.2 5.8 copy-start.56
  2042.0 124.4 %copy-start.14 = (bf16[768,768]{1,0:T(8,128)(2,1)S(1)}, bf16[768,768]{1,0:T(8,128)(2,1)}, u32[]{:S(2)}) copy-start(bf16[768,768]{1,0:T(8,128)(2,1)} %all-gather.14.cloned.1.call-done) | copy-start | bytes 3538948
  2155.8 13.2 copy-start.47
  2155.8 13.2 copy-start.49
  2350.4 4.7 copy-start.22
  (118 other events, 314.5 us)
Sparse Core Ops, SparseCore 0:
  9.7 37.4 all-gather.7
  48.8 20.9 all-gather.13
  72.0 205.6 all-gather.11
  279.8 177.0 all-gather.9
  458.4 39.5 all-gather.15
  499.5 40.8 all-gather.17
  1434.0 206.3 reduce-scatter.6
  1642.8 188.0 reduce-scatter.8
  1833.6 52.0 reduce-scatter.14
  1888.4 54.1 reduce-scatter.16
  1945.8 32.0 reduce-scatter.12
  1980.6 46.7 reduce-scatter.10
  2030.2 320.1 all-reduce.26
where the time goes:
time: 2380 us; the launch traced here: 2360 us
  waiting for transfers between devices  1030 us (43%)
  local copies, waits for them, and re-layouts  624 us (26%)
  matrix products  294 us (12%)
  other arithmetic  230 us (10%)
  blocking collectives  124 us (5%)
  loops' own time  40.4 us (2%)
    all_gather x1, waiting for transfers between devices, on_device(): lax.all_gather(key_rows.reshape(TOK_DEV, D), 'ctx', axis=0, tiled=True)  204 us
    reduce_scatter x1, waiting for transfers between devices, on_device(): lax.psum_scatter(running[2].reshape(-1, D).astype(jnp.bfloat16), 'ctx', s...  187 us
    psum x1, waiting for transfers between devices, on_device(): lax.psum(for_sending(tuple(grad_parts)), 'ctx')  180 us
    reduce_scatter x1, waiting for transfers between devices, on_device(): lax.psum_scatter(running[1].reshape(-1, D).astype(jnp.bfloat16), 'ctx', s...  138 us
    all_gather x1, waiting for transfers between devices, on_device(): lax.all_gather(value_rows, 'ctx', axis=0, tiled=True)  107 us
    unnamed x112, local copies, waits for them, and re-layouts  101 us
    gather x34, local copies, waits for them, and re-layouts, tile_scores(): key_tile = key_stack[chosen].reshape(tile_rows, HEADS, HD)  99.4 us
    reshape x34, local copies, waits for them, and re-layouts, tile_step(): key_grads = running[1].at[chosen].add(key_part.reshape(group_size, BLK, D))  89.7 us
  transfers between devices with their start and end apart: 13, of which 11 were waited for; matrix products, arithmetic and copies ran while one was open for 47% of the time, Pallas kernels for 0%

commit v1 on v0

v1 whole, which is shorter than its diff:
```python
import functools

import jax
import jax.numpy as jnp
from jax import lax
from jax.experimental import pallas as pl
from jax.experimental.pallas import tpu as pltpu
from jax.sharding import PartitionSpec as P

G = 3; BLK = 128; LOG2E = 1.4426950408889634
NEG = -1e30

def attn_kernel(chunk, qpos, lay, qdo, kv_hbm, odq, dkv_hbm, kv, kvt, acc, stage, sem, osem):
    blocks = chunk // BLK
    nblk = kv.shape[0] // BLK
    f32, bf = jnp.float32, jnp.bfloat16

    def load(i, _):
        pltpu.make_async_copy(kv_hbm.at[pl.ds(pl.multiple_of(lay[i] * BLK, BLK), BLK)], kv.at[pl.ds(pl.multiple_of(i * BLK, BLK), BLK)], sem.at[i]).start()
        return 0
    lax.fori_loop(0, nblk, load, 0)

    def land(i, _):
        rows = pl.ds(pl.multiple_of(i * BLK, BLK), BLK)
        pltpu.make_async_copy(kv_hbm.at[pl.ds(0, BLK)], kv.at[rows], sem.at[i]).wait()
        acc[rows] = jnp.zeros((BLK, G * 128), f32)
        kvt[:, rows] = kv[rows].T
        return 0
    lax.fori_loop(0, nblk, land, 0)

    upper = lax.broadcasted_iota(jnp.int32, (128, 128), 0) < 64
    left = lax.broadcasted_iota(jnp.int32, (128, 128), 1) < 64

    def q_block(i, _):
        b = qpos[i]
        qrows = pl.ds(pl.multiple_of(i * BLK, BLK), BLK)
        last = b // blocks
        pairs = [qdo[qrows, h * 128:(h + 1) * 128] for h in range(G)]
        turned = [p.astype(f32).T for p in pairs]
        q_side = [jnp.where(upper, t, 0.0).astype(bf) for t in turned]
        wide = [jnp.concatenate([q_side[h], jnp.where(upper, 0.0, turned[h]).astype(bf)], 1) for h in range(G)]
        key_i = lax.broadcasted_iota(jnp.int32, (chunk, BLK), 0)
        row_i = lax.broadcasted_iota(jnp.int32, (chunk, BLK), 1) + (b - last * blocks) * BLK

        def fwd(c, state, masked):
            at = pl.ds(pl.multiple_of(c * chunk, chunk), chunk)
            out = []
            for h in range(G):
                m, l, o = state[h]
                s = jnp.dot(kv[at, h * 128:(h + 1) * 128], q_side[h], preferred_element_type=f32)
                if masked:
                    s = jnp.where(key_i <= row_i, s, NEG)
                new = jnp.maximum(m, jnp.max(s, 0, keepdims=True))
                p = jnp.exp(s - new)
                a = jnp.exp(m - new)
                l = l * a + jnp.sum(p, 0, keepdims=True)
                o = o * a + jnp.dot(kvt[h * 128 + 64:(h + 1) * 128, at], p.astype(bf), preferred_element_type=f32)
                out.append((new, l, o))
            return tuple(out)

        state = tuple((jnp.full((1, BLK), NEG, f32), jnp.zeros((1, BLK), f32), jnp.zeros((64, BLK), f32)) for _ in range(G))
        state = lax.fori_loop(0, last, lambda c, s: fwd(c, s, False), state)
        state = fwd(last, state, True)
        lse, delta, outs = [], [], []
        for h in range(G):
            m, l, o = state[h]
            o = o / l
            outs.append(o)
            lse.append(m + jnp.log(l))
            delta.append(jnp.sum(o * turned[h][64:], 0, keepdims=True))
        narrow = [jnp.concatenate([jnp.where(left, pairs[h], jnp.zeros_like(pairs[h])), jnp.where(left, jnp.zeros_like(pairs[h]), pairs[h])], 0) for h in range(G)]

        def bwd(c, state, masked):
            at = pl.ds(pl.multiple_of(c * chunk, chunk), chunk)
            out = []
            for h in range(G):
                cols = slice(h * 128, (h + 1) * 128)
                both = jnp.dot(kv[at, cols], wide[h], preferred_element_type=f32)
                p = jnp.exp(both[:, :128] - lse[h])
                if masked:
                    p = jnp.where(key_i <= row_i, p, 0.0)
                ds = (p * (both[:, 128:] - delta[h])).astype(bf)
                pair = jnp.concatenate([ds, p.astype(bf)], 1)
                acc[at, cols] += jnp.dot(pair, narrow[h], preferred_element_type=f32)
                out.append(state[h] + jnp.dot(kvt[h * 128:h * 128 + 64, at], ds, preferred_element_type=f32))
            return tuple(out)

        dq = tuple(jnp.zeros((64, BLK), f32) for _ in range(G))
        dq = lax.fori_loop(0, last, lambda c, s: bwd(c, s, False), dq)
        dq = bwd(last, dq, True)
        for h in range(G):
            odq[qrows, h * 128:(h + 1) * 128] = jnp.concatenate([outs[h], dq[h]], 0).T.astype(bf)
        return 0
    lax.fori_loop(0, qpos.shape[0], q_block, 0)

    def send(i, _):
        slot = lax.rem(i, 8)
        @pl.when(i >= 8)
        def _():
            pltpu.make_async_copy(stage.at[slot], dkv_hbm.at[pl.ds(0, BLK)], osem.at[slot]).wait()
        stage[slot] = acc[pl.ds(pl.multiple_of(i * BLK, BLK), BLK)].astype(bf)
        pltpu.make_async_copy(stage.at[slot], dkv_hbm.at[pl.ds(pl.multiple_of(lay[i] * BLK, BLK), BLK)], osem.at[slot]).start()
        return 0
    lax.fori_loop(0, nblk, send, 0)
    for slot in range(8):
        pltpu.make_async_copy(stage.at[slot], dkv_hbm.at[pl.ds(0, BLK)], osem.at[slot]).wait()

def attention(qpos, lay, qdo, kv, chunk=1024):
    n = kv.shape[0]
    smem = pl.BlockSpec(memory_space=pltpu.SMEM)
    vmem = pl.BlockSpec(memory_space=pltpu.VMEM)
    hbm = pl.BlockSpec(memory_space=pl.ANY)
    return pl.pallas_call(
        functools.partial(attn_kernel, chunk),
        out_shape=(jax.ShapeDtypeStruct(qdo.shape, jnp.bfloat16), jax.ShapeDtypeStruct(kv.shape, jnp.bfloat16)),
        in_specs=[smem, smem, vmem, hbm], out_specs=(vmem, hbm),
        scratch_shapes=[pltpu.VMEM((n, G * 128), jnp.bfloat16), pltpu.VMEM((G * 128, n), jnp.bfloat16),
            pltpu.VMEM((n, G * 128), jnp.float32), pltpu.VMEM((8, BLK, G * 128), jnp.bfloat16),
            pltpu.SemaphoreType.DMA((n // BLK,)), pltpu.SemaphoreType.DMA((8,))],
        compiler_params=pltpu.CompilerParams(vmem_limit_bytes=56 * 2**20),
        name="attention",
    )(qpos, lay, qdo, kv)


MESH = pl.DeviceIdType.MESH
ROWS, WIDE = 256, 384


def place():
    c, w = lax.axis_index("ctx"), lax.axis_index("wsh")
    return c // 8, lax.rem(c // 4, 2), lax.rem(c, 4), w // 2, lax.rem(w, 2)


def device(z, yl, x, yh, core):
    return (z * 8 + yl * 4 + x, yh * 2 + core)


def greet(devices, extra=None, extra_count=0):
    barrier = pltpu.get_barrier_semaphore()
    for d in devices:
        pl.semaphore_signal(barrier, inc=1, device_id=d, device_id_type=MESH)
    if extra is not None:
        @pl.when(extra_count == 1)
        def _():
            pl.semaphore_signal(barrier, inc=1, device_id=extra, device_id_type=MESH)
    pl.semaphore_wait(barrier, len(devices) + extra_count)


def landed(ref, sem):
    pltpu.make_async_copy(ref, ref, sem).wait()


def spread_kernel(kvs, qds, kv_all, qdo, kv_send, kv_recv, q_send, q_recv, z_send, z_recv, half_send, half_recv, sib_send, sib_recv):
    z, yl, x, yh, core = place()
    swap = yl != core
    partner = [device(z, core, lax.rem(x + d, 4), yh, yl) for d in range(4)]
    up = device(lax.rem(z + 1, 4), yl, x, yh, core)
    down = device(lax.rem(z + 3, 4), yl, x, yh, core)
    sib = device(z, yl, x, yh, 1 - core)
    greet(partner[1:] + [up, down, sib], partner[0], lax.rem(yl + core, 2))

    def slot(zz, cc, d):
        return kv_all.at[lax.rem(zz, 4) * 8 + cc * 4 + lax.rem(x + 4 - d, 4)]

    def remote(src, dst, send, recv, to):
        copy = pltpu.make_async_remote_copy(src_ref=src, dst_ref=dst, send_sem=send, recv_sem=recv, device_id=to, device_id_type=MESH)
        copy.start()
        return copy

    def exchange(src, dst_of, send, recv):
        sent = [None] * 4
        for d in (0, 2, 1, 3):
            h = lax.rem(x + d, 4)
            args = (src.at[h], dst_of, send.at[d], recv.at[d], partner[d])
            if d == 0:
                @pl.when(swap)
                def _():
                    remote(*args)
                @pl.when(jnp.logical_not(swap))
                def _():
                    pltpu.make_async_copy(args[0], args[1], args[3]).start()
            else:
                remote(*args)
            sent[d] = pltpu.make_async_remote_copy(src_ref=args[0], dst_ref=args[1], send_sem=args[2], recv_sem=args[3], device_id=args[4], device_id_type=MESH)
        return sent

    waits = []
    mine = z * 8 + yl * 4 + x
    sent_kv = exchange(kvs, kv_all.at[mine], kv_send, kv_recv)
    sent_q = exchange(qds, qdo.at[x], q_send, q_recv)
    for d in (0, 1, 3, 2):
        here = slot(z, core, d)
        landed(here, kv_recv.at[d])
        waits.append(remote(here, here, z_send.at[0, d], z_recv.at[0, d], up))
        waits.append(remote(here, here, z_send.at[1, d], z_recv.at[1, d], down))
        waits.append(remote(here, here, sib_send.at[0, d], sib_recv.at[0, d], sib))
    half = ROWS // 2
    for d in (0, 1, 3, 2):
        for way, zz, to in ((0, z + 3, up), (1, z + 1, down)):
            here = slot(zz, core, d)
            landed(here, z_recv.at[way, d])
            part = here.at[pl.ds(way * half, half)]
            waits.append(remote(part, part, half_send.at[way, d], half_recv.at[way, d], to))
            waits.append(remote(here, here, sib_send.at[1 + way, d], sib_recv.at[1 + way, d], sib))
    for d in (0, 1, 3, 2):
        for way in (0, 1):
            part = slot(z + 2, core, d).at[pl.ds(way * half, half)]
            landed(part, half_recv.at[way, d])
            waits.append(remote(part, part, sib_send.at[3 + way, d], sib_recv.at[3 + way, d], sib))
    other = 1 - core
    for d in range(4):
        landed(slot(z, other, d), sib_recv.at[0, d])
        landed(slot(z + 3, other, d), sib_recv.at[1, d])
        landed(slot(z + 1, other, d), sib_recv.at[2, d])
        for way in (0, 1):
            landed(slot(z + 2, other, d).at[pl.ds(way * half, half)], sib_recv.at[3 + way, d])
        landed(qdo.at[lax.rem(x + 4 - d, 4)], q_recv.at[d])
    for copy in waits:
        copy.wait_send()
    for sent in (sent_kv, sent_q):
        for d in range(4):
            if d == 0:
                @pl.when(swap)
                def _():
                    sent[d].wait_send()
            else:
                sent[d].wait_send()


def spread(kvs, qds, collective_id=0):
    hbm = pl.BlockSpec(memory_space=pl.ANY)
    dma = pltpu.SemaphoreType.DMA
    return pl.pallas_call(
        spread_kernel,
        out_shape=(jax.ShapeDtypeStruct((32, ROWS, WIDE), jnp.bfloat16), jax.ShapeDtypeStruct((4, ROWS, WIDE), jnp.bfloat16)),
        in_specs=[hbm, hbm], out_specs=(hbm, hbm),
        scratch_shapes=[dma((4,)), dma((4,)), dma((4,)), dma((4,)), dma((2, 4)), dma((2, 4)), dma((2, 4)), dma((2, 4)), dma((5, 4)), dma((5, 4))],
        compiler_params=pltpu.CompilerParams(collective_id=collective_id, has_side_effects=True),
        name="spread",
    )(kvs, qds)


def collect_kernel(odq, dkv, odq_own, dkv_own, own, sib_in, far_in, near_out, near_in, done,
                   load_sem, o_send, o_recv, sib_send, sib_recv, far_send, far_recv, near_send, near_recv, g_send, g_recv):
    z, yl, x, yh, core = place()
    swap = yl != core
    partner = [device(z, core, lax.rem(x + d, 4), yh, yl) for d in range(4)]
    up = device(lax.rem(z + 1, 4), yl, x, yh, core)
    down = device(lax.rem(z + 3, 4), yl, x, yh, core)
    sib = device(z, yl, x, yh, 1 - core)
    greet(partner[1:] + [up, down, sib], partner[0], lax.rem(yl + core, 2))
    f32, bf = jnp.float32, jnp.bfloat16

    def remote(src, dst, send, recv, to):
        copy = pltpu.make_async_remote_copy(src_ref=src, dst_ref=dst, send_sem=send, recv_sem=recv, device_id=to, device_id_type=MESH)
        copy.start()
        return copy

    def exchange(src, dst_of, send, recv, d):
        args = (src.at[lax.rem(x + d, 4)], dst_of, send.at[d], recv.at[d], partner[d])
        if d == 0:
            @pl.when(swap)
            def _():
                remote(*args)
            @pl.when(jnp.logical_not(swap))
            def _():
                pltpu.make_async_copy(args[0], args[1], args[3]).start()
        else:
            remote(*args)
        return pltpu.make_async_remote_copy(src_ref=args[0], dst_ref=args[1], send_sem=args[2], recv_sem=args[3], device_id=args[4], device_id_type=MESH)

    def group(zz, cc):
        return dkv.at[pl.ds(lax.rem(zz, 4) * 8 + cc * 4, 4)]

    waits, loads = [], []
    order = (z + 2, z + 1, z + 3, z)
    for k, zz in enumerate(order):
        waits.append(remote(group(zz, 1 - core), sib_in.at[k], sib_send.at[k], sib_recv.at[k], sib))
        load = pltpu.make_async_copy(group(zz, core), own.at[k], load_sem.at[k])
        load.start()
        loads.append(load)
    sent_o = [exchange(odq, odq_own.at[x], o_send, o_recv, d) for d in range(4)]

    def add(first, k, also=()):
        def step(i, _):
            j, r = i // 2, pl.ds(pl.multiple_of(lax.rem(i, 2) * 128, 128), 128)
            total = own[k, j, r].astype(f32) + sib_in[k, j, r].astype(f32)
            for ref, low, high in also:
                if (low, high) == (0, 4):
                    total = total + ref[j, r].astype(f32)
            first[j, r] = total.astype(bf)
            return 0
        lax.fori_loop(0, 8, step, 0)

    loads[0].wait()
    landed(sib_in.at[0], sib_recv.at[0])
    add(done, 0)
    for way, to in ((0, up), (1, down)):
        waits.append(remote(done.at[pl.ds(2 * way, 2)], far_in.at[way], far_send.at[way], far_recv.at[way], to))
    for way, to in ((0, up), (1, down)):
        k = 1 + way
        loads[k].wait()
        landed(sib_in.at[k], sib_recv.at[k])
        add(near_out.at[way], k)
        landed(far_in.at[way], far_recv.at[way])

        def more(i, _):
            j, r = i // 2, pl.ds(pl.multiple_of(lax.rem(i, 2) * 128, 128), 128)
            near_out[way, 2 * way + j, r] = (own[k, 2 * way + j, r].astype(f32) + sib_in[k, 2 * way + j, r].astype(f32) + far_in[way, j, r].astype(f32)).astype(bf)
            return 0
        lax.fori_loop(0, 4, more, 0)
        waits.append(remote(near_out.at[way], near_in.at[way], near_send.at[way], near_recv.at[way], to))
    loads[3].wait()
    landed(sib_in.at[3], sib_recv.at[3])
    for way in (0, 1):
        landed(near_in.at[way], near_recv.at[way])
    for copy in waits[4:6]:
        copy.wait_send()
    sent_g = []
    for d in range(4):
        j = lax.rem(x + d, 4)
        done[j] = (own[3, j].astype(f32) + sib_in[3, j].astype(f32) + near_in[0, j].astype(f32) + near_in[1, j].astype(f32)).astype(bf)
        sent_g.append(exchange(done, dkv_own.at[x], g_send, g_recv, d))
    for d in range(4):
        h = lax.rem(x + 4 - d, 4)
        landed(odq_own.at[h], o_recv.at[d])
        landed(dkv_own.at[h], g_recv.at[d])
    for i, copy in enumerate(waits):
        if i not in (4, 5):
            copy.wait_send()
    for sent in (sent_o, sent_g):
        for d in range(4):
            if d == 0:
                @pl.when(swap)
                def _():
                    sent[d].wait_send()
            else:
                sent[d].wait_send()


def collect(odq, dkv, collective_id=1):
    hbm = pl.BlockSpec(memory_space=pl.ANY)
    dma = pltpu.SemaphoreType.DMA
    bf = jnp.bfloat16
    one = jax.ShapeDtypeStruct((4, ROWS, WIDE), bf)
    return pl.pallas_call(
        collect_kernel,
        out_shape=(one, one),
        in_specs=[hbm, hbm], out_specs=(hbm, hbm),
        scratch_shapes=[pltpu.VMEM((4, 4, ROWS, WIDE), bf), pltpu.VMEM((4, 4, ROWS, WIDE), bf), pltpu.VMEM((2, 2, ROWS, WIDE), bf),
            pltpu.VMEM((2, 4, ROWS, WIDE), bf), pltpu.VMEM((2, 4, ROWS, WIDE), bf), pltpu.VMEM((4, ROWS, WIDE), bf),
            dma((4,)), dma((4,)), dma((4,)), dma((4,)), dma((4,)), dma((2,)), dma((2,)), dma((2,)), dma((2,)), dma((4,)), dma((4,))],
        compiler_params=pltpu.CompilerParams(collective_id=collective_id, has_side_effects=True, vmem_limit_bytes=40 * 2**20),
        name="collect",
    )(odq, dkv)


PARTS = ((192, 768, True), (192, 768, False), (192, 384, True), (192, 384, False), (64, 128, True))


def reduce_kernel(wide, upper, lower, tiny, *refs):
    outs, refs = refs[:5], refs[5:]
    own, sib_in, far_in, near_in, far_two, near_two, y_in = (refs[5 * i : 5 * i + 5] for i in range(7))
    load_sem, send_sem, recv_sem = refs[35:]
    z, yl, x, yh, core = place()
    f32, bf = jnp.float32, jnp.bfloat16
    xs = [device(z, yl, lax.rem(x + d, 4), yh, core) for d in (1, 3)]
    zs = [device(lax.rem(z + d, 4), yl, x, yh, core) for d in (1, 3)]
    ys = [device(z, 1 - yl, x, yh, core), device(z, yl, x, 1 - yh, core), device(z, 1 - yl, x, 1 - yh, core)]
    sib = device(z, yl, x, yh, 1 - core)
    greet([sib] + xs + zs + ys)
    count = [0]
    sent = []

    def remote(src, dst, to, sem=None):
        if sem is None:
            sem = count[0]
            count[0] += 1
        copy = pltpu.make_async_remote_copy(src_ref=src, dst_ref=dst, send_sem=send_sem.at[sem], recv_sem=recv_sem.at[sem], device_id=to, device_id_type=MESH)
        copy.start()
        sent.append((src, sem, copy))
        return sem

    def arrive(ref, sem):
        landed(ref, recv_sem.at[sem])

    def piece(p, w, a):
        if p < 2:
            return (wide, upper)[p].at[pl.ds(pl.multiple_of(w * 192, 192), 192), pl.ds(pl.multiple_of(a * 768, 768), 768)]
        if p < 4:
            return lower.at[pl.ds(pl.multiple_of(w * 768 + a * 192, 192), 192), pl.ds(384 * (p - 2), 384)]
        return tiny.at[w, a]

    first = [x if part[2] else z for part in PARTS]
    second = [z if part[2] else x for part in PARTS]
    ring_one = [xs if part[2] else zs for part in PARTS]
    ring_two = [zs if part[2] else xs for part in PARTS]
    everyone = range(5)

    sib_sem = {}
    pairs = []
    for k, ahead in enumerate((2, 1, 3, 0)):
        for p in everyone:
            a = lax.rem(first[p] + ahead, 4)
            sem = count[0]
            count[0] += 1
            sib_sem[p, k] = sem
            for s in (0, 1):
                pltpu.make_async_copy(piece(p, 2 * s + core, a), own[p].at[k, s], load_sem.at[p * 4 + k]).start()
                pltpu.make_async_remote_copy(src_ref=piece(p, 2 * s + 1 - core, a), dst_ref=sib_in[p].at[k, s], send_sem=send_sem.at[sem], recv_sem=recv_sem.at[sem], device_id=sib, device_id_type=MESH).start()
            pairs.append((sib_in[p].at[k], sem))

    def gather_one(p, k):
        landed(own[p].at[k], load_sem.at[p * 4 + k])
        arrive(sib_in[p].at[k], sib_sem[p, k])

    def add(p, rows, into, terms):
        step = 16 if PARTS[p][1] > 384 or rows % 32 else 32

        def body(i, _):
            at = pl.ds(pl.multiple_of(i * step, step), step)
            total = into[at].astype(f32)
            for term in terms:
                total = total + term[at].astype(f32)
            into[at] = total.astype(bf)
            return 0
        lax.fori_loop(0, rows // step, body, 0)

    far_sem, near_sem = {}, {}
    for p in everyone:
        gather_one(p, 0)
        for s in (0, 1):
            add(p, PARTS[p][0], own[p].at[0, s], [sib_in[p].at[0, s]])
            far_sem[p, s] = remote(own[p].at[0, s], far_in[p].at[s], ring_one[p][s])
    for way in (0, 1):
        for p in everyone:
            k = 1 + way
            gather_one(p, k)
            add(p, PARTS[p][0], own[p].at[k, 1 - way], [sib_in[p].at[k, 1 - way]])
            arrive(far_in[p].at[way], far_sem[p, way])
            add(p, PARTS[p][0], own[p].at[k, way], [sib_in[p].at[k, way], far_in[p].at[way]])
            near_sem[p, way] = remote(own[p].at[k], near_in[p].at[way], ring_one[p][way])

    def quarter(p, b):
        rows = PARTS[p][0] // 4
        return pl.ds(pl.multiple_of(lax.rem(b, 4) * rows, rows), rows)

    far_sem2, near_sem2, y_sem = {}, {}, {}
    for p in everyone:
        gather_one(p, 3)
        for way in (0, 1):
            arrive(near_in[p].at[way], near_sem[p, way])
        for s in (0, 1):
            add(p, PARTS[p][0], own[p].at[3, s], [sib_in[p].at[3, s], near_in[p].at[0, s], near_in[p].at[1, s]])
        at = quarter(p, second[p] + 2)
        for s in (0, 1):
            far_sem2[p, s] = remote(own[p].at[3, s, at], far_two[p].at[s], ring_two[p][s])
    for way in (0, 1):
        for p in everyone:
            at = quarter(p, second[p] + 1 + 2 * way)
            arrive(far_two[p].at[way], far_sem2[p, way])
            add(p, PARTS[p][0] // 4, own[p].at[3, way, at], [far_two[p].at[way]])
            near_sem2[p, way] = remote(own[p].at[3, :, at], near_two[p].at[way], ring_two[p][way])
    for p in everyone:
        at = quarter(p, second[p])
        for way in (0, 1):
            arrive(near_two[p].at[way], near_sem2[p, way])
        for s in (0, 1):
            add(p, PARTS[p][0] // 4, own[p].at[3, s, at], [near_two[p].at[0, s], near_two[p].at[1, s]])
        for i, half in enumerate((yh, 1 - yh, 1 - yh)):
            y_sem[p, i] = remote(own[p].at[3, half, at], y_in[p].at[i], ys[i])
    ring_sem = {}
    for p in everyone:
        at = quarter(p, second[p])
        for i in range(3):
            arrive(y_in[p].at[i], y_sem[p, i])
        rows = PARTS[p][0] // 4
        total = own[p][3, yh, at].astype(f32)
        for i in range(3):
            total = total + y_in[p][i].astype(f32)
        outs[p][first[p], at] = total.astype(bf)
        mine = outs[p].at[first[p], at]
        for way in (0, 1):
            ring_sem[p, way] = remote(mine, mine, ring_two[p][way])

    relay_sem = {}
    for way in (0, 1):
        for p in everyone:
            b = lax.rem(second[p] + 3 - 2 * way, 4)
            arrive(outs[p].at[first[p], quarter(p, b)], ring_sem[p, way])
            rows = PARTS[p][0] // 4
            low, high = ((0, 32), (32, 48))[way] if rows == 48 else ((0, 16), (16, 16))[way]
            if high > low:
                part = outs[p].at[first[p], pl.ds(pl.multiple_of(b * rows + low, 16), high - low)]
                relay_sem[p, way] = (remote(part, part, ring_two[p][way]), low, high)
    last_sem = {}
    for p in everyone:
        rows = PARTS[p][0] // 4
        b = lax.rem(second[p] + 2, 4)
        for way in (0, 1):
            if (p, way) in relay_sem:
                sem, low, high = relay_sem[p, way]
                arrive(outs[p].at[first[p], pl.ds(pl.multiple_of(b * rows + low, 16), high - low)], sem)
        mine = outs[p].at[first[p]]
        for way in (0, 1):
            last_sem[p, way] = remote(mine, mine, ring_one[p][way])
    end_sem = {}
    for way in (0, 1):
        for p in everyone:
            block = outs[p].at[lax.rem(first[p] + 3 - 2 * way, 4)]
            arrive(block, last_sem[p, way])
            half = PARTS[p][0] // 2
            part = block.at[pl.ds(way * half, half)]
            end_sem[p, way] = remote(part, part, ring_one[p][way])
    for way in (0, 1):
        for p in everyone:
            half = PARTS[p][0] // 2
            arrive(outs[p].at[lax.rem(first[p] + 2, 4)].at[pl.ds(way * half, half)], end_sem[p, way])
    for ref, sem in pairs:
        landed(ref, send_sem.at[sem])
    for src, sem, copy in sent:
        copy.wait_send()


def reduce_all(wide, upper, lower, tiny, collective_id=2):
    hbm = pl.BlockSpec(memory_space=pl.ANY)
    vmem = pl.BlockSpec(memory_space=pltpu.VMEM)
    dma = pltpu.SemaphoreType.DMA
    bf = jnp.bfloat16
    scratch = []
    for lead in ((4, 2, 1), (4, 2, 1), (2, 0, 1), (2, 2, 1), (2, 0, 4), (2, 2, 4), (3, 0, 4)):
        for rows, columns, _ in PARTS:
            front = tuple(n for n in lead[:2] if n)
            scratch.append(pltpu.VMEM(front + (rows // lead[2], columns), bf))
    return pl.pallas_call(
        reduce_kernel,
        out_shape=tuple(jax.ShapeDtypeStruct((4, rows, columns), bf) for rows, columns, _ in PARTS),
        in_specs=[hbm] * 4, out_specs=(vmem,) * 5,
        scratch_shapes=scratch + [dma((20,)), dma((140,)), dma((140,))],
        compiler_params=pltpu.CompilerParams(collective_id=collective_id, has_side_effects=True, vmem_limit_bytes=50 * 2**20),
        name="reduce",
    )(wide, upper, lower, tiny)


def sum_gradients(gain_one, shift_one, qkv, qkv_bias, dense, gain_two, shift_two, up, up_bias, down, out_bias):
    bf, f32 = jnp.bfloat16, jnp.float32
    small = (gain_one, shift_one, gain_two, shift_two, out_bias, qkv_bias, up_bias)
    flat = jnp.concatenate([v.reshape(4, -1) for v in small], 1).astype(bf)
    tiny = jnp.pad(flat.reshape(4, 16, 144), ((0, 0), (0, 0), (0, 2048 - 144))).reshape(4, 4, 64, 128)
    wide = jnp.concatenate([qkv.astype(bf), dense.astype(bf)], 1)
    wide, upper, left, right, tiny = reduce_all(wide, up.astype(bf), down.astype(bf), tiny)
    wide = wide.astype(f32).transpose(1, 0, 2).reshape(192, 3072)
    upper = upper.astype(f32).transpose(1, 0, 2).reshape(192, 3072)
    lower = jnp.concatenate([left.astype(f32), right.astype(f32)], 2).reshape(768, 768)
    flat = tiny.astype(f32).reshape(16, 2048)[:, :144].reshape(-1)
    parts, start = [], 0
    for v in small:
        parts.append(flat[start : start + v.shape[0] // 4])
        start += v.shape[0] // 4
    gain_one, shift_one, gain_two, shift_two, out_bias, qkv_bias, up_bias = parts
    return gain_one, shift_one, wide[:, :2304], qkv_bias, wide[:, 2304:], gain_two, shift_two, upper, up_bias, lower, out_bias


D = 768
HEADS = 12
HD = 64
ROT = 16
TOK_DEV = 256


def layer_norm(values, norm_gain, norm_shift):
    row_mean = jnp.mean(values, -1, keepdims=True)
    centered = values - row_mean
    row_var = jnp.mean(centered * centered, -1, keepdims=True)
    return centered * lax.rsqrt(row_var + 1e-05) * norm_gain + norm_shift


def rotary_tables(positions):
    half_dims = ROT // 2
    exponents = jnp.arange(half_dims).astype(jnp.float32) * 2.0 / ROT
    inverse = 10000.0 ** (-exponents)
    angles = positions.astype(jnp.float32)[:, None] * inverse[None, :]
    cosine, sine = jnp.cos(angles), jnp.sin(angles)
    rest = jnp.ones((positions.shape[0], HD - ROT), jnp.float32)
    none = jnp.zeros((positions.shape[0], half_dims), jnp.float32)
    keep = jnp.concatenate([cosine, cosine, rest], 1)
    ahead = jnp.concatenate([-sine, none, 0.0 * rest], 1)
    behind = jnp.concatenate([none, sine, 0.0 * rest], 1)
    return tuple(jnp.tile(table, (1, HEADS)) for table in (keep, ahead, behind))


def rotate(rows, tables):
    keep, ahead, behind = tables
    return rows * keep + jnp.roll(rows, -8, 1) * ahead + jnp.roll(rows, 8, 1) * behind


def rotate_back(rows, tables):
    keep, ahead, behind = tables
    return rows * keep + jnp.roll(rows * ahead, 8, 1) + jnp.roll(rows * behind, -8, 1)


def contract(left_side, right_side, left_dim, right_dim):
    return lax.dot_general(
        left_side,
        right_side,
        (((left_dim,), (right_dim,)), ((), ())),
        preferred_element_type=jnp.float32,
    )


def gelu_exact(values):
    return jax.nn.gelu(values, approximate=False)


def slabs(first, second):
    both = jnp.stack([first.reshape(TOK_DEV, HEADS, HD), second.reshape(TOK_DEV, HEADS, HD)], 2)
    return both.reshape(TOK_DEV, 4, WIDE).transpose(1, 0, 2)


def unslab(pairs):
    both = pairs.transpose(1, 0, 2).reshape(TOK_DEV, HEADS, 2, HD)
    return both[:, :, 0].reshape(TOK_DEV, D), both[:, :, 1].reshape(TOK_DEV, D)


def on_device(
    tokens, cotangent, pairing, first_gain, first_shift, qkv_weight, qkv_bias, dense_weight,
    second_gain, second_shift, up_weight, up_bias, down_weight, out_bias,
):
    bf, f32 = jnp.bfloat16, jnp.float32
    total_blocks = 64
    offsets = jnp.arange(BLK, dtype=jnp.int32)
    ctx_index = lax.axis_index("ctx")
    core = lax.rem(lax.axis_index("wsh"), 2)
    seq_of_layout = jnp.stack([pairing, total_blocks - 1 - pairing], 1).reshape(-1)
    layout_of_seq = (
        jnp.zeros((total_blocks,), jnp.int32)
        .at[seq_of_layout]
        .set(jnp.arange(total_blocks, dtype=jnp.int32))
    )
    own_blocks = lax.dynamic_slice(seq_of_layout, (2 * ctx_index,), (2,))
    row_blocks = lax.dynamic_slice(seq_of_layout, (16 * (ctx_index // 8) + 8 * core,), (8,))
    local_pos = (own_blocks[:, None] * BLK + offsets[None, :]).reshape(-1)
    tables = rotary_tables(local_pos)
    query_scale = HD ** (-0.5)

    small = (first_gain, first_shift, second_gain, second_shift, out_bias, qkv_bias, up_bias)
    sizes = [v.shape[0] for v in small]
    gathered = lax.all_gather(jnp.concatenate(small), "wsh", axis=0)
    vectors, start = [], 0
    for size in sizes:
        vectors.append(gathered[:, start : start + size].reshape(-1).astype(f32))
        start += size
    gain_one, shift_one, gain_two, shift_two, out_offset, qkv_offset, up_offset = vectors
    qkv_matrix = lax.all_gather(qkv_weight, "wsh", axis=0, tiled=True)
    dense_matrix = lax.all_gather(dense_weight, "wsh", axis=0, tiled=True)
    up_matrix = lax.all_gather(up_weight, "wsh", axis=0, tiled=True)
    down_matrix = lax.all_gather(down_weight, "wsh", axis=0, tiled=True)

    inputs = tokens[0].astype(f32)
    grad_rows = cotangent[0]
    grad_float = grad_rows.astype(f32)
    normed_one = layer_norm(inputs, gain_one, shift_one).astype(bf)
    mixed = jnp.dot(normed_one, qkv_matrix, preferred_element_type=f32) + qkv_offset
    queries = (rotate(mixed[:, :D], tables) * query_scale).astype(bf)
    key_rows = rotate(mixed[:, D : 2 * D], tables).astype(bf)
    value_rows = mixed[:, 2 * D :].astype(bf)
    grad_attended = contract(grad_rows, dense_matrix, 1, 1).astype(bf)

    keys_values, queries_grads = spread(slabs(key_rows, value_rows), slabs(queries, grad_attended))
    attended_dq, grad_kv = attention(row_blocks, layout_of_seq, queries_grads.reshape(1024, WIDE), keys_values.reshape(8192, WIDE))
    attended_dq, grad_kv = collect(attended_dq.reshape(4, ROWS, WIDE), grad_kv.reshape(32, ROWS, WIDE))
    attended_low, grad_queries = unslab(attended_dq)
    grad_keys, grad_values = unslab(grad_kv)

    attention_out = jnp.dot(attended_low, dense_matrix, preferred_element_type=f32)
    normed_two = layer_norm(inputs, gain_two, shift_two).astype(bf)
    upper_rows = jnp.dot(normed_two, up_matrix, preferred_element_type=f32) + up_offset
    activated = gelu_exact(upper_rows).astype(bf)
    mlp_out = jnp.dot(activated, down_matrix, preferred_element_type=f32)
    layer_output = (inputs + attention_out + mlp_out + out_offset).astype(bf)[None]

    out_offset_grad = jnp.sum(grad_float, 0)
    dense_grad = contract(attended_low, grad_rows, 0, 0)
    down_grad = contract(activated, grad_rows, 0, 0)
    grad_activated = contract(grad_rows, down_matrix, 1, 1)
    gelu_back = jax.vjp(gelu_exact, upper_rows)[1]
    grad_upper = gelu_back(grad_activated)[0].astype(bf)
    up_grad = contract(normed_two, grad_upper, 0, 0)
    up_offset_grad = jnp.sum(grad_upper.astype(f32), 0)
    grad_normed_two = contract(grad_upper, up_matrix, 1, 1)

    grad_mixed = jnp.concatenate(
        [
            rotate_back(grad_queries.astype(f32) * query_scale, tables).astype(bf),
            rotate_back(grad_keys.astype(f32), tables).astype(bf),
            grad_values,
        ],
        1,
    )
    qkv_grad = contract(normed_one, grad_mixed, 0, 0)
    qkv_offset_grad = jnp.sum(grad_mixed.astype(f32), 0)
    grad_normed_one = contract(grad_mixed, qkv_matrix, 1, 1)
    grad_in_one, gain_one_grad, shift_one_grad = jax.vjp(layer_norm, inputs, gain_one, shift_one)[1](grad_normed_one)
    grad_in_two, gain_two_grad, shift_two_grad = jax.vjp(layer_norm, inputs, gain_two, shift_two)[1](grad_normed_two)
    input_grad = (grad_float + grad_in_one + grad_in_two).astype(bf)[None]

    return (layer_output, input_grad) + sum_gradients(
        gain_one_grad, shift_one_grad, qkv_grad, qkv_offset_grad, dense_grad, gain_two_grad, shift_two_grad,
        up_grad, up_offset_grad, down_grad, out_offset_grad,
    )


def solution(mesh):
    rows, split, flat = P("wsh", "ctx", None), P("wsh", None), P("wsh")
    return jax.shard_map(
        on_device,
        mesh=mesh,
        in_specs=(rows, rows, P(), flat, flat, split, flat, split, flat, flat, split, flat, split, flat),
        out_specs=(rows, rows, flat, flat, split, flat, split, flat, flat, split, flat, split, flat),
        check_vma=False,
    )
```

time: 2380 us -> 444 us (0.19)
  waiting for transfers between devices: 1030 us -> 41.4 us
  local copies, waits for them, and re-layouts: 624 us -> 32.3 us
  Pallas kernels: 0 us -> 288 us
  matrix products: 294 us -> 41.5 us
  other arithmetic: 230 us -> 13.1 us
  blocking collectives: 124 us -> 6.7 us
  loops' own time: 40.4 us -> 0 us
    reduce_scatter x6 -> x0, waiting for transfers between devices: 517 us -> none  [the longest x1 187 us: on_device(): lax.psum_scatter(running[2].reshape(-1, D).astype(jnp.bfloat16), 'ctx', s...]
    all_gather x6 -> x4, waiting for transfers between devices: 333 us -> 38.9 us  [the longest x1 33.2 us: on_device(): qkv_matrix = lax.all_gather(qkv_weight, 'wsh', axis=0, tiled=True)]
    pallas_call x0 -> x4, Pallas kernels: none -> 288 us  [the longest x1 111 us: attention(): pl.pallas_call(functools.partial(attn_kernel, chunk), out_shape=(jax.Shap...]
    gather x136 -> x0, local copies, waits for them, and re-layouts: 271 us -> none  [the longest x34 99.4 us: tile_scores(): key_tile = key_stack[chosen].reshape(tile_rows, HEADS, HD)]
    dot_general x123 -> x4, matrix products: 265 us -> 19.8 us  [the longest x1 11.5 us: on_device(): jnp.dot(normed_two, up_matrix, preferred_element_type=f32) + up_offset]
    psum x1 -> x0, waiting for transfers between devices: 180 us -> none  [on_device(): lax.psum(for_sending(tuple(grad_parts)), 'ctx')]
    reshape x85 -> x14, local copies, waits for them, and re-layouts: 168 us -> 8.22 us  [the longest x7 3.76 us: sum_gradients(): flat = jnp.concatenate([v.reshape(4, -1) for v in small], 1).astype(bf)]
    scatter-add x34 -> x0, other arithmetic: 136 us -> none  [the longest x17 72.3 us: tile_step(): key_grads = running[1].at[chosen].add(key_part.reshape(group_size, BLK, D))]
  transfers between devices with their start and end apart: 13 -> 4, of which waited for: 11 -> 2; matrix products, arithmetic and copies ran while one was open for 47% -> 10% of each run, Pallas kernels for 0% -> 46%
where the time goes in v1:
time: 444 us; the launch traced here: 438 us
  Pallas kernels  288 us (65%)
  matrix products  41.5 us (9%)
  waiting for transfers between devices  41.4 us (9%)
  local copies, waits for them, and re-layouts  32.3 us (7%)
  between operations  14.8 us (3%)
  other arithmetic  13.1 us (3%)
  blocking collectives  6.7 us (2%)
    pallas_call x1, Pallas kernels, attention(): pl.pallas_call(functools.partial(attn_kernel, chunk), out_shape=(jax.Shap...  111 us
    pallas_call x1, Pallas kernels, reduce_all(): pl.pallas_call(reduce_kernel, out_shape=tuple((jax.ShapeDtypeStruct((4, r...  86.5 us
    pallas_call x1, Pallas kernels, collect(): pl.pallas_call(collect_kernel, out_shape=(one, one), in_specs=[hbm, hbm],...  45.3 us
    pallas_call x1, Pallas kernels, spread(): pl.pallas_call(spread_kernel, out_shape=(jax.ShapeDtypeStruct((32, ROWS,...  44.7 us
    all_gather x1, waiting for transfers between devices, on_device(): qkv_matrix = lax.all_gather(qkv_weight, 'wsh', axis=0, tiled=True)  33.2 us
    dot_general x8, matrix products, contract(): lax.dot_general(left_side, right_side, (((left_dim,), (right_dim,)), ((),...  21.7 us
    dot_general x1, matrix products, on_device(): jnp.dot(normed_two, up_matrix, preferred_element_type=f32) + up_offset  11.5 us
  transfers between devices with their start and end apart: 4, of which 2 were waited for; matrix products, arithmetic and copies ran while one was open for 10% of the time, Pallas kernels for 46%

profile of v1, /device:TPU:0, one launch (start us, length us, event | category | flops | bytes accessed | tf_op | source)
XLA Modules:
  0.0 437.8 jit_solution(4215639423262690447)
XLA Ops:
  7.2 0.7 all-gather.9.cloned.1.call-update
  8.0 0.7 all-gather.7.cloned.1.call-update
  8.7 0.7 all-gather.11.cloned.1.call-update
  9.5 0.5 all-gather.13.cloned.1.call-update
  11.0 0.5 copy-done.14
  12.2 0.9 tile.31
  13.2 1.4 copy.55
  14.8 6.7 %all-gather.1 = bf16[4,1,2304]{2,1,0:T(2,128)(2,1)S(1)} all-gather(bf16[1,1,2304]{2,1,0:T(2,128)(2,1)S(1)} %reshape.347), channel_id=2, replica_groups=mesh['ctx'=32,'wsh'=4] {'wsh'}, dimensions={0}, use_global_device_ids=true | all-gather | bytes 23040 | tf_op jit(solution)/shard_map/all_gather | solution.py:648
  21.6 0.7 reshape.321
  22.4 0.7 reshape.322
  23.1 0.6 dynamic_slice.6.qpos
  23.8 0.6 reshape.325
  24.5 0.7 reshape.307
  25.2 0.7 reshape.326
  25.8 1.3 scatter_custom_fusion.lay
  27.5 0.6 fusion.51
  28.1 5.6 %all-gather.9.cloned.1.call-done = bf16[768,768]{1,0:T(8,128)(2,1)} async-done(((bf16[192,768]{1,0:T(8,128)(2,1)}), bf16[768,768]{1,0:T(8,128)(2,1)}) %all-gather.9.cloned.1.call-update) | async-done | bytes 1179664 | tf_op jit(solution)/shard_map/all_gather | solution.py:655
  33.7 1.8 convolution_convert_fusion.4
  35.5 0.9 copy.64
  36.4 33.2 %all-gather.7.cloned.1.call-done = bf16[768,2304]{1,0:T(8,128)(2,1)} async-done(((bf16[192,2304]{1,0:T(8,128)(2,1)}), bf16[768,2304]{1,0:T(8,128)(2,1)}) %all-gather.7.cloned.1.call-update) | async-done | bytes 3538960 | tf_op jit(solution)/shard_map/all_gather | solution.py:654
  69.7 3.2 convolution_add_fusion
  72.9 0.8 slice.240
  73.8 0.5 fusion.67
  74.3 1.4 fusion.36
  75.6 1.2 copy.63
  76.9 1.1 pad_maximum_fusion.4
  78.0 1.2 copy.66
  79.7 1.2 copy.59
  80.8 44.7 %spread.1 = (bf16[32,256,384]{2,1,0:T(8,128)(2,1)}, bf16[4,256,384]{2,1,0:T(8,128)(2,1)}) custom-call(bf16[4,256,384]{2,1,0:T(8,128)(2,1)} %bitcast.166, bf16[4,256,384]{2,1,0:T(8,128)(2,1)} %bitcast.164), custom_call_target="tpu_custom_call" | custom-call | tf_op jit(solution)/shard_map/spread/pallas_call | solution.py:233
  125.5 111.4 %attention.1 = (bf16[1024,384]{1,0:T(8,128)(2,1)}, bf16[8192,384]{1,0:T(8,128)(2,1)}) custom-call(s32[8]{0:T(128)} %dynamic_slice.6.qpos, s32[64]{0:T(128)} %scatter_custom_fusion.lay, bf16[1024,384]{1,0:T(8,128)(2,1)} %bitcast.180, bf16[8192,384]{1,0:T(8,128)(2,1)} %bitcast.159), custom_call_target="tpu_custom_call" | custom-call | tf_op jit(solution)/shard_map/attention/pallas_call | solution.py:113
  236.9 2.8 copy-done
  239.7 1.1 copy-done.1
  240.8 45.3 %collect.1 = (bf16[4,256,384]{2,1,0:T(8,128)(2,1)S(1)}, bf16[4,256,384]{2,1,0:T(8,128)(2,1)S(1)}) custom-call(bf16[4,256,384]{2,1,0:T(8,128)(2,1)S(1)} %bitcast.154, bf16[32,256,384]{2,1,0:T(8,128)(2,1)S(1)} %bitcast.153), custom_call_target="tpu_custom_call" | custom-call | tf_op jit(solution)/shard_map/collect/pallas_call | solution.py:346
  286.9 1.1 convert_multiply_fusion
  288.4 0.6 copy-done.15
  289.0 0.5 fusion.41
  289.4 0.4 fusion.59
  289.8 0.7 reshape.308
  290.5 0.5 convolution_convert_fusion.3
  291.0 1.3 convolution_convert_fusion.2
  292.3 2.8 pad_maximum_fusion.wide
  295.1 11.5 %multiply_convert_fusion = (bf16[256,3072]{1,0:T(8,128)(2,1)S(1)}, f32[256,3072]{1,0:T(8,128)}, f32[256,3072]{1,0:T(8,128)}) fusion(f32[3072]{0:T(1024)} %reshape.325, bf16[768,3072]{1,0:T(8,128)(2,1)} %all-gather.11.cloned.1.call-done, bf16[1,256,768]{2,1,0:T(8,128)(2,1)S(1)} %copy-done.2, f32[768]{0:T(1024)S(1)} %reshape.324, f32[768]{0:T(1024)S(1)} %reshape.323, ...), kind=kOutput, calls=%fused_computation.10 | convolution fusion | flops 1261043712 | bytes 12996608 | tf_op jit(solution)/shard_map/dot_general | solution.py:677
  306.7 7.4 %fusion.70 = (bf16[3072]{0:T(1024)(128)(2,1)}, bf16[256,3072]{1,0:T(8,128)(2,1)S(1)}) fusion(f32[256,3072]{1,0:T(8,128)} %get-tuple-element.48, f32[256,3072]{1,0:T(8,128)} %get-tuple-element.86, bf16[3072,768]{1,0:T(8,128)(2,1)} %all-gather.13.cloned.1.call-done, bf16[1,256,768]{2,1,0:T(8,128)(2,1)S(1)} %copy-done.3), kind=kOutput, calls=%fused_computation.138 | convolution fusion | flops 1219752960 | bytes 12982272 | tf_op jit(solution)/shard_map/dot_general | solution.py:603
  314.1 3.8 convolution_convert_fusion.1.upper
  317.8 1.5 fusion.72
  319.3 0.5 copy-done.34
  319.8 1.8 fusion.64
  321.7 0.7 fusion.26
  322.7 0.8 reshape.304
  323.5 0.8 reshape.306
  324.3 0.7 reshape.309
  325.0 0.8 concatenate.66
  326.1 3.6 convolution_convert_fusion.lower
  329.7 86.5 %reduce.8 = (bf16[4,192,768]{2,1,0:T(8,128)(2,1)S(1)}, bf16[4,192,768]{2,1,0:T(8,128)(2,1)S(1)}, bf16[4,192,384]{2,1,0:T(8,128)(2,1)S(1)}, bf16[4,192,384]{2,1,0:T(8,128)(2,1)S(1)}, bf16[4,64,128]{2,1,0:T(8,128)(2,1)S(1)}) custom-call(bf16[768,3072]{1,0:T(8,128)(2,1)} %pad_maximum_fusion.wide, bf16[768,3072]{1,0:T(8,128)(2,1)} %convolution_convert_fusion.1.upper, ...), custom_call_target="tpu_custom_call" | custom-call | tf_op jit(solution)/shard_map/reduce/pallas_call | solution.py:535
  416.6 1.3 slice.207
  418.0 0.9 slice.209
  419.0 0.6 fusion.69
  419.6 0.7 slice.208
  420.3 0.6 slice.212
  421.0 1.7 bitcast_convert_fusion
  422.9 1.7 copy.75
  424.6 1.3 fusion.42
  425.9 3.8 fusion.71
  429.7 1.3 fusion.9
  (140 shorter events, 5.9 us)
Async XLA Ops:
  7.2 2.8 copy-start.32
  7.2 26.5 %all-gather.9.cloned.1.call-start = ((), (), s32[]{:S(2)}) async-start(), calls=%async_computation.1 | async-start | bytes 1474560 | tf_op jit(solution)/shard_map/all_gather | solution.py:655
  7.9 61.7 %all-gather.7.cloned.1.call-start = ((), (), s32[]{:S(2)}) async-start(), calls=%async_computation | async-start | bytes 4423680 | tf_op jit(solution)/shard_map/all_gather | solution.py:654
  8.7 286.4 %all-gather.11.cloned.1.call-start = ((), (), s32[]{:S(2)}) async-start(), calls=%async_computation.2 | async-start | bytes 5898240 | tf_op jit(solution)/shard_map/all_gather | solution.py:656
  9.4 297.2 %all-gather.13.cloned.1.call-start = ((), (), s32[]{:S(2)}) async-start(), calls=%async_computation.3 | async-start | bytes 5898240 | tf_op jit(solution)/shard_map/all_gather | solution.py:657
  10.9 0.6 copy-start.14
  10.9 3.7 copy-start.16
  10.9 3.7 copy-start.17
  11.5 3.1 copy-start.25
  11.5 3.1 copy-start.26
  11.5 3.1 copy-start.27
  11.5 3.1 copy-start.28
  11.5 3.1 copy-start.29
  11.5 3.1 copy-start.30
  11.6 3.1 copy-start.31
  11.6 12.8 %copy-start.3 = (bf16[1,256,768]{2,1,0:T(8,128)(2,1)S(1)}, bf16[1,256,768]{2,1,0:T(8,128)(2,1)}, u32[]{:S(2)}) copy-start(bf16[1,256,768]{2,1,0:T(8,128)(2,1)} %param.15) | copy-start | bytes 1179652
  11.9 15.3 %copy-start.2 = (bf16[1,256,768]{2,1,0:T(8,128)(2,1)S(1)}, bf16[1,256,768]{2,1,0:T(8,128)(2,1)}, u32[]{:S(2)}) copy-start(bf16[1,256,768]{2,1,0:T(8,128)(2,1)} %param.14) | copy-start | bytes 1179652
  27.5 0.6 copy-start.22
  75.6 3.7 copy-start.13
  236.9 2.8 copy-start
  239.7 1.1 copy-start.1
  288.1 0.8 copy-start.15
  288.9 1.5 copy-start.5
  288.9 2.0 copy-start.18
  289.0 2.0 copy-start.24
  306.6 19.4 %copy-start.7 = (bf16[256,3072]{1,0:T(8,128)(2,1)}, bf16[256,3072]{1,0:T(8,128)(2,1)S(1)}, u32[]{:S(2)}) copy-start(bf16[256,3072]{1,0:T(8,128)(2,1)S(1)} %get-tuple-element.47) | copy-start | bytes 4718596
  306.7 7.4 %copy-start.19 = (f32[256]{0:T(256)S(1)}, f32[256]{0:T(256)}, u32[]{:S(2)}) copy-start(f32[256]{0:T(256)} %fusion.51) | copy-start | bytes 3076
  314.0 3.8 copy-start.33
  317.8 2.0 copy-start.34
  319.8 1.9 copy-start.9
  319.8 1.9 copy-start.23
  321.7 0.9 copy-start.11
  422.8 1.7 copy-start.10
  422.8 1.7 copy-start.12
  422.8 1.7 copy-start.20
  422.8 3.0 copy-start.8
  425.9 3.9 copy-start.4
  425.9 3.9 copy-start.6
  425.9 3.9 copy-start.21
Sparse Core Ops, SparseCore 0:
  9.7 23.9 all-gather.8
  35.4 34.2 all-gather.6
  71.3 57.7 all-gather.10
  130.7 40.8 all-gather.12

commit v2 on v1

--- a/solution.py
+++ b/solution.py
@@ -10,7 +10,7 @@
 G = 3; BLK = 128; LOG2E = 1.4426950408889634
 NEG = -1e30
 
-def attn_kernel(chunk, qpos, lay, qdo, kv_hbm, odq, dkv_hbm, kv, kvt, acc, stage, sem, osem):
+def attn_kernel(chunk, qpos, lay, qdo, kv_hbm, odq, dkv_hbm, kv, kvt, acc, probs, grads, tops, stage, sem, osem):
     blocks = chunk // BLK
     nblk = kv.shape[0] // BLK
     f32, bf = jnp.float32, jnp.bfloat16
@@ -37,24 +37,32 @@
         last = b // blocks
         pairs = [qdo[qrows, h * 128:(h + 1) * 128] for h in range(G)]
         turned = [p.astype(f32).T for p in pairs]
-        q_side = [jnp.where(upper, t, 0.0).astype(bf) for t in turned]
-        wide = [jnp.concatenate([q_side[h], jnp.where(upper, 0.0, turned[h]).astype(bf)], 1) for h in range(G)]
+        wide = [jnp.concatenate([jnp.where(upper, turned[h], 0.0).astype(bf), jnp.where(upper, 0.0, turned[h]).astype(bf)], 1) for h in range(G)]
         key_i = lax.broadcasted_iota(jnp.int32, (chunk, BLK), 0)
         row_i = lax.broadcasted_iota(jnp.int32, (chunk, BLK), 1) + (b - last * blocks) * BLK
 
         def fwd(c, state, masked):
             at = pl.ds(pl.multiple_of(c * chunk, chunk), chunk)
             out = []
+            every = [jnp.dot(kv[at, h * 128:(h + 1) * 128], wide[h], preferred_element_type=f32) for h in range(G)]
+            kept = []
             for h in range(G):
                 m, l, o = state[h]
-                s = jnp.dot(kv[at, h * 128:(h + 1) * 128], q_side[h], preferred_element_type=f32)
+                s = every[h][:, :128]
+                grads[at, h * 128:(h + 1) * 128] = every[h][:, 128:]
                 if masked:
                     s = jnp.where(key_i <= row_i, s, NEG)
                 new = jnp.maximum(m, jnp.max(s, 0, keepdims=True))
                 p = jnp.exp(s - new)
                 a = jnp.exp(m - new)
                 l = l * a + jnp.sum(p, 0, keepdims=True)
-                o = o * a + jnp.dot(kvt[h * 128 + 64:(h + 1) * 128, at], p.astype(bf), preferred_element_type=f32)
+                p = p.astype(bf)
+                probs[at, h * 128:(h + 1) * 128] = p
+                tops[c, h] = jnp.broadcast_to(new, (8, BLK))
+                kept.append((new, l, o * a, p))
+            for h in range(G):
+                new, l, o, p = kept[h]
+                o = o + jnp.dot(kvt[h * 128 + 64:(h + 1) * 128, at], p, preferred_element_type=f32)
                 out.append((new, l, o))
             return tuple(out)
 
@@ -70,24 +78,22 @@
             delta.append(jnp.sum(o * turned[h][64:], 0, keepdims=True))
         narrow = [jnp.concatenate([jnp.where(left, pairs[h], jnp.zeros_like(pairs[h])), jnp.where(left, jnp.zeros_like(pairs[h]), pairs[h])], 0) for h in range(G)]
 
-        def bwd(c, state, masked):
+        def bwd(c, state):
             at = pl.ds(pl.multiple_of(c * chunk, chunk), chunk)
-            out = []
+            out, work = [], []
             for h in range(G):
                 cols = slice(h * 128, (h + 1) * 128)
-                both = jnp.dot(kv[at, cols], wide[h], preferred_element_type=f32)
-                p = jnp.exp(both[:, :128] - lse[h])
-                if masked:
-                    p = jnp.where(key_i <= row_i, p, 0.0)
-                ds = (p * (both[:, 128:] - delta[h])).astype(bf)
-                pair = jnp.concatenate([ds, p.astype(bf)], 1)
-                acc[at, cols] += jnp.dot(pair, narrow[h], preferred_element_type=f32)
+                p = probs[at, cols].astype(f32) * jnp.exp(tops[c, h, 0:1] - lse[h])
+                ds = (p * (grads[at, cols] - delta[h])).astype(bf)
+                work.append((jnp.concatenate([ds, p.astype(bf)], 1), ds))
+            for h in range(G):
+                pair, ds = work[h]
+                acc[at, h * 128:(h + 1) * 128] += jnp.dot(pair, narrow[h], preferred_element_type=f32)
                 out.append(state[h] + jnp.dot(kvt[h * 128:h * 128 + 64, at], ds, preferred_element_type=f32))
             return tuple(out)
 
         dq = tuple(jnp.zeros((64, BLK), f32) for _ in range(G))
-        dq = lax.fori_loop(0, last, lambda c, s: bwd(c, s, False), dq)
-        dq = bwd(last, dq, True)
+        dq = lax.fori_loop(0, last + 1, bwd, dq)
         for h in range(G):
             odq[qrows, h * 128:(h + 1) * 128] = jnp.concatenate([outs[h], dq[h]], 0).T.astype(bf)
         return 0
@@ -115,9 +121,10 @@
         out_shape=(jax.ShapeDtypeStruct(qdo.shape, jnp.bfloat16), jax.ShapeDtypeStruct(kv.shape, jnp.bfloat16)),
         in_specs=[smem, smem, vmem, hbm], out_specs=(vmem, hbm),
         scratch_shapes=[pltpu.VMEM((n, G * 128), jnp.bfloat16), pltpu.VMEM((G * 128, n), jnp.bfloat16),
-            pltpu.VMEM((n, G * 128), jnp.float32), pltpu.VMEM((8, BLK, G * 128), jnp.bfloat16),
+            pltpu.VMEM((n, G * 128), jnp.float32), pltpu.VMEM((n, G * 128), jnp.bfloat16), pltpu.VMEM((n, G * 128), jnp.float32), pltpu.VMEM((n // chunk, G, 8, BLK), jnp.float32),
+            pltpu.VMEM((8, BLK, G * 128), jnp.bfloat16),
             pltpu.SemaphoreType.DMA((n // BLK,)), pltpu.SemaphoreType.DMA((8,))],
-        compiler_params=pltpu.CompilerParams(vmem_limit_bytes=56 * 2**20),
+        compiler_params=pltpu.CompilerParams(vmem_limit_bytes=62 * 2**20),
         name="attention",
     )(qpos, lay, qdo, kv)
 
@@ -150,106 +157,54 @@
     pltpu.make_async_copy(ref, ref, sem).wait()
 
 
-def spread_kernel(kvs, qds, kv_all, qdo, kv_send, kv_recv, q_send, q_recv, z_send, z_recv, half_send, half_recv, sib_send, sib_recv):
+TILE = 384
+
+
+def erf(values):
+    v = jnp.clip(values, -4.0, 4.0)
+    s = v * v
+    top = jnp.float32(-2.72614225801306e-10)
+    for coefficient in (2.77068142495902e-08, -2.10102402082508e-06, -5.69250639462346e-05, -7.34990630326855e-04, -2.95459980854025e-03, -1.60960333262415e-02):
+        top = top * s + coefficient
+    low = jnp.float32(-1.45660718464996e-05)
+    for coefficient in (-2.13374055278905e-04, -1.68282697438203e-03, -7.37332916720468e-03, -1.42647390514189e-02):
+        low = low * s + coefficient
+    return v * top / low
+
+
+def collect_kernel(odq, dkv, normed, grad, up_hbm, up_bias, down_hbm, odq_own, dkv_own, mlp_out, back_out, up_grad, down_grad, bias_grad, own, sib_in, far_in, near_out, near_in, done,
+                   load_sem, o_send, o_recv, sib_send, sib_recv, far_send, far_recv, near_send, near_recv, g_send, g_recv,
+                   up, down_w, up_stage, down_stage, up_sem, down_sem, in_sem):
     z, yl, x, yh, core = place()
     swap = yl != core
     partner = [device(z, core, lax.rem(x + d, 4), yh, yl) for d in range(4)]
-    up = device(lax.rem(z + 1, 4), yl, x, yh, core)
-    down = device(lax.rem(z + 3, 4), yl, x, yh, core)
+    above = device(lax.rem(z + 1, 4), yl, x, yh, core)
+    below = device(lax.rem(z + 3, 4), yl, x, yh, core)
     sib = device(z, yl, x, yh, 1 - core)
-    greet(partner[1:] + [up, down, sib], partner[0], lax.rem(yl + core, 2))
-
-    def slot(zz, cc, d):
-        return kv_all.at[lax.rem(zz, 4) * 8 + cc * 4 + lax.rem(x + 4 - d, 4)]
-
-    def remote(src, dst, send, recv, to):
-        copy = pltpu.make_async_remote_copy(src_ref=src, dst_ref=dst, send_sem=send, recv_sem=recv, device_id=to, device_id_type=MESH)
+    greet(partner[1:] + [above, below, sib], partner[0], lax.rem(yl + core, 2))
+    f32, bf = jnp.float32, jnp.bfloat16
+    fetch = [pltpu.make_async_copy(up_hbm, up, in_sem.at[0]), pltpu.make_async_copy(down_hbm, down_w, in_sem.at[1])]
+    for copy in fetch:
         copy.start()
-        return copy
-
-    def exchange(src, dst_of, send, recv):
-        sent = [None] * 4
-        for d in (0, 2, 1, 3):
-            h = lax.rem(x + d, 4)
-            args = (src.at[h], dst_of, send.at[d], recv.at[d], partner[d])
-            if d == 0:
-                @pl.when(swap)
-                def _():
-                    remote(*args)
-                @pl.when(jnp.logical_not(swap))
-                def _():
-                    pltpu.make_async_copy(args[0], args[1], args[3]).start()
-            else:
-                remote(*args)
-            sent[d] = pltpu.make_async_remote_copy(src_ref=args[0], dst_ref=args[1], send_sem=args[2], recv_sem=args[3], device_id=args[4], device_id_type=MESH)
-        return sent
-
-    waits = []
-    mine = z * 8 + yl * 4 + x
-    sent_kv = exchange(kvs, kv_all.at[mine], kv_send, kv_recv)
-    sent_q = exchange(qds, qdo.at[x], q_send, q_recv)
-    for d in (0, 1, 3, 2):
-        here = slot(z, core, d)
-        landed(here, kv_recv.at[d])
-        waits.append(remote(here, here, z_send.at[0, d], z_recv.at[0, d], up))
-        waits.append(remote(here, here, z_send.at[1, d], z_recv.at[1, d], down))
-        waits.append(remote(here, here, sib_send.at[0, d], sib_recv.at[0, d], sib))
-    half = ROWS // 2
-    for d in (0, 1, 3, 2):
-        for way, zz, to in ((0, z + 3, up), (1, z + 1, down)):
-            here = slot(zz, core, d)
-            landed(here, z_recv.at[way, d])
-            part = here.at[pl.ds(way * half, half)]
-            waits.append(remote(part, part, half_send.at[way, d], half_recv.at[way, d], to))
-            waits.append(remote(here, here, sib_send.at[1 + way, d], sib_recv.at[1 + way, d], sib))
-    for d in (0, 1, 3, 2):
-        for way in (0, 1):
-            part = slot(z + 2, core, d).at[pl.ds(way * half, half)]
-            landed(part, half_recv.at[way, d])
-            waits.append(remote(part, part, sib_send.at[3 + way, d], sib_recv.at[3 + way, d], sib))
-    other = 1 - core
-    for d in range(4):
-        landed(slot(z, other, d), sib_recv.at[0, d])
-        landed(slot(z + 3, other, d), sib_recv.at[1, d])
-        landed(slot(z + 1, other, d), sib_recv.at[2, d])
-        for way in (0, 1):
-            landed(slot(z + 2, other, d).at[pl.ds(way * half, half)], sib_recv.at[3 + way, d])
-        landed(qdo.at[lax.rem(x + 4 - d, 4)], q_recv.at[d])
-    for copy in waits:
-        copy.wait_send()
-    for sent in (sent_kv, sent_q):
-        for d in range(4):
-            if d == 0:
-                @pl.when(swap)
-                def _():
-                    sent[d].wait_send()
-            else:
-                sent[d].wait_send()
-
-
-def spread(kvs, qds, collective_id=0):
-    hbm = pl.BlockSpec(memory_space=pl.ANY)
-    dma = pltpu.SemaphoreType.DMA
-    return pl.pallas_call(
-        spread_kernel,
-        out_shape=(jax.ShapeDtypeStruct((32, ROWS, WIDE), jnp.bfloat16), jax.ShapeDtypeStruct((4, ROWS, WIDE), jnp.bfloat16)),
-        in_specs=[hbm, hbm], out_specs=(hbm, hbm),
-        scratch_shapes=[dma((4,)), dma((4,)), dma((4,)), dma((4,)), dma((2, 4)), dma((2, 4)), dma((2, 4)), dma((2, 4)), dma((5, 4)), dma((5, 4))],
-        compiler_params=pltpu.CompilerParams(collective_id=collective_id, has_side_effects=True),
-        name="spread",
-    )(kvs, qds)
-
-
-def collect_kernel(odq, dkv, odq_own, dkv_own, own, sib_in, far_in, near_out, near_in, done,
-                   load_sem, o_send, o_recv, sib_send, sib_recv, far_send, far_recv, near_send, near_recv, g_send, g_recv):
-    z, yl, x, yh, core = place()
-    swap = yl != core
-    partner = [device(z, core, lax.rem(x + d, 4), yh, yl) for d in range(4)]
-    up = device(lax.rem(z + 1, 4), yl, x, yh, core)
-    down = device(lax.rem(z + 3, 4), yl, x, yh, core)
-    sib = device(z, yl, x, yh, 1 - core)
-    greet(partner[1:] + [up, down, sib], partner[0], lax.rem(yl + core, 2))
-    f32, bf = jnp.float32, jnp.bfloat16
+
+    def dot(left, right, left_dim, right_dim):
+        return lax.dot_general(left, right, (((left_dim,), (right_dim,)), ((), ())), preferred_element_type=f32)
+
+    def feed(t, _):
+        at = pl.ds(pl.multiple_of(t * TILE, TILE), TILE)
+        values = dot(normed[...], up[:, at], 1, 0) + up_bias[0:1, at]
+        inner = 0.5 + 0.5 * erf(values * 0.7071067811865476)
+        slope = inner + values * (0.3989422804014327 * jnp.exp(-0.5 * values * values))
+        active = (values * inner).astype(bf)
+        grads = (dot(grad[...], down_w[at], 1, 1) * slope).astype(bf)
+        mlp_out[...] += dot(active, down_w[at], 1, 0)
+        back_out[...] += dot(grads, up[:, at], 1, 1)
+        bias_grad[0:1, at] = jnp.sum(grads.astype(f32), 0, keepdims=True)
+        up_stage[t] = dot(normed[...], grads, 0, 0).astype(bf)
+        down_stage[at] = dot(active, grad[...], 0, 0).astype(bf)
+        pltpu.make_async_copy(up_stage.at[t], up_grad.at[:, at], up_sem.at[t]).start()
+        pltpu.make_async_copy(down_stage.at[at], down_grad.at[at], down_sem.at[t]).start()
+        return 0
 
     def remote(src, dst, send, recv, to):
         copy = pltpu.make_async_remote_copy(src_ref=src, dst_ref=dst, send_sem=send, recv_sem=recv, device_id=to, device_id_type=MESH)
@@ -292,12 +247,18 @@
             return 0
         lax.fori_loop(0, 8, step, 0)
 
+    mlp_out[...] = jnp.zeros_like(mlp_out)
+    back_out[...] = jnp.zeros_like(back_out)
+    for copy in fetch:
+        copy.wait()
+    lax.fori_loop(0, 1, feed, 0)
     loads[0].wait()
     landed(sib_in.at[0], sib_recv.at[0])
     add(done, 0)
-    for way, to in ((0, up), (1, down)):
+    for way, to in ((0, above), (1, below)):
         waits.append(remote(done.at[pl.ds(2 * way, 2)], far_in.at[way], far_send.at[way], far_recv.at[way], to))
-    for way, to in ((0, up), (1, down)):
+    lax.fori_loop(1, 3, feed, 0)
+    for way, to in ((0, above), (1, below)):
         k = 1 + way
         loads[k].wait()
         landed(sib_in.at[k], sib_recv.at[k])
@@ -310,6 +271,7 @@
             return 0
         lax.fori_loop(0, 4, more, 0)
         waits.append(remote(near_out.at[way], near_in.at[way], near_send.at[way], near_recv.at[way], to))
+    lax.fori_loop(3, 5, feed, 0)
     loads[3].wait()
     landed(sib_in.at[3], sib_recv.at[3])
     for way in (0, 1):
@@ -321,6 +283,11 @@
         j = lax.rem(x + d, 4)
         done[j] = (own[3, j].astype(f32) + sib_in[3, j].astype(f32) + near_in[0, j].astype(f32) + near_in[1, j].astype(f32)).astype(bf)
         sent_g.append(exchange(done, dkv_own.at[x], g_send, g_recv, d))
+    lax.fori_loop(5, 8, feed, 0)
+    for t in range(8):
+        at = pl.ds(t * TILE, TILE)
+        pltpu.make_async_copy(up_stage.at[t], up_grad.at[:, at], up_sem.at[t]).wait()
+        pltpu.make_async_copy(down_stage.at[at], down_grad.at[at], down_sem.at[t]).wait()
     for d in range(4):
         h = lax.rem(x + 4 - d, 4)
         landed(odq_own.at[h], o_recv.at[d])
@@ -338,21 +305,230 @@
                 sent[d].wait_send()
 
 
-def collect(odq, dkv, collective_id=1):
+def collect(odq, dkv, normed, grad, up, up_bias, down, collective_id=1):
     hbm = pl.BlockSpec(memory_space=pl.ANY)
+    vmem = pl.BlockSpec(memory_space=pltpu.VMEM)
     dma = pltpu.SemaphoreType.DMA
-    bf = jnp.bfloat16
+    bf, f32 = jnp.bfloat16, jnp.float32
     one = jax.ShapeDtypeStruct((4, ROWS, WIDE), bf)
+    rows = jax.ShapeDtypeStruct((ROWS, 768), f32)
     return pl.pallas_call(
         collect_kernel,
-        out_shape=(one, one),
-        in_specs=[hbm, hbm], out_specs=(hbm, hbm),
+        out_shape=(one, one, rows, rows, jax.ShapeDtypeStruct((768, 3072), bf), jax.ShapeDtypeStruct((3072, 768), bf), jax.ShapeDtypeStruct((8, 3072), f32)),
+        in_specs=[hbm, hbm, vmem, vmem, hbm, vmem, hbm], out_specs=(hbm, hbm, vmem, vmem, hbm, hbm, vmem),
         scratch_shapes=[pltpu.VMEM((4, 4, ROWS, WIDE), bf), pltpu.VMEM((4, 4, ROWS, WIDE), bf), pltpu.VMEM((2, 2, ROWS, WIDE), bf),
             pltpu.VMEM((2, 4, ROWS, WIDE), bf), pltpu.VMEM((2, 4, ROWS, WIDE), bf), pltpu.VMEM((4, ROWS, WIDE), bf),
-            dma((4,)), dma((4,)), dma((4,)), dma((4,)), dma((4,)), dma((2,)), dma((2,)), dma((2,)), dma((2,)), dma((4,)), dma((4,))],
+            dma((4,)), dma((4,)), dma((4,)), dma((4,)), dma((4,)), dma((2,)), dma((2,)), dma((2,)), dma((2,)), dma((4,)), dma((4,)),
+            pltpu.VMEM((768, 3072), bf), pltpu.VMEM((3072, 768), bf), pltpu.VMEM((8, 768, TILE), bf), pltpu.VMEM((3072, 768), bf),
+            dma((8,)), dma((8,)), dma((2,))],
+        compiler_params=pltpu.CompilerParams(collective_id=collective_id, has_side_effects=True, vmem_limit_bytes=60 * 2**20),
+        name="collect",
+    )(odq, dkv, normed, grad, up, up_bias, down)
+
+
+def front_kernel(tokens, grad, tables, qkv, dense, vectors, kv_all, qdo, normed_one, normed_two, all_vectors, weights_out,
+                 weights, vec_in, kvs, qds, local_sem, send_sem, recv_sem, kv_send, kv_recv, q_send, q_recv):
+    z, yl, x, yh, core = place()
+    f32, bf = jnp.float32, jnp.bfloat16
+    me = yh * 2 + core
+    far = (1 - yh) * 2 + core
+    other = (1 - yh) * 2 + 1 - core
+    swap = yl != core
+    partner = [device(z, core, lax.rem(x + d, 4), yh, yl) for d in range(4)]
+    sib = device(z, yl, x, yh, 1 - core)
+    cross = device(z, 1 - yl, x, 1 - yh, core)
+    others = [device(z, yl, x, 1 - yh, core), device(z, yl, x, 1 - yh, 1 - core)]
+    xs = [device(z, yl, lax.rem(x + d, 4), yh, core) for d in (1, 3)]
+    zs = [device(lax.rem(z + d, 4), yl, x, yh, core) for d in (1, 3)]
+    greet([sib, cross] + others + xs + zs + partner[1:], partner[0], lax.rem(yl + core, 2))
+    count = [0]
+    sent = []
+
+    def remote(src, dst, to):
+        sem = count[0]
+        count[0] += 1
+        copy = pltpu.make_async_remote_copy(src_ref=src, dst_ref=dst, send_sem=send_sem.at[sem], recv_sem=recv_sem.at[sem], device_id=to, device_id_type=MESH)
+        copy.start()
+        sent.append(copy)
+        return sem
+
+    def arrive(ref, sem):
+        landed(ref, recv_sem.at[sem])
+
+    def rows(i, start, size):
+        return weights.at[i, pl.ds(pl.multiple_of(start, 16), size)]
+
+    shards = [qkv.at[:, pl.ds(768, 768)], qkv.at[:, pl.ds(1536, 768)], qkv.at[:, pl.ds(0, 768)], dense]
+    quarter = [x, z, x, z]
+    ring = [xs, zs, xs, zs]
+    vec_sem = [remote(vectors, vec_in.at[i], to) for i, to in enumerate([sib] + others)]
+    cross_sem = [remote(shards[i].at[pl.ds(pl.multiple_of(quarter[i] * 48, 16), 48)], rows(i, me * 192 + quarter[i] * 48, 48), cross) for i in range(4)]
+    own, late = [], [[], [], [], []]
+    for i in range(4):
+        copy = pltpu.make_async_copy(shards[i], rows(i, me * 192, 192), local_sem.at[i])
+        copy.start()
+        own.append(copy)
+        late[i].append((rows(i, (yh * 2 + 1 - core) * 192, 192), remote(shards[i], rows(i, me * 192, 192), sib)))
+
+    values = tokens[...].astype(f32)
+    centered = values - jnp.mean(values, -1, keepdims=True)
+    unit = centered * lax.rsqrt(jnp.mean(centered * centered, -1, keepdims=True) + 1e-05)
+    for i in range(3):
+        arrive(vec_in.at[i], vec_sem[i])
+    vec = vectors[...].astype(f32) + vec_in[0].astype(f32) + vec_in[1].astype(f32) + vec_in[2].astype(f32)
+    all_vectors[...] = vec
+    normed_one[...] = (unit * vec[0:1] + vec[1:2]).astype(bf)
+    normed_two[...] = (unit * vec[2:3] + vec[3:4]).astype(bf)
+
+    cuts = ((0, 32), (32, 16))
+    ring_sem, half_sem = {}, {}
+
+    def start_ring(i):
+        mine = rows(i, far * 192 + quarter[i] * 48, 48)
+        arrive(mine, cross_sem[i])
+        for way in (0, 1):
+            ring_sem[i, way] = remote(mine, mine, ring[i][way])
+        late[i].append((rows(i, other * 192 + quarter[i] * 48, 48), remote(mine, mine, sib)))
+
+    def relay(i):
+        for way in (0, 1):
+            b = lax.rem(quarter[i] + 3 - 2 * way, 4)
+            got = rows(i, far * 192 + b * 48, 48)
+            arrive(got, ring_sem[i, way])
+            part = rows(i, far * 192 + b * 48 + cuts[way][0], cuts[way][1])
+            half_sem[i, way] = remote(part, part, ring[i][way])
+            late[i].append((rows(i, other * 192 + b * 48, 48), remote(got, got, sib)))
+
+    def finish(i):
+        for way in (0, 1):
+            start = lax.rem(quarter[i] + 2, 4) * 48 + cuts[way][0]
+            got = rows(i, far * 192 + start, cuts[way][1])
+            arrive(got, half_sem[i, way])
+            late[i].append((rows(i, other * 192 + start, cuts[way][1]), remote(got, got, sib)))
+
+    def complete(i):
+        for ref, sem in late[i]:
+            arrive(ref, sem)
+        own[i].wait()
+
+    left = lax.broadcasted_iota(jnp.int32, (ROWS, 128), 1) < 64
+    keep, ahead, behind = tables[0], tables[1], tables[2]
+
+    def turn(tile):
+        return tile * keep + pltpu.roll(tile, 120, 1) * ahead + pltpu.roll(tile, 8, 1) * behind
+
+    def pack(into, first, second):
+        for t in range(6):
+            lanes = slice(128 * t, 128 * t + 128)
+            a, b = first(lanes), second(lanes)
+            for head, tile in ((2 * t, jnp.where(left, a, pltpu.roll(b, 64, 1))), (2 * t + 1, jnp.where(left, pltpu.roll(a, 64, 1), b))):
+                into[head // 3, :, 128 * (head % 3):128 * (head % 3) + 128] = tile.astype(bf)
+
+    def dot(a, b):
+        return jnp.dot(a, b, preferred_element_type=f32)
+
+    def exchange(src, dst_of, send, recv):
+        out = []
+        for d in (0, 2, 1, 3):
+            args = (src.at[lax.rem(x + d, 4)], dst_of, send.at[d], recv.at[d], partner[d])
+            copy = pltpu.make_async_remote_copy(src_ref=args[0], dst_ref=args[1], send_sem=args[2], recv_sem=args[3], device_id=args[4], device_id_type=MESH)
+            if d == 0:
+                @pl.when(swap)
+                def _():
+                    copy.start()
+                @pl.when(jnp.logical_not(swap))
+                def _():
+                    pltpu.make_async_copy(args[0], args[1], args[3]).start()
+            else:
+                copy.start()
+            out.append((d, copy))
+        return out
+
+    for i in range(4):
+        start_ring(i)
+    for i in (0, 1):
+        relay(i)
+    for i in (0, 1):
+        finish(i)
+    for i in (0, 1):
+        complete(i)
+    one = normed_one[...]
+    pack(kvs,
+         lambda lanes: turn(dot(one, weights[0, :, lanes]) + vec[6:7, lanes]),
+         lambda lanes: dot(one, weights[1, :, lanes]) + vec[7:8, lanes])
+    mine = z * 8 + yl * 4 + x
+    sent_kv = exchange(kvs, kv_all.at[mine], kv_send, kv_recv)
+    for i in (2, 3):
+        relay(i)
+    for i in (2, 3):
+        finish(i)
+    for i in (2, 3):
+        complete(i)
+    g = grad[...]
+    pack(qds,
+         lambda lanes: turn(dot(one, weights[2, :, lanes]) + vec[5:6, lanes]) * 0.125,
+         lambda lanes: lax.dot_general(g, weights[3, lanes, :], (((1,), (1,)), ((), ())), preferred_element_type=f32))
+    sent_q = exchange(qds, qdo.at[x], q_send, q_recv)
+    keep_out = pltpu.make_async_copy(weights, weights_out, local_sem.at[4])
+    keep_out.start()
+
+    def slot(zz, cc, d):
+        return kv_all.at[lax.rem(zz, 4) * 8 + cc * 4 + lax.rem(x + 4 - d, 4)]
+
+    half = ROWS // 2
+    up_sem, part_sem, sib_sem = {}, {}, {}
+    for d in (0, 1, 3, 2):
+        here = slot(z, core, d)
+        landed(here, kv_recv.at[d])
+        for way in (0, 1):
+            up_sem[way, d] = remote(here, here, zs[way])
+        sib_sem[0, d] = remote(here, here, sib)
+    for d in (0, 1, 3, 2):
+        for way in (0, 1):
+            here = slot(z + 3 - 2 * way, core, d)
+            arrive(here, up_sem[way, d])
+            part = here.at[pl.ds(way * half, half)]
+            part_sem[way, d] = remote(part, part, zs[way])
+            sib_sem[1 + way, d] = remote(here, here, sib)
+    for d in (0, 1, 3, 2):
+        for way in (0, 1):
+            part = slot(z + 2, core, d).at[pl.ds(way * half, half)]
+            arrive(part, part_sem[way, d])
+            sib_sem[3 + way, d] = remote(part, part, sib)
+    for d in range(4):
+        arrive(slot(z, 1 - core, d), sib_sem[0, d])
+        for way in (0, 1):
+            arrive(slot(z + 3 - 2 * way, 1 - core, d), sib_sem[1 + way, d])
+            arrive(slot(z + 2, 1 - core, d).at[pl.ds(way * half, half)], sib_sem[3 + way, d])
+        landed(qdo.at[lax.rem(x + 4 - d, 4)], q_recv.at[d])
+    keep_out.wait()
+    for copy in sent:
+        copy.wait_send()
+    for d, copy in sent_kv + sent_q:
+        if d == 0:
+            @pl.when(swap)
+            def _():
+                copy.wait_send()
+        else:
+            copy.wait_send()
+
+
+def front(tokens, grad, tables, qkv, dense, vectors, collective_id=0):
+    hbm = pl.BlockSpec(memory_space=pl.ANY)
+    vmem = pl.BlockSpec(memory_space=pltpu.VMEM)
+    dma = pltpu.SemaphoreType.DMA
+    bf, f32 = jnp.bfloat16, jnp.float32
+    rows = jax.ShapeDtypeStruct((ROWS, 768), bf)
+    return pl.pallas_call(
+        front_kernel,
+        out_shape=(jax.ShapeDtypeStruct((32, ROWS, WIDE), bf), jax.ShapeDtypeStruct((4, ROWS, WIDE), bf), rows, rows,
+                   jax.ShapeDtypeStruct((16, 768), f32), jax.ShapeDtypeStruct((4, 768, 768), bf)),
+        in_specs=[vmem, vmem, vmem, hbm, hbm, vmem], out_specs=(hbm, hbm, vmem, vmem, vmem, hbm),
+        scratch_shapes=[pltpu.VMEM((4, 768, 768), bf), pltpu.VMEM((3, 16, 768), bf), pltpu.VMEM((4, ROWS, WIDE), bf), pltpu.VMEM((4, ROWS, WIDE), bf),
+                        dma((5,)), dma((100,)), dma((100,)), dma((4,)), dma((4,)), dma((4,)), dma((4,))],
         compiler_params=pltpu.CompilerParams(collective_id=collective_id, has_side_effects=True, vmem_limit_bytes=40 * 2**20),
-        name="collect",
-    )(odq, dkv)
+        name="front",
+    )(tokens, grad, tables, qkv, dense, vectors)
 
 
 PARTS = ((192, 768, True), (192, 768, False), (192, 384, True), (192, 384, False), (64, 128, True))
@@ -537,7 +713,7 @@
         out_shape=tuple(jax.ShapeDtypeStruct((4, rows, columns), bf) for rows, columns, _ in PARTS),
         in_specs=[hbm] * 4, out_specs=(vmem,) * 5,
         scratch_shapes=scratch + [dma((20,)), dma((140,)), dma((140,))],
-        compiler_params=pltpu.CompilerParams(collective_id=collective_id, has_side_effects=True, vmem_limit_bytes=50 * 2**20),
+        compiler_params=pltpu.CompilerParams(collective_id=collective_id, has_side_effects=True, vmem_limit_bytes=60 * 2**20),
         name="reduce",
     )(wide, upper, lower, tiny)
 
@@ -576,26 +752,19 @@
 
 
 def rotary_tables(positions):
-    half_dims = ROT // 2
-    exponents = jnp.arange(half_dims).astype(jnp.float32) * 2.0 / ROT
+    lanes = jnp.arange(128) % HD
+    exponents = (lanes % 8).astype(jnp.float32) * 2.0 / ROT
     inverse = 10000.0 ** (-exponents)
     angles = positions.astype(jnp.float32)[:, None] * inverse[None, :]
     cosine, sine = jnp.cos(angles), jnp.sin(angles)
-    rest = jnp.ones((positions.shape[0], HD - ROT), jnp.float32)
-    none = jnp.zeros((positions.shape[0], half_dims), jnp.float32)
-    keep = jnp.concatenate([cosine, cosine, rest], 1)
-    ahead = jnp.concatenate([-sine, none, 0.0 * rest], 1)
-    behind = jnp.concatenate([none, sine, 0.0 * rest], 1)
-    return tuple(jnp.tile(table, (1, HEADS)) for table in (keep, ahead, behind))
-
-
-def rotate(rows, tables):
-    keep, ahead, behind = tables
-    return rows * keep + jnp.roll(rows, -8, 1) * ahead + jnp.roll(rows, 8, 1) * behind
+    keep = jnp.where(lanes < ROT, cosine, 1.0)
+    ahead = jnp.where(lanes < 8, -sine, 0.0)
+    behind = jnp.where((lanes >= 8) & (lanes < ROT), sine, 0.0)
+    return jnp.stack([keep, ahead, behind])
 
 
 def rotate_back(rows, tables):
-    keep, ahead, behind = tables
+    keep, ahead, behind = (jnp.tile(table, (1, 6)) for table in tables)
     return rows * keep + jnp.roll(rows * ahead, 8, 1) + jnp.roll(rows * behind, -8, 1)
 
 
@@ -606,15 +775,6 @@
         (((left_dim,), (right_dim,)), ((), ())),
         preferred_element_type=jnp.float32,
     )
-
-
-def gelu_exact(values):
-    return jax.nn.gelu(values, approximate=False)
-
-
-def slabs(first, second):
-    both = jnp.stack([first.reshape(TOK_DEV, HEADS, HD), second.reshape(TOK_DEV, HEADS, HD)], 2)
-    return both.reshape(TOK_DEV, 4, WIDE).transpose(1, 0, 2)
 
 
 def unslab(pairs):
@@ -643,52 +803,36 @@
     tables = rotary_tables(local_pos)
     query_scale = HD ** (-0.5)
 
+    shard = lax.broadcasted_iota(jnp.int32, (4, 1), 0) == lax.axis_index("wsh")
     small = (first_gain, first_shift, second_gain, second_shift, out_bias, qkv_bias, up_bias)
-    sizes = [v.shape[0] for v in small]
-    gathered = lax.all_gather(jnp.concatenate(small), "wsh", axis=0)
-    vectors, start = [], 0
-    for size in sizes:
-        vectors.append(gathered[:, start : start + size].reshape(-1).astype(f32))
-        start += size
-    gain_one, shift_one, gain_two, shift_two, out_offset, qkv_offset, up_offset = vectors
-    qkv_matrix = lax.all_gather(qkv_weight, "wsh", axis=0, tiled=True)
-    dense_matrix = lax.all_gather(dense_weight, "wsh", axis=0, tiled=True)
-    up_matrix = lax.all_gather(up_weight, "wsh", axis=0, tiled=True)
-    down_matrix = lax.all_gather(down_weight, "wsh", axis=0, tiled=True)
-
+    spots = [jnp.where(shard, v[None, :], 0.0).astype(bf).reshape(-1) for v in small]
+    vectors = jnp.concatenate(spots + [jnp.zeros((4 * D,), bf)]).reshape(16, D)
     inputs = tokens[0].astype(f32)
     grad_rows = cotangent[0]
     grad_float = grad_rows.astype(f32)
-    normed_one = layer_norm(inputs, gain_one, shift_one).astype(bf)
-    mixed = jnp.dot(normed_one, qkv_matrix, preferred_element_type=f32) + qkv_offset
-    queries = (rotate(mixed[:, :D], tables) * query_scale).astype(bf)
-    key_rows = rotate(mixed[:, D : 2 * D], tables).astype(bf)
-    value_rows = mixed[:, 2 * D :].astype(bf)
-    grad_attended = contract(grad_rows, dense_matrix, 1, 1).astype(bf)
-
-    keys_values, queries_grads = spread(slabs(key_rows, value_rows), slabs(queries, grad_attended))
+    keys_values, queries_grads, normed_one, normed_two, vectors, matrices = front(
+        tokens[0], grad_rows, tables, qkv_weight, dense_weight, vectors
+    )
+    gain_one, shift_one, gain_two, shift_two, out_offset = (vectors[i] for i in range(5))
+    up_offset = vectors[8:12].reshape(-1)
+    dense_matrix = matrices[3]
+    up_shard, down_shard, keys_values = lax.optimization_barrier((up_weight, down_weight, keys_values))
+    up_matrix = lax.all_gather(up_shard, "wsh", axis=0, tiled=True)
+    down_matrix = lax.all_gather(down_shard, "wsh", axis=0, tiled=True)
     attended_dq, grad_kv = attention(row_blocks, layout_of_seq, queries_grads.reshape(1024, WIDE), keys_values.reshape(8192, WIDE))
-    attended_dq, grad_kv = collect(attended_dq.reshape(4, ROWS, WIDE), grad_kv.reshape(32, ROWS, WIDE))
+    attended_dq, grad_kv, mlp_out, grad_normed_two, up_grad, down_grad, up_offset_grad = collect(
+        attended_dq.reshape(4, ROWS, WIDE), grad_kv.reshape(32, ROWS, WIDE), normed_two, grad_rows,
+        up_matrix, jnp.broadcast_to(up_offset, (8, 3072)), down_matrix,
+    )
+    up_offset_grad = up_offset_grad[0]
     attended_low, grad_queries = unslab(attended_dq)
     grad_keys, grad_values = unslab(grad_kv)
 
     attention_out = jnp.dot(attended_low, dense_matrix, preferred_element_type=f32)
-    normed_two = layer_norm(inputs, gain_two, shift_two).astype(bf)
-    upper_rows = jnp.dot(normed_two, up_matrix, preferred_element_type=f32) + up_offset
-    activated = gelu_exact(upper_rows).astype(bf)
-    mlp_out = jnp.dot(activated, down_matrix, preferred_element_type=f32)
     layer_output = (inputs + attention_out + mlp_out + out_offset).astype(bf)[None]
 
     out_offset_grad = jnp.sum(grad_float, 0)
     dense_grad = contract(attended_low, grad_rows, 0, 0)
-    down_grad = contract(activated, grad_rows, 0, 0)
-    grad_activated = contract(grad_rows, down_matrix, 1, 1)
-    gelu_back = jax.vjp(gelu_exact, upper_rows)[1]
-    grad_upper = gelu_back(grad_activated)[0].astype(bf)
-    up_grad = contract(normed_two, grad_upper, 0, 0)
-    up_offset_grad = jnp.sum(grad_upper.astype(f32), 0)
-    grad_normed_two = contract(grad_upper, up_matrix, 1, 1)
-
     grad_mixed = jnp.concatenate(
         [
             rotate_back(grad_queries.astype(f32) * query_scale, tables).astype(bf),
@@ -699,7 +843,11 @@
     )
     qkv_grad = contract(normed_one, grad_mixed, 0, 0)
     qkv_offset_grad = jnp.sum(grad_mixed.astype(f32), 0)
-    grad_normed_one = contract(grad_mixed, qkv_matrix, 1, 1)
+    grad_normed_one = (
+        contract(grad_mixed[:, :D], matrices[2], 1, 1)
+        + contract(grad_mixed[:, D : 2 * D], matrices[0], 1, 1)
+        + contract(grad_mixed[:, 2 * D :], matrices[1], 1, 1)
+    )
     grad_in_one, gain_one_grad, shift_one_grad = jax.vjp(layer_norm, inputs, gain_one, shift_one)[1](grad_normed_one)
     grad_in_two, gain_two_grad, shift_two_grad = jax.vjp(layer_norm, inputs, gain_two, shift_two)[1](grad_normed_two)
     input_grad = (grad_float + grad_in_one + grad_in_two).astype(bf)[None]

time: 444 us -> 362 us (0.82); the launches traced: 438 us -> 361 us
  waiting for transfers between devices: 41.4 us -> 0.75 us
  matrix products: 41.5 us -> 11.2 us
  other arithmetic: 13.1 us -> 21.5 us
  local copies, waits for them, and re-layouts: 32.3 us -> 25.1 us
  blocking collectives: 6.7 us -> 0 us
    all_gather x4 -> x2, waiting for transfers between devices: 38.9 us -> 0.04 us  [the longest x1 0.02 us: on_device(): up_matrix = lax.all_gather(up_shard, 'wsh', axis=0, tiled=True)]
    pallas_call x2, Pallas kernels: 90 us -> 121 us  [the longest x1 69.5 us: front(): pl.pallas_call(front_kernel, out_shape=(jax.ShapeDtypeStruct((32, ROWS, W...]
    pallas_call x1, Pallas kernels: 111 us -> 83.2 us  [attention(): pl.pallas_call(functools.partial(attn_kernel, chunk), out_shape=(jax.Shap...]
    dot_general x3 -> x0, matrix products: 18.6 us -> none  [the longest x1 11.5 us: on_device(): jnp.dot(normed_two, up_matrix, preferred_element_type=f32) + up_offset]
    dot_general x8 -> x5, matrix products: 21.7 us -> 8.61 us  [contract(): lax.dot_general(left_side, right_side, (((left_dim,), (right_dim,)), ((),...]
    all_gather x1 -> x0, blocking collectives: 6.7 us -> none  [on_device(): gathered = lax.all_gather(jnp.concatenate(small), 'wsh', axis=0)]
    convert_element_type x10 -> x0, local copies, waits for them, and re-layouts: 5.17 us -> none  [the longest x7 2.86 us: on_device(): vectors.append(gathered[:, start:start + size].reshape(-1).astype(f32))]
    unnamed x72 -> x55, local copies, waits for them, and re-layouts: 5.89 us -> 10 us
  transfers between devices with their start and end apart: 4 -> 2, of which waited for: 2 -> 0; matrix products, arithmetic and copies ran while one was open for 10% -> 1% of each run, Pallas kernels for 46% -> 23%
where the time goes in v2:
time: 362 us; the launch traced here: 361 us
  Pallas kernels  288 us (80%)
  local copies, waits for them, and re-layouts  25.1 us (7%)
  other arithmetic  21.5 us (6%)
  between operations  14.6 us (4%)
  matrix products  11.2 us (3%)
    pallas_call x1, Pallas kernels, reduce_all(): pl.pallas_call(reduce_kernel, out_shape=tuple((jax.ShapeDtypeStruct((4, r...  83.4 us
    pallas_call x1, Pallas kernels, attention(): pl.pallas_call(functools.partial(attn_kernel, chunk), out_shape=(jax.Shap...  83.2 us
    pallas_call x1, Pallas kernels, front(): pl.pallas_call(front_kernel, out_shape=(jax.ShapeDtypeStruct((32, ROWS, W...  69.5 us
    pallas_call x1, Pallas kernels, collect(): pl.pallas_call(collect_kernel, out_shape=(one, one, rows, rows, jax.Shape...  51.8 us
    unnamed x55, local copies, waits for them, and re-layouts  10 us
    dot_general x5, matrix products, contract(): lax.dot_general(left_side, right_side, (((left_dim,), (right_dim,)), ((),...  8.61 us
  transfers between devices with their start and end apart: 2, of which 0 were waited for; matrix products, arithmetic and copies ran while one was open for 1% of the time, Pallas kernels for 23%

profile of v2, /device:TPU:0, one launch (start us, length us, event | category | flops | bytes accessed | tf_op | source)
XLA Modules:
  0.0 361.2 jit_solution(519648648338969339)
XLA Ops:
  7.3 0.7 subtract_bitcast_fusion
  7.9 0.7 pad_add_fusion
  8.7 0.1 reshape.682
  9.0 0.8 broadcast_select_fusion.2
  10.2 0.8 broadcast_select_fusion.1
  11.0 0.8 broadcast_select_fusion
  11.8 0.2 dynamic-update-slice
  12.0 0.2 dynamic-update-slice.1
  12.3 0.2 dynamic-update-slice.2
  12.5 0.2 dynamic-update-slice.3
  12.7 0.2 dynamic-update-slice.4
  12.9 0.3 dynamic-update-slice.5
  13.2 0.6 fusion.40
  13.8 1.0 copy-done
  14.8 1.0 copy-done.3
  15.8 1.2 copy-done.6
  16.9 1.0 copy-done.9
  17.9 69.5 %front.1 = (bf16[32,256,384]{2,1,0:T(8,128)(2,1)}, bf16[4,256,384]{2,1,0:T(8,128)(2,1)S(1)}, bf16[256,768]{1,0:T(8,128)(2,1)S(1)}, bf16[256,768]{1,0:T(8,128)(2,...) custom-call(bf16[256,768]{1,0:T(8,128)(2,1)S(1)} %bitcast.113, bf16[256,768]{1,0:T(8,128)(2,1)S(1)} %bitcast.112, ...), custom_call_target="tpu_custom_call" | custom-call | tf_op jit(solution)/shard_map/front/pallas_call | solution.py:522
  87.5 2.1 copy-done.5
  89.6 0.9 copy-done.7
  90.4 0.7 copy-done.8
  91.3 0.7 all-gather.5.cloned.1.call-update
  92.1 0.6 dynamic_slice.6.qpos
  92.9 1.3 scatter_custom_fusion.lay
  94.2 83.2 %attention.1 = (bf16[1024,384]{1,0:T(8,128)(2,1)}, bf16[8192,384]{1,0:T(8,128)(2,1)}) custom-call(s32[8]{0:T(128)} %dynamic_slice.6.qpos, s32[64]{0:T(128)} %scatter_custom_fusion.lay, bf16[1024,384]{1,0:T(8,128)(2,1)} %bitcast.114, bf16[8192,384]{1,0:T(8,128)(2,1)} %bitcast.121), custom_call_target="tpu_custom_call" | custom-call | tf_op jit(solution)/shard_map/attention/pallas_call | solution.py:119
  177.4 0.1 convert_reduce_fusion
  177.6 0.6 fusion.41
  178.2 0.6 broadcast_in_dim.183.up_bias
  178.9 51.8 %collect.1 = (bf16[4,256,384]{2,1,0:T(8,128)(2,1)}, bf16[4,256,384]{2,1,0:T(8,128)(2,1)}, f32[256,768]{1,0:T(8,128)}, f32[256,768]{1,0:T(8,128)}, bf16[768,3072]...) custom-call(bf16[4,256,384]{2,1,0:T(8,128)(2,1)} %bitcast.138, bf16[32,256,384]{2,1,0:T(8,128)(2,1)} %bitcast.120, ...), custom_call_target="tpu_custom_call" | custom-call | tf_op jit(solution)/shard_map/collect/pallas_call | solution.py:315
  230.7 1.4 copy.32
  232.2 0.8 copy-done.10
  233.0 1.4 copy.33
  234.4 0.2 bitcast_multiply_fusion.5
  235.0 1.0 fusion.58
  236.0 1.1 slice_convert_fusion
  237.1 1.9 fusion.28
  239.0 0.4 fusion.32
  239.5 1.9 add_convert_fusion.2
  241.4 1.8 fusion.12
  243.3 0.2 add_convert_fusion.1
  243.5 1.9 convolution_add_fusion.1
  245.4 2.1 fusion.56
  247.6 0.7 fusion.22
  248.6 0.9 fusion.42
  249.6 0.1 concatenate.50
  249.7 0.1 convert_element_type.155
  249.8 0.8 reshape.698.tiny
  250.6 2.3 convolution_convert_fusion
  253.0 0.5 convolution_convert_fusion.1
  253.5 2.8 pad_maximum_fusion.wide
  256.2 83.4 %reduce.13 = (bf16[4,192,768]{2,1,0:T(8,128)(2,1)}, bf16[4,192,768]{2,1,0:T(8,128)(2,1)}, bf16[4,192,384]{2,1,0:T(8,128)(2,1)}, bf16[4,192,384]{2,1,0:T(8,128)(2,1)}, bf16[4,64,128]{2,1,0:T(8,128)(2,1)}) custom-call(bf16[768,3072]{1,0:T(8,128)(2,1)} %pad_maximum_fusion.wide, bf16[768,3072]{1,0:T(8,128)(2,1)} %get-tuple-element.51.upper, ...), custom_call_target="tpu_custom_call" | custom-call | tf_op jit(solution)/shard_map/reduce/pallas_call | solution.py:711
  339.6 1.5 convert_bitcast_fusion.1
  341.1 0.3 copy.38
  341.4 1.3 slice.146
  342.7 0.9 slice.148
  343.7 0.6 fusion.59
  344.4 0.7 slice.147
  345.0 0.6 slice.151
  345.6 1.3 pad_maximum_fusion.2
  347.0 1.7 bitcast_convert_fusion
  348.6 0.2 convert_bitcast_fusion
  348.8 1.7 copy.39
  350.5 1.3 fusion.33
  351.8 2.6 fusion.3
  (96 shorter events, 2.3 us)
Async XLA Ops:
  7.2 171.0 %all-gather.3.cloned.1.call-start = ((), (), s32[]{:S(2)}) async-start(), calls=%async_computation | async-start | bytes 5898240 | tf_op jit(solution)/shard_map/all_gather | solution.py:820
  13.8 1.0 copy-start
  14.8 1.0 copy-start.3
  15.8 1.2 copy-start.6
  16.9 1.0 copy-start.9
  17.9 74.8 %copy-start.1 = (bf16[1,256,768]{2,1,0:T(8,128)(2,1)S(1)}, bf16[1,256,768]{2,1,0:T(8,128)(2,1)}, u32[]{:S(2)}) copy-start(bf16[1,256,768]{2,1,0:T(8,128)(2,1)} %param.15) | copy-start | bytes 1179652
  87.5 2.1 copy-start.5
  89.6 0.9 copy-start.7
  90.4 0.7 copy-start.8
  91.2 87.0 %all-gather.5.cloned.1.call-start = ((), (), s32[]{:S(2)}) async-start(), calls=%async_computation.1 | async-start | bytes 5898240 | tf_op jit(solution)/shard_map/all_gather | solution.py:821
  94.2 83.3 %copy-start.4 = (bf16[1,256,768]{2,1,0:T(8,128)(2,1)S(1)}, bf16[1,256,768]{2,1,0:T(8,128)(2,1)}, u32[]{:S(2)}) copy-start(bf16[1,256,768]{2,1,0:T(8,128)(2,1)} %param.14) | copy-start | bytes 1179652
  232.1 0.9 copy-start.10
  234.8 1.1 copy-start.11
  235.9 3.1 copy-start.17
  239.0 4.2 %copy-start.16 = (bf16[256,768]{0,1:T(8,128)(2,1)}, bf16[256,768]{0,1:T(8,128)(2,1)S(1)}, u32[]{:S(2)}) copy-start(bf16[256,768]{0,1:T(8,128)(2,1)S(1)} %get-tuple-element.96) | copy-start | bytes 1179652
  239.5 3.8 %copy-start.12 = (f32[256,768]{0,1:T(8,128)S(1)}, f32[256,768]{0,1:T(8,128)}, u32[]{:S(2)}) copy-start(f32[256,768]{0,1:T(8,128)} %get-tuple-element.94) | copy-start | bytes 2359300
  239.5 3.8 %copy-start.13 = (f32[256,768]{0,1:T(8,128)S(1)}, f32[256,768]{0,1:T(8,128)}, u32[]{:S(2)}) copy-start(f32[256,768]{0,1:T(8,128)} %get-tuple-element.95) | copy-start | bytes 2359300
  239.5 3.8 %copy-start.15 = (f32[256,12,1,64]{0,3,2,1:T(8,128)S(1)}, f32[256,12,1,64]{0,3,2,1:T(8,128)}, u32[]{:S(2)}) copy-start(f32[256,12,1,64]{0,3,2,1:T(8,128)} %get-tuple-element.82) | copy-start | bytes 2359300
  243.3 2.1 copy-start.14
  243.3 2.1 copy-start.18
  250.6 2.3 copy-start.2
  250.6 2.3 copy-start.19
  341.4 2.2 copy-start.22
  347.0 1.7 copy-start.21
  350.5 1.3 copy-start.20
  350.5 1.3 copy-start.23
Sparse Core Ops, SparseCore 0:
  91.3 38.9 all-gather.2
  132.0 40.9 all-gather.4

commit v3 on v2

v3 whole, which is shorter than its diff:
```python
import functools

import jax
import jax.numpy as jnp
from jax import lax
from jax.experimental import pallas as pl
from jax.experimental.pallas import tpu as pltpu
from jax.sharding import PartitionSpec as P

G = 3; BLK = 128; LOG2E = 1.4426950408889634
NEG = -1e30

def attn_kernel(chunk, qpos, lay, qdo, kv_hbm, odq, dkv_hbm, kv, kvt, acc, probs, grads, tops, stage, sem, osem):
    blocks = chunk // BLK
    nblk = kv.shape[0] // BLK
    f32, bf = jnp.float32, jnp.bfloat16

    def load(i, _):
        pltpu.make_async_copy(kv_hbm.at[pl.ds(pl.multiple_of(lay[i] * BLK, BLK), BLK)], kv.at[pl.ds(pl.multiple_of(i * BLK, BLK), BLK)], sem.at[i]).start()
        return 0
    lax.fori_loop(0, nblk, load, 0)

    def land(i, _):
        rows = pl.ds(pl.multiple_of(i * BLK, BLK), BLK)
        pltpu.make_async_copy(kv_hbm.at[pl.ds(0, BLK)], kv.at[rows], sem.at[i]).wait()
        acc[rows] = jnp.zeros((BLK, G * 128), f32)
        kvt[:, rows] = kv[rows].T
        return 0
    lax.fori_loop(0, nblk, land, 0)

    upper = lax.broadcasted_iota(jnp.int32, (128, 128), 0) < 64
    left = lax.broadcasted_iota(jnp.int32, (128, 128), 1) < 64

    def q_block(i, _):
        b = qpos[i]
        qrows = pl.ds(pl.multiple_of(i * BLK, BLK), BLK)
        last = b // blocks
        pairs = [qdo[qrows, h * 128:(h + 1) * 128] for h in range(G)]
        turned = [p.astype(f32).T for p in pairs]
        wide = [jnp.concatenate([jnp.where(upper, turned[h], 0.0).astype(bf), jnp.where(upper, 0.0, turned[h]).astype(bf)], 1) for h in range(G)]
        key_i = lax.broadcasted_iota(jnp.int32, (chunk, BLK), 0)
        row_i = lax.broadcasted_iota(jnp.int32, (chunk, BLK), 1) + (b - last * blocks) * BLK

        def fwd(c, state, masked):
            at = pl.ds(pl.multiple_of(c * chunk, chunk), chunk)
            out = []
            every = [jnp.dot(kv[at, h * 128:(h + 1) * 128], wide[h], preferred_element_type=f32) for h in range(G)]
            kept = []
            for h in range(G):
                m, l, o = state[h]
                s = every[h][:, :128]
                grads[at, h * 128:(h + 1) * 128] = every[h][:, 128:]
                if masked:
                    s = jnp.where(key_i <= row_i, s, NEG)
                new = jnp.maximum(m, jnp.max(s, 0, keepdims=True))
                p = jnp.exp(s - new)
                a = jnp.exp(m - new)
                l = l * a + jnp.sum(p, 0, keepdims=True)
                p = p.astype(bf)
                probs[at, h * 128:(h + 1) * 128] = p
                tops[c, h] = jnp.broadcast_to(new, (8, BLK))
                kept.append((new, l, o * a, p))
            for h in range(G):
                new, l, o, p = kept[h]
                o = o + jnp.dot(kvt[h * 128 + 64:(h + 1) * 128, at], p, preferred_element_type=f32)
                out.append((new, l, o))
            return tuple(out)

        state = tuple((jnp.full((1, BLK), NEG, f32), jnp.zeros((1, BLK), f32), jnp.zeros((64, BLK), f32)) for _ in range(G))
        state = lax.fori_loop(0, last, lambda c, s: fwd(c, s, False), state)
        state = fwd(last, state, True)
        lse, delta, outs = [], [], []
        for h in range(G):
            m, l, o = state[h]
            o = o / l
            outs.append(o)
            lse.append(m + jnp.log(l))
            delta.append(jnp.sum(o * turned[h][64:], 0, keepdims=True))
        narrow = [jnp.concatenate([jnp.where(left, pairs[h], jnp.zeros_like(pairs[h])), jnp.where(left, jnp.zeros_like(pairs[h]), pairs[h])], 0) for h in range(G)]

        def bwd(c, state):
            at = pl.ds(pl.multiple_of(c * chunk, chunk), chunk)
            out, work = [], []
            for h in range(G):
                cols = slice(h * 128, (h + 1) * 128)
                p = probs[at, cols].astype(f32) * jnp.exp(tops[c, h, 0:1] - lse[h])
                ds = (p * (grads[at, cols] - delta[h])).astype(bf)
                work.append((jnp.concatenate([ds, p.astype(bf)], 1), ds))
            for h in range(G):
                pair, ds = work[h]
                acc[at, h * 128:(h + 1) * 128] += jnp.dot(pair, narrow[h], preferred_element_type=f32)
                out.append(state[h] + jnp.dot(kvt[h * 128:h * 128 + 64, at], ds, preferred_element_type=f32))
            return tuple(out)

        dq = tuple(jnp.zeros((64, BLK), f32) for _ in range(G))
        dq = lax.fori_loop(0, last + 1, bwd, dq)
        for h in range(G):
            odq[qrows, h * 128:(h + 1) * 128] = jnp.concatenate([outs[h], dq[h]], 0).T.astype(bf)
        return 0
    lax.fori_loop(0, qpos.shape[0], q_block, 0)

    def send(i, _):
        slot = lax.rem(i, 8)
        @pl.when(i >= 8)
        def _():
            pltpu.make_async_copy(stage.at[slot], dkv_hbm.at[pl.ds(0, BLK)], osem.at[slot]).wait()
        stage[slot] = acc[pl.ds(pl.multiple_of(i * BLK, BLK), BLK)].astype(bf)
        pltpu.make_async_copy(stage.at[slot], dkv_hbm.at[pl.ds(pl.multiple_of(lay[i] * BLK, BLK), BLK)], osem.at[slot]).start()
        return 0
    lax.fori_loop(0, nblk, send, 0)
    for slot in range(8):
        pltpu.make_async_copy(stage.at[slot], dkv_hbm.at[pl.ds(0, BLK)], osem.at[slot]).wait()

def attention(qpos, lay, qdo, kv, chunk=1024):
    n = kv.shape[0]
    smem = pl.BlockSpec(memory_space=pltpu.SMEM)
    vmem = pl.BlockSpec(memory_space=pltpu.VMEM)
    hbm = pl.BlockSpec(memory_space=pl.ANY)
    return pl.pallas_call(
        functools.partial(attn_kernel, chunk),
        out_shape=(jax.ShapeDtypeStruct(qdo.shape, jnp.bfloat16), jax.ShapeDtypeStruct(kv.shape, jnp.bfloat16)),
        in_specs=[smem, smem, vmem, hbm], out_specs=(vmem, hbm),
        scratch_shapes=[pltpu.VMEM((n, G * 128), jnp.bfloat16), pltpu.VMEM((G * 128, n), jnp.bfloat16),
            pltpu.VMEM((n, G * 128), jnp.float32), pltpu.VMEM((n, G * 128), jnp.bfloat16), pltpu.VMEM((n, G * 128), jnp.float32), pltpu.VMEM((n // chunk, G, 8, BLK), jnp.float32),
            pltpu.VMEM((8, BLK, G * 128), jnp.bfloat16),
            pltpu.SemaphoreType.DMA((n // BLK,)), pltpu.SemaphoreType.DMA((8,))],
        compiler_params=pltpu.CompilerParams(vmem_limit_bytes=62 * 2**20),
        name="attention",
    )(qpos, lay, qdo, kv)


MESH = pl.DeviceIdType.MESH
ROWS, WIDE = 256, 384


def place():
    c, w = lax.axis_index("ctx"), lax.axis_index("wsh")
    return c // 8, lax.rem(c // 4, 2), lax.rem(c, 4), w // 2, lax.rem(w, 2)


def device(z, yl, x, yh, core):
    return (z * 8 + yl * 4 + x, yh * 2 + core)


def greet(devices, extra=None, extra_count=0):
    barrier = pltpu.get_barrier_semaphore()
    for d in devices:
        pl.semaphore_signal(barrier, inc=1, device_id=d, device_id_type=MESH)
    if extra is not None:
        @pl.when(extra_count == 1)
        def _():
            pl.semaphore_signal(barrier, inc=1, device_id=extra, device_id_type=MESH)
    pl.semaphore_wait(barrier, len(devices) + extra_count)


def landed(ref, sem):
    pltpu.make_async_copy(ref, ref, sem).wait()


def front_kernel(tokens, grad, tables, qkv, dense, vectors, kv_all, qdo, normed_one, normed_two, all_vectors, weights_out,
                 weights, vec_in, kvs, qds, local_sem, send_sem, recv_sem, kv_send, kv_recv, q_send, q_recv):
    z, yl, x, yh, core = place()
    f32, bf = jnp.float32, jnp.bfloat16
    me = yh * 2 + core
    far = (1 - yh) * 2 + core
    other = (1 - yh) * 2 + 1 - core
    swap = yl != core
    partner = [device(z, core, lax.rem(x + d, 4), yh, yl) for d in range(4)]
    sib = device(z, yl, x, yh, 1 - core)
    cross = device(z, 1 - yl, x, 1 - yh, core)
    others = [device(z, yl, x, 1 - yh, core), device(z, yl, x, 1 - yh, 1 - core)]
    xs = [device(z, yl, lax.rem(x + d, 4), yh, core) for d in (1, 3)]
    zs = [device(lax.rem(z + d, 4), yl, x, yh, core) for d in (1, 3)]
    greet([sib, cross] + others + xs + zs + partner[1:], partner[0], lax.rem(yl + core, 2))
    count = [0]
    sent = []

    def remote(src, dst, to):
        sem = count[0]
        count[0] += 1
        copy = pltpu.make_async_remote_copy(src_ref=src, dst_ref=dst, send_sem=send_sem.at[sem], recv_sem=recv_sem.at[sem], device_id=to, device_id_type=MESH)
        copy.start()
        sent.append(copy)
        return sem

    def arrive(ref, sem):
        landed(ref, recv_sem.at[sem])

    def rows(i, start, size):
        return weights.at[i, pl.ds(pl.multiple_of(start, 16), size)]

    shards = [qkv.at[:, pl.ds(768, 768)], qkv.at[:, pl.ds(1536, 768)], qkv.at[:, pl.ds(0, 768)], dense]
    quarter = [x, z, x, z]
    ring = [xs, zs, xs, zs]
    vec_sem = [remote(vectors, vec_in.at[i], to) for i, to in enumerate([sib] + others)]
    cross_sem = [remote(shards[i].at[pl.ds(pl.multiple_of(quarter[i] * 48, 16), 48)], rows(i, me * 192 + quarter[i] * 48, 48), cross) for i in range(4)]
    own, late = [], [[], [], [], []]
    for i in range(4):
        copy = pltpu.make_async_copy(shards[i], rows(i, me * 192, 192), local_sem.at[i])
        copy.start()
        own.append(copy)
        late[i].append((rows(i, (yh * 2 + 1 - core) * 192, 192), remote(shards[i], rows(i, me * 192, 192), sib)))

    values = tokens[...].astype(f32)
    centered = values - jnp.mean(values, -1, keepdims=True)
    unit = centered * lax.rsqrt(jnp.mean(centered * centered, -1, keepdims=True) + 1e-05)
    for i in range(3):
        arrive(vec_in.at[i], vec_sem[i])
    vec = vectors[...].astype(f32) + vec_in[0].astype(f32) + vec_in[1].astype(f32) + vec_in[2].astype(f32)
    all_vectors[...] = vec
    normed_one[...] = (unit * vec[0:1] + vec[1:2]).astype(bf)
    normed_two[...] = (unit * vec[2:3] + vec[3:4]).astype(bf)

    cuts = ((0, 32), (32, 16))
    ring_sem, half_sem = {}, {}

    def start_ring(i):
        mine = rows(i, far * 192 + quarter[i] * 48, 48)
        arrive(mine, cross_sem[i])
        for way in (0, 1):
            ring_sem[i, way] = remote(mine, mine, ring[i][way])
        late[i].append((rows(i, other * 192 + quarter[i] * 48, 48), remote(mine, mine, sib)))

    def relay(i):
        for way in (0, 1):
            b = lax.rem(quarter[i] + 3 - 2 * way, 4)
            got = rows(i, far * 192 + b * 48, 48)
            arrive(got, ring_sem[i, way])
            part = rows(i, far * 192 + b * 48 + cuts[way][0], cuts[way][1])
            half_sem[i, way] = remote(part, part, ring[i][way])
            late[i].append((rows(i, other * 192 + b * 48, 48), remote(got, got, sib)))

    def finish(i):
        for way in (0, 1):
            start = lax.rem(quarter[i] + 2, 4) * 48 + cuts[way][0]
            got = rows(i, far * 192 + start, cuts[way][1])
            arrive(got, half_sem[i, way])
            late[i].append((rows(i, other * 192 + start, cuts[way][1]), remote(got, got, sib)))

    def complete(i):
        for ref, sem in late[i]:
            arrive(ref, sem)
        own[i].wait()

    left = lax.broadcasted_iota(jnp.int32, (ROWS, 128), 1) < 64
    keep, ahead, behind = tables[0], tables[1], tables[2]

    def turn(tile):
        return tile * keep + pltpu.roll(tile, 120, 1) * ahead + pltpu.roll(tile, 8, 1) * behind

    def pack(into, first, second):
        for t in range(6):
            lanes = slice(128 * t, 128 * t + 128)
            a, b = first(lanes), second(lanes)
            for head, tile in ((2 * t, jnp.where(left, a, pltpu.roll(b, 64, 1))), (2 * t + 1, jnp.where(left, pltpu.roll(a, 64, 1), b))):
                into[head // 3, :, 128 * (head % 3):128 * (head % 3) + 128] = tile.astype(bf)

    def dot(a, b):
        return jnp.dot(a, b, preferred_element_type=f32)

    def exchange(src, dst_of, send, recv):
        out = []
        for d in (0, 2, 1, 3):
            args = (src.at[lax.rem(x + d, 4)], dst_of, send.at[d], recv.at[d], partner[d])
            copy = pltpu.make_async_remote_copy(src_ref=args[0], dst_ref=args[1], send_sem=args[2], recv_sem=args[3], device_id=args[4], device_id_type=MESH)
            if d == 0:
                @pl.when(swap)
                def _():
                    copy.start()
                @pl.when(jnp.logical_not(swap))
                def _():
                    pltpu.make_async_copy(args[0], args[1], args[3]).start()
            else:
                copy.start()
            out.append((d, copy))
        return out

    for i in range(4):
        start_ring(i)
    for i in (0, 1):
        relay(i)
    for i in (0, 1):
        finish(i)
    for i in (0, 1):
        complete(i)
    one = normed_one[...]
    pack(kvs,
         lambda lanes: turn(dot(one, weights[0, :, lanes]) + vec[6:7, lanes]),
         lambda lanes: dot(one, weights[1, :, lanes]) + vec[7:8, lanes])
    mine = z * 8 + yl * 4 + x
    sent_kv = exchange(kvs, kv_all.at[mine], kv_send, kv_recv)
    for i in (2, 3):
        relay(i)
    for i in (2, 3):
        finish(i)
    for i in (2, 3):
        complete(i)
    g = grad[...]
    pack(qds,
         lambda lanes: turn(dot(one, weights[2, :, lanes]) + vec[5:6, lanes]) * 0.125,
         lambda lanes: lax.dot_general(g, weights[3, lanes, :], (((1,), (1,)), ((), ())), preferred_element_type=f32))
    sent_q = exchange(qds, qdo.at[x], q_send, q_recv)
    keep_out = pltpu.make_async_copy(weights, weights_out, local_sem.at[4])
    keep_out.start()

    def slot(zz, cc, d):
        return kv_all.at[lax.rem(zz, 4) * 8 + cc * 4 + lax.rem(x + 4 - d, 4)]

    half = ROWS // 2
    up_sem, part_sem, sib_sem = {}, {}, {}
    for d in (0, 1, 3, 2):
        here = slot(z, core, d)
        landed(here, kv_recv.at[d])
        for way in (0, 1):
            up_sem[way, d] = remote(here, here, zs[way])
        sib_sem[0, d] = remote(here, here, sib)
    for d in (0, 1, 3, 2):
        for way in (0, 1):
            here = slot(z + 3 - 2 * way, core, d)
            arrive(here, up_sem[way, d])
            part = here.at[pl.ds(way * half, half)]
            part_sem[way, d] = remote(part, part, zs[way])
            sib_sem[1 + way, d] = remote(here, here, sib)
    for d in (0, 1, 3, 2):
        for way in (0, 1):
            part = slot(z + 2, core, d).at[pl.ds(way * half, half)]
            arrive(part, part_sem[way, d])
            sib_sem[3 + way, d] = remote(part, part, sib)
    for d in range(4):
        arrive(slot(z, 1 - core, d), sib_sem[0, d])
        for way in (0, 1):
            arrive(slot(z + 3 - 2 * way, 1 - core, d), sib_sem[1 + way, d])
            arrive(slot(z + 2, 1 - core, d).at[pl.ds(way * half, half)], sib_sem[3 + way, d])
        landed(qdo.at[lax.rem(x + 4 - d, 4)], q_recv.at[d])
    keep_out.wait()
    for copy in sent:
        copy.wait_send()
    for d, copy in sent_kv + sent_q:
        if d == 0:
            @pl.when(swap)
            def _():
                copy.wait_send()
        else:
            copy.wait_send()


def front(tokens, grad, tables, qkv, dense, vectors, collective_id=0):
    hbm = pl.BlockSpec(memory_space=pl.ANY)
    vmem = pl.BlockSpec(memory_space=pltpu.VMEM)
    dma = pltpu.SemaphoreType.DMA
    bf, f32 = jnp.bfloat16, jnp.float32
    rows = jax.ShapeDtypeStruct((ROWS, 768), bf)
    return pl.pallas_call(
        front_kernel,
        out_shape=(jax.ShapeDtypeStruct((32, ROWS, WIDE), bf), jax.ShapeDtypeStruct((4, ROWS, WIDE), bf), rows, rows,
                   jax.ShapeDtypeStruct((16, 768), f32), jax.ShapeDtypeStruct((4, 768, 768), bf)),
        in_specs=[vmem, vmem, vmem, hbm, hbm, vmem], out_specs=(hbm, hbm, vmem, vmem, vmem, hbm),
        scratch_shapes=[pltpu.VMEM((4, 768, 768), bf), pltpu.VMEM((3, 16, 768), bf), pltpu.VMEM((4, ROWS, WIDE), bf), pltpu.VMEM((4, ROWS, WIDE), bf),
                        dma((5,)), dma((100,)), dma((100,)), dma((4,)), dma((4,)), dma((4,)), dma((4,))],
        compiler_params=pltpu.CompilerParams(collective_id=collective_id, has_side_effects=True, vmem_limit_bytes=40 * 2**20),
        name="front",
    )(tokens, grad, tables, qkv, dense, vectors)


PARTS = ((768, False), (768, True), (384, True), (384, False))
TILE = 384


def erf(values):
    v = jnp.clip(values, -4.0, 4.0)
    s = v * v
    top = jnp.float32(-2.72614225801306e-10)
    for coefficient in (2.77068142495902e-08, -2.10102402082508e-06, -5.69250639462346e-05, -7.34990630326855e-04, -2.95459980854025e-03, -1.60960333262415e-02):
        top = top * s + coefficient
    low = jnp.float32(-1.45660718464996e-05)
    for coefficient in (-2.13374055278905e-04, -1.68282697438203e-03, -7.37332916720468e-03, -1.42647390514189e-02):
        low = low * s + coefficient
    return v * top / low


def back_kernel(odq, dkv, tokens_hbm, grad_hbm, one_hbm, two_hbm, vectors_hbm, tables_hbm, matrices, up_hbm, down_hbm,
                layer_output, input_grad, wide_out, upper_out, lower_out, vector_out, *refs):
    sib_in, far_in, near_in, far_two, near_two, y_in = (refs[4 * i : 4 * i + 4] for i in range(6))
    (tokens, grad, normed_one, normed_two, vectors, tables, up, down_w, upper, lower, mlp, back_two, up_bias, bias_grad,
     held, held_in, held_far, held_near, odq_own, dkv_own, attended, mixed, tiny, tiny_in, send_sem, recv_sem, local_sem) = refs[24:]
    z, yl, x, yh, core = place()
    f32, bf = jnp.float32, jnp.bfloat16
    swapped_place = yl != core
    partner = [device(z, core, lax.rem(x + d, 4), yh, yl) for d in range(4)]
    xs = [device(z, yl, lax.rem(x + d, 4), yh, core) for d in (1, 3, 2)]
    zs = [device(lax.rem(z + d, 4), yl, x, yh, core) for d in (1, 3, 2)]
    ys = [device(z, 1 - yl, x, yh, core), device(z, yl, x, 1 - yh, core), device(z, 1 - yl, x, 1 - yh, core)]
    sib = device(z, yl, x, yh, 1 - core)
    greet([sib] + xs + zs + ys + partner[1:], partner[0], lax.rem(yl + core, 2))
    count = [0]
    local_count = [0]
    sent, maybe = [], []
    pairs = []

    def bring(src, dst):
        copy = pltpu.make_async_copy(src, dst, local_sem.at[local_count[0]])
        local_count[0] += 1
        copy.start()
        return copy

    def number():
        count[0] += 1
        return count[0] - 1

    def describe(src, dst, sem, to):
        return pltpu.make_async_remote_copy(src_ref=src, dst_ref=dst, send_sem=send_sem.at[sem], recv_sem=recv_sem.at[sem], device_id=to, device_id_type=MESH)

    def remote(src, dst, to):
        sem = number()
        copy = describe(src, dst, sem, to)
        copy.start()
        sent.append(copy)
        return sem

    def both(sources, dst, to):
        sem = number()
        for s in (0, 1):
            describe(sources[s], dst.at[s], sem, to).start()
        pairs.append((dst, sem))
        return sem

    def arrive(ref, sem):
        landed(ref, recv_sem.at[sem])

    def exchange(src, dst, d):
        sem = number()
        part = src.at[lax.rem(x + d, 4)]
        copy = describe(part, dst, sem, partner[d])
        if d == 0:
            @pl.when(swapped_place)
            def _():
                copy.start()
            @pl.when(jnp.logical_not(swapped_place))
            def _():
                pltpu.make_async_copy(part, dst, recv_sem.at[sem]).start()
            maybe.append(copy)
        else:
            copy.start()
            sent.append(copy)
        return sem

    def dot(left, right, left_dim, right_dim):
        return lax.dot_general(left, right, (((left_dim,), (right_dim,)), ((), ())), preferred_element_type=f32)

    def group(zz, cc):
        return dkv.at[pl.ds(lax.rem(zz, 4) * 8 + cc * 4, 4)]

    held_sem, held_load = [], []
    for k, zz in enumerate((z + 2, z + 1, z + 3, z)):
        held_sem.append(remote(group(zz, 1 - core), held_in.at[k], sib))
        held_load.append(bring(group(zz, core), held.at[k]))
    inputs = [bring(src, dst) for src, dst in ((two_hbm, normed_two), (grad_hbm, grad), (vectors_hbm, vectors), (up_hbm, up), (down_hbm, down_w),
                                               (tokens_hbm, tokens), (one_hbm, normed_one), (tables_hbm, tables))]
    odq_sem = [exchange(odq, odq_own.at[x], d) for d in range(4)]
    mlp[...] = jnp.zeros_like(mlp)
    back_two[...] = jnp.zeros_like(back_two)
    for copy in inputs:
        copy.wait()
    for i in range(4):
        up_bias[0:1, 768 * i:768 * i + 768] = vectors[8 + i:9 + i]

    def feed(t, _):
        at = pl.ds(pl.multiple_of(t * TILE, TILE), TILE)
        values = dot(normed_two[...], up[:, at], 1, 0) + up_bias[0:1, at]
        inner = 0.5 + 0.5 * erf(values * 0.7071067811865476)
        slope = inner + values * (0.3989422804014327 * jnp.exp(-0.5 * values * values))
        active = (values * inner).astype(bf)
        grads = (dot(grad[...], down_w[at], 1, 1) * slope).astype(bf)
        mlp[...] += dot(active, down_w[at], 1, 0)
        back_two[...] += dot(grads, up[:, at], 1, 1)
        bias_grad[0:1, at] = jnp.sum(grads.astype(f32), 0, keepdims=True)
        upper[:, at] = dot(normed_two[...], grads, 0, 0).astype(bf)
        lower[at] = dot(active, grad[...], 0, 0).astype(bf)
        return 0

    def sum_held(k, chunks, terms):
        def step(i, _):
            j, r = chunks[0] + i // 2, pl.ds(pl.multiple_of(lax.rem(i, 2) * 128, 128), 128)
            value = held[k, j, r].astype(f32) + held_in[k, j, r].astype(f32)
            for ref, low in terms:
                value = value + ref[j - low, r].astype(f32)
            held[k, j, r] = value.astype(bf)
            return 0
        lax.fori_loop(0, 2 * (chunks[1] - chunks[0]), step, 0)

    lax.fori_loop(0, 1, feed, 0)
    held_load[0].wait()
    arrive(held_in.at[0], held_sem[0])
    sum_held(0, (0, 4), [])
    held_far_sem = [remote(held.at[0, pl.ds(2 * way, 2)], held_far.at[way], zs[way]) for way in (0, 1)]
    lax.fori_loop(1, 3, feed, 0)
    held_near_sem = []
    for way in (0, 1):
        k = 1 + way
        held_load[k].wait()
        arrive(held_in.at[k], held_sem[k])
        sum_held(k, (2 - 2 * way, 4 - 2 * way), [])
        arrive(held_far.at[way], held_far_sem[way])
        sum_held(k, (2 * way, 2 * way + 2), [(held_far.at[way], 2 * way)])
        held_near_sem.append(remote(held.at[k], held_near.at[way], zs[way]))
    lax.fori_loop(3, 8, feed, 0)
    fetch = [bring(matrices.at[i], up.at[:, pl.ds(768 * i, 768)]) for i in range(4)]

    def piece(p, w, a):
        if p == 0:
            return down_w.at[pl.ds(pl.multiple_of(a * 768 + w * 192, 192), 192)]
        if p == 1:
            return upper.at[pl.ds(pl.multiple_of(w * 192, 192), 192), pl.ds(pl.multiple_of(a * 768, 768), 768)]
        return lower.at[pl.ds(pl.multiple_of(w * 768 + a * 192, 192), 192), pl.ds(384 * (p - 2), 384)]

    def own(p, k, s):
        return piece(p, 2 * s + core, lax.rem(first[p] + (2, 1, 3, 0)[k], 4))

    def result(p, a, start, size):
        if p < 2:
            return (wide_out, upper_out)[p].at[pl.ds(start, size), pl.ds(pl.multiple_of(a * 768, 768), 768)]
        return lower_out.at[pl.ds(pl.multiple_of(a * 192 + start, 16), size), pl.ds(384 * (p - 2), 384)]

    first = [x if part[1] else z for part in PARTS]
    second = [z if part[1] else x for part in PARTS]
    ring_one = [xs if part[1] else zs for part in PARTS]
    ring_two = [zs if part[1] else xs for part in PARTS]
    sems = {}

    def swap(p):
        for k, ahead in enumerate((2, 1, 3, 0)):
            a = lax.rem(first[p] + ahead, 4)
            sems["sib", p, k] = both([piece(p, 2 * s + 1 - core, a) for s in (0, 1)], sib_in[p].at[k], sib)

    def swapped(p, k):
        arrive(sib_in[p].at[k], sems["sib", p, k])

    def add(rows, into, terms):
        def body(i, _):
            at = pl.ds(pl.multiple_of(i * 48, 48), 48)
            total = into[at].astype(f32)
            for term in terms:
                total = total + term[at].astype(f32)
            into[at] = total.astype(bf)
            return 0
        lax.fori_loop(0, rows // 48, body, 0)

    def quarter(b):
        return pl.ds(pl.multiple_of(lax.rem(b, 4) * 48, 48), 48)

    def far(p):
        swapped(p, 0)
        for s in (0, 1):
            add(192, own(p, 0, s), [sib_in[p].at[0, s]])
            sems["far", p, s] = remote(own(p, 0, s), far_in[p].at[s], ring_one[p][s])

    def near(p):
        for way in (0, 1):
            k = 1 + way
            swapped(p, k)
            add(192, own(p, k, 1 - way), [sib_in[p].at[k, 1 - way]])
            arrive(far_in[p].at[way], sems["far", p, way])
            add(192, own(p, k, way), [sib_in[p].at[k, way], far_in[p].at[way]])
            sems["near", p, way] = both([own(p, k, s) for s in (0, 1)], near_in[p].at[way], ring_one[p][way])

    def mine(p):
        swapped(p, 3)
        for way in (0, 1):
            arrive(near_in[p].at[way], sems["near", p, way])
        for s in (0, 1):
            add(192, own(p, 3, s), [sib_in[p].at[3, s], near_in[p].at[0, s], near_in[p].at[1, s]])
        for s in (0, 1):
            sems["far2", p, s] = remote(own(p, 3, s).at[quarter(second[p] + 2)], far_two[p].at[s], ring_two[p][s])

    def near2(p):
        for way in (0, 1):
            at = quarter(second[p] + 1 + 2 * way)
            arrive(far_two[p].at[way], sems["far2", p, way])
            add(48, own(p, 3, way).at[at], [far_two[p].at[way]])
            sems["near2", p, way] = both([own(p, 3, s).at[at] for s in (0, 1)], near_two[p].at[way], ring_two[p][way])

    def mine2(p):
        at = quarter(second[p])
        for way in (0, 1):
            arrive(near_two[p].at[way], sems["near2", p, way])
        for s in (0, 1):
            add(48, own(p, 3, s).at[at], [near_two[p].at[0, s], near_two[p].at[1, s]])
        for i, half in enumerate((yh, 1 - yh, 1 - yh)):
            sems["y", p, i] = remote(own(p, 3, half).at[at], y_in[p].at[i], ys[i])

    def total(p):
        for i in range(3):
            arrive(y_in[p].at[i], sems["y", p, i])
        value = own(p, 3, yh)[quarter(second[p])].astype(f32)
        for i in range(3):
            value = value + y_in[p][i].astype(f32)
        done = result(p, first[p], pl.multiple_of(second[p] * 48, 16), 48)
        done[...] = value.astype(bf)
        for way in (0, 1):
            sems["ring", p, way] = remote(done, done, ring_two[p][way])

    cuts = ((0, 32), (32, 16))

    def relay(p):
        for way in (0, 1):
            b = lax.rem(second[p] + 3 - 2 * way, 4)
            arrive(result(p, first[p], pl.multiple_of(b * 48, 16), 48), sems["ring", p, way])
            part = result(p, first[p], pl.multiple_of(b * 48 + cuts[way][0], 16), cuts[way][1])
            sems["relay", p, way] = remote(part, part, ring_two[p][way])

    def last(p):
        b = lax.rem(second[p] + 2, 4)
        for way in (0, 1):
            arrive(result(p, first[p], pl.multiple_of(b * 48 + cuts[way][0], 16), cuts[way][1]), sems["relay", p, way])
        block = result(p, first[p], 0, 192)
        for way in (0, 1):
            sems["last", p, way] = remote(block, block, ring_one[p][way])

    def end(p):
        for way in (0, 1):
            a = lax.rem(first[p] + 3 - 2 * way, 4)
            arrive(result(p, a, 0, 192), sems["last", p, way])
            part = result(p, a, 96 * way, 96)
            sems["end", p, way] = remote(part, part, ring_one[p][way])

    def close(p):
        for way in (0, 1):
            arrive(result(p, lax.rem(first[p] + 2, 4), 96 * way, 96), sems["end", p, way])

    def tiny_stage(step):
        groups = ([sib], xs, zs, ys)
        if step > 0:
            for i in range(len(groups[step - 1])):
                arrive(tiny_in.at[step - 1, i], sems["tiny", step - 1, i])
            value = tiny[step - 1]
            for i in range(len(groups[step - 1])):
                value = value + tiny_in[step - 1, i]
            if step == 4:
                vector_out[...] = value
                return
            tiny[step] = value
        for i, to in enumerate(groups[step]):
            sems["tiny", step, i] = remote(tiny.at[step], tiny_in.at[step, i], to)

    group_one = (1, 2, 3)
    for p in group_one:
        swap(p)
    for way in (0, 1):
        arrive(held_near.at[way], held_near_sem[way])
    held_load[3].wait()
    arrive(held_in.at[3], held_sem[3])
    sum_held(3, (0, 4), [(held_near.at[0], 0), (held_near.at[1], 0)])
    dkv_sem = [exchange(held.at[3], dkv_own.at[x], d) for d in range(4)]
    for p in group_one:
        far(p)
    for d in range(4):
        h = lax.rem(x + 4 - d, 4)
        arrive(odq_own.at[h], odq_sem[d])
        arrive(dkv_own.at[h], dkv_sem[d])

    left = lax.broadcasted_iota(jnp.int32, (ROWS, 128), 1) < 64
    keep, ahead, behind = tables[0], tables[1], tables[2]

    def turn_back(tile):
        return tile * keep + pltpu.roll(tile * ahead, 8, 1) + pltpu.roll(tile * behind, 120, 1)

    def unpack(slabs, t):
        even, odd = (slabs[h // 3, :, 128 * (h % 3):128 * (h % 3) + 128].astype(f32) for h in (2 * t, 2 * t + 1))
        return jnp.where(left, even, pltpu.roll(odd, 64, 1)), jnp.where(left, pltpu.roll(even, 64, 1), odd)

    for t in range(6):
        lanes = slice(128 * t, 128 * t + 128)
        out, query = unpack(odq_own, t)
        key, value = unpack(dkv_own, t)
        attended[:, lanes] = out.astype(bf)
        mixed[0, :, lanes] = (turn_back(query) * 0.125).astype(bf)
        mixed[1, :, lanes] = turn_back(key).astype(bf)
        mixed[2, :, lanes] = value.astype(bf)
    g = grad[...]
    one = normed_one[...]
    for i in range(3):
        down_w[768 * i:768 * i + 768] = dot(one, mixed[i], 0, 0).astype(bf)
    down_w[2304:] = dot(attended[...], g, 0, 0).astype(bf)
    swap(0)
    for p in group_one:
        near(p)
    far(0)
    for copy in fetch:
        copy.wait()
    values = tokens[...].astype(f32)
    centered = values - jnp.mean(values, -1, keepdims=True)
    scale = lax.rsqrt(jnp.mean(centered * centered, -1, keepdims=True) + 1e-05)
    unit = centered * scale
    back_one = dot(mixed[0], up[:, 1536:2304], 1, 1) + dot(mixed[1], up[:, 0:768], 1, 1) + dot(mixed[2], up[:, 768:1536], 1, 1)
    wide_grad = g.astype(f32)
    into = wide_grad
    sums = []
    for back, gain in ((back_one, vectors[0:1]), (back_two[...], vectors[2:3])):
        sums.append(jnp.sum(back * unit, 0, keepdims=True))
        sums.append(jnp.sum(back, 0, keepdims=True))
        scaled = back * gain
        into = into + scale * (scaled - jnp.mean(scaled, -1, keepdims=True) - unit * jnp.mean(scaled * unit, -1, keepdims=True))
    input_grad[...] = into.astype(bf)
    sums.append(jnp.sum(wide_grad, 0, keepdims=True))
    sums.extend(jnp.sum(mixed[i].astype(f32), 0, keepdims=True) for i in range(3))
    sums.extend(bias_grad[0:1, 768 * i:768 * i + 768] for i in range(4))
    tiny[0] = jnp.concatenate(sums + [jnp.zeros((4, 768), f32)], 0)
    tiny_stage(0)
    for p in group_one:
        mine(p)
    layer_output[...] = (values + mlp[...] + dot(attended[...], up[:, 2304:3072], 1, 0) + vectors[4:5]).astype(bf)
    tiny_stage(1)
    near(0)
    for p in group_one:
        near2(p)
    tiny_stage(2)
    mine(0)
    for p in group_one:
        mine2(p)
    tiny_stage(3)
    for p in group_one:
        total(p)
    near2(0)
    for p in group_one:
        relay(p)
    mine2(0)
    for p in group_one:
        last(p)
    total(0)
    tiny_stage(4)
    relay(0)
    for p in group_one:
        end(p)
    last(0)
    for p in group_one:
        close(p)
    end(0)
    close(0)
    for ref, sem in pairs:
        landed(ref, send_sem.at[sem])
    for copy in sent:
        copy.wait_send()
    for copy in maybe:
        @pl.when(swapped_place)
        def _():
            copy.wait_send()


def back(odq, dkv, tokens, grad, normed_one, normed_two, vectors, tables, matrices, up, down, collective_id=1):
    hbm = pl.BlockSpec(memory_space=pl.ANY)
    vmem = pl.BlockSpec(memory_space=pltpu.VMEM)
    dma = pltpu.SemaphoreType.DMA
    bf, f32 = jnp.bfloat16, jnp.float32
    scratch = []
    for front_dims, rows in (((4, 2), 192), ((2,), 192), ((2, 2), 192), ((2,), 48), ((2, 2), 48), ((3,), 48)):
        for columns, _ in PARTS:
            scratch.append(pltpu.VMEM(front_dims + (rows, columns), bf))
    plain = ((ROWS, 768), bf)
    for shape, kind in (
        plain, plain, plain, plain, ((16, 768), f32), ((3, ROWS, 128), f32), ((768, 3072), bf), ((3072, 768), bf),
        ((768, 3072), bf), ((3072, 768), bf), ((ROWS, 768), f32), ((ROWS, 768), f32), ((8, 3072), f32), ((8, 3072), f32),
        ((4, 4, ROWS, WIDE), bf), ((4, 4, ROWS, WIDE), bf), ((2, 2, ROWS, WIDE), bf), ((2, 4, ROWS, WIDE), bf),
        ((4, ROWS, WIDE), bf), ((4, ROWS, WIDE), bf), plain, ((3, ROWS, 768), bf), ((4, 16, 768), f32), ((4, 3, 16, 768), f32),
    ):
        scratch.append(pltpu.VMEM(shape, kind))
    scratch += [dma((140,)), dma((140,)), dma((16,))]
    rows = jax.ShapeDtypeStruct((ROWS, 768), bf)
    return pl.pallas_call(
        back_kernel,
        out_shape=(rows, rows, jax.ShapeDtypeStruct((192, 3072), bf), jax.ShapeDtypeStruct((192, 3072), bf),
                   jax.ShapeDtypeStruct((768, 768), bf), jax.ShapeDtypeStruct((16, 768), f32)),
        in_specs=[hbm] * 11, out_specs=(vmem,) * 6,
        scratch_shapes=scratch,
        compiler_params=pltpu.CompilerParams(collective_id=collective_id, has_side_effects=True, vmem_limit_bytes=62 * 2**20),
        name="back",
    )(odq, dkv, tokens, grad, normed_one, normed_two, vectors, tables, matrices, up, down)


D = 768
HEADS = 12
HD = 64
ROT = 16
TOK_DEV = 256


def rotary_tables(positions):
    lanes = jnp.arange(128) % HD
    exponents = (lanes % 8).astype(jnp.float32) * 2.0 / ROT
    inverse = 10000.0 ** (-exponents)
    angles = positions.astype(jnp.float32)[:, None] * inverse[None, :]
    cosine, sine = jnp.cos(angles), jnp.sin(angles)
    keep = jnp.where(lanes < ROT, cosine, 1.0)
    ahead = jnp.where(lanes < 8, -sine, 0.0)
    behind = jnp.where((lanes >= 8) & (lanes < ROT), sine, 0.0)
    return jnp.stack([keep, ahead, behind])


def on_device(
    tokens, cotangent, pairing, first_gain, first_shift, qkv_weight, qkv_bias, dense_weight,
    second_gain, second_shift, up_weight, up_bias, down_weight, out_bias,
):
    bf, f32 = jnp.bfloat16, jnp.float32
    total_blocks = 64
    offsets = jnp.arange(BLK, dtype=jnp.int32)
    ctx_index = lax.axis_index("ctx")
    core = lax.rem(lax.axis_index("wsh"), 2)
    seq_of_layout = jnp.stack([pairing, total_blocks - 1 - pairing], 1).reshape(-1)
    layout_of_seq = (
        jnp.zeros((total_blocks,), jnp.int32)
        .at[seq_of_layout]
        .set(jnp.arange(total_blocks, dtype=jnp.int32))
    )
    own_blocks = lax.dynamic_slice(seq_of_layout, (2 * ctx_index,), (2,))
    row_blocks = lax.dynamic_slice(seq_of_layout, (16 * (ctx_index // 8) + 8 * core,), (8,))
    local_pos = (own_blocks[:, None] * BLK + offsets[None, :]).reshape(-1)
    tables = rotary_tables(local_pos)
    query_scale = HD ** (-0.5)

    shard = lax.broadcasted_iota(jnp.int32, (4, 1), 0) == lax.axis_index("wsh")
    small = (first_gain, first_shift, second_gain, second_shift, out_bias, qkv_bias, up_bias)
    spots = [jnp.where(shard, v[None, :], 0.0).astype(bf).reshape(-1) for v in small]
    vectors = jnp.concatenate(spots + [jnp.zeros((4 * D,), bf)]).reshape(16, D)
    grad_rows = cotangent[0]
    keys_values, queries_grads, normed_one, normed_two, vectors, matrices = front(
        tokens[0], grad_rows, tables, qkv_weight, dense_weight, vectors
    )
    up_shard, down_shard, keys_values = lax.optimization_barrier((up_weight, down_weight, keys_values))
    up_matrix = lax.all_gather(up_shard, "wsh", axis=0, tiled=True)
    down_matrix = lax.all_gather(down_shard, "wsh", axis=0, tiled=True)
    attended_dq, grad_kv = attention(row_blocks, layout_of_seq, queries_grads.reshape(1024, WIDE), keys_values.reshape(8192, WIDE))
    layer_output, input_grad, wide, upper, lower, sums = back(
        attended_dq.reshape(4, ROWS, WIDE), grad_kv.reshape(32, ROWS, WIDE), tokens[0], grad_rows, normed_one, normed_two,
        vectors, tables, matrices, up_matrix, down_matrix,
    )
    mine = lax.axis_index("wsh")
    gains = lax.dynamic_slice(sums, (0, 192 * mine), (5, 192))
    qkv_offset_grad = lax.dynamic_slice(sums[5:8].reshape(-1), (576 * mine,), (576,))
    up_offset_grad = lax.dynamic_slice(sums, (8 + mine, 0), (1, D))[0]
    return (
        layer_output[None], input_grad[None], gains[0], gains[1], wide[:, :2304].astype(f32), qkv_offset_grad,
        wide[:, 2304:].astype(f32), gains[2], gains[3], upper.astype(f32), up_offset_grad, lower.astype(f32), gains[4],
    )


def solution(mesh):
    rows, split, flat = P("wsh", "ctx", None), P("wsh", None), P("wsh")
    return jax.shard_map(
        on_device,
        mesh=mesh,
        in_specs=(rows, rows, P(), flat, flat, split, flat, split, flat, flat, split, flat, split, flat),
        out_specs=(rows, rows, flat, flat, split, flat, split, flat, flat, split, flat, split, flat),
        check_vma=False,
    )
```

time: 362 us -> 344 us (0.950)
  matrix products: 11.2 us -> 0 us
  Pallas kernels: 288 us -> 298 us
  other arithmetic: 21.5 us -> 12.1 us
  local copies, waits for them, and re-layouts: 25.1 us -> 18.1 us
    dot_general x6 -> x0, matrix products: 11.2 us -> none  [the longest x5 8.61 us: contract(): lax.dot_general(left_side, right_side, (((left_dim,), (right_dim,)), ((),...]
    pallas_call x2 -> x1, Pallas kernels: 135 us -> 145 us  [back(): pl.pallas_call(back_kernel, out_shape=(rows, rows, jax.ShapeDtypeStruct((...]
    concatenate x2 -> x0, other arithmetic: 4.11 us -> none  [the longest x1 2.77 us: sum_gradients(): wide = jnp.concatenate([qkv.astype(bf), dense.astype(bf)], 1)]
    unnamed x55 -> x37, local copies, waits for them, and re-layouts: 10 us -> 11.1 us
  transfers between devices with their start and end apart: 2 -> 2, of which waited for: 0 -> 0; matrix products, arithmetic and copies ran while one was open for 1% -> 1% of each run, Pallas kernels for 23% -> 24%
where the time goes in v3:
time: 344 us; the launch traced here: 343 us
  Pallas kernels  298 us (87%)
  local copies, waits for them, and re-layouts  18.1 us (5%)
  between operations  14.3 us (4%)
  other arithmetic  12.1 us (4%)
    pallas_call x1, Pallas kernels, back(): pl.pallas_call(back_kernel, out_shape=(rows, rows, jax.ShapeDtypeStruct((...  145 us
    pallas_call x1, Pallas kernels, attention(): pl.pallas_call(functools.partial(attn_kernel, chunk), out_shape=(jax.Shap...  83.2 us
    pallas_call x1, Pallas kernels, front(): pl.pallas_call(front_kernel, out_shape=(jax.ShapeDtypeStruct((32, ROWS, W...  69.6 us
    unnamed x37, local copies, waits for them, and re-layouts  11.1 us
  transfers between devices with their start and end apart: 2, of which 0 were waited for; matrix products, arithmetic and copies ran while one was open for 1% of the time, Pallas kernels for 24%

profile of v3, /device:TPU:0, one launch (start us, length us, event | category | flops | bytes accessed | tf_op | source)
XLA Modules:
  0.0 343.1 jit_solution(2045217598707059115)
XLA Ops:
  7.2 0.0 copy-start.4
  7.2 0.0 all-gather.3.cloned.1.call-start
  7.3 0.7 subtract_bitcast_fusion
  8.0 0.7 pad_add_fusion
  8.7 0.1 copy.29
  8.8 0.1 reshape.366
  8.9 0.8 broadcast_select_fusion.2
  9.7 0.1 select_n.147
  9.8 0.1 select_n.149
  9.9 0.1 select_n.151
  9.9 0.1 select_n.153
  10.0 0.1 select_n.155
  10.1 0.8 broadcast_select_fusion.1
  10.9 0.1 select_n.157
  11.0 0.8 broadcast_select_fusion
  11.7 0.2 dynamic-update-slice
  12.0 0.2 dynamic-update-slice.1
  12.2 0.2 dynamic-update-slice.2
  12.4 0.2 dynamic-update-slice.3
  12.6 0.2 dynamic-update-slice.4
  12.8 0.3 dynamic-update-slice.5
  13.1 0.1 dynamic-slice_multiply_fusion
  13.2 0.1 convert_bitcast_fusion
  13.3 0.6 fusion.3
  13.9 0.0 copy-start.1
  13.9 0.0 copy-done.4
  13.9 0.0 copy-start.2
  13.9 1.1 copy-done.2
  15.0 0.0 copy-start.3
  15.0 1.0 copy-done.3
  16.0 1.0 copy-done.8
  17.0 69.6 %front.1 = (bf16[32,256,384]{2,1,0:T(8,128)(2,1)}, bf16[4,256,384]{2,1,0:T(8,128)(2,1)S(1)}, bf16[256,768]{1,0:T(8,128)(2,1)S(1)}, bf16[256,768]{1,0:T(8,128)(2,...) custom-call(bf16[256,768]{1,0:T(8,128)(2,1)S(1)} %bitcast.21, bf16[256,768]{1,0:T(8,128)(2,1)S(1)} %bitcast.23, ...), custom_call_target="tpu_custom_call" | custom-call | tf_op jit(solution)/shard_map/front/pallas_call | solution.py:353
  86.6 0.0 copy-start
  86.6 2.2 copy-done
  88.8 0.9 copy-done.5
  89.7 0.7 copy-done.6
  90.4 0.7 copy-done.7
  91.1 0.6 copy-done.9
  91.8 0.0 all-gather.3.cloned.1.call-update
  91.8 0.0 copy-done.1
  91.8 0.0 all-gather.5.cloned.1.call-start
  91.9 0.7 all-gather.5.cloned.1.call-update
  92.6 0.1 reshape.367
  92.7 0.6 dynamic_slice.15.qpos
  93.3 1.3 scatter_custom_fusion.lay
  94.5 83.2 %attention.1 = (bf16[1024,384]{1,0:T(8,128)(2,1)}, bf16[8192,384]{1,0:T(8,128)(2,1)}) custom-call(s32[8]{0:T(128)} %dynamic_slice.15.qpos, s32[64]{0:T(128)} %scatter_custom_fusion.lay, bf16[1024,384]{1,0:T(8,128)(2,1)} %bitcast.24, bf16[8192,384]{1,0:T(8,128)(2,1)} %bitcast.25), custom_call_target="tpu_custom_call" | custom-call | tf_op jit(solution)/shard_map/attention/pallas_call | solution.py:119
  177.8 0.0 all-gather.3.cloned.1.call-done.up_hbm
  177.8 0.0 all-gather.5.cloned.1.call-done.down_hbm
  177.9 144.9 %back.1 = (bf16[256,768]{1,0:T(8,128)(2,1)}, bf16[256,768]{1,0:T(8,128)(2,1)}, bf16[192,3072]{1,0:T(8,128)(2,1)}, bf16[192,3072]{1,0:T(8,128)(2,1)}, bf16[768,768]{1,0:T(8,128)(2,1)}, /*index=5*/f32[16,768]{1,0:T(8,128)}) custom-call(bf16[4,256,384]{2,1,0:T(8,128)(2,1)} %bitcast.27, bf16[32,256,384]{2,1,0:T(8,128)(2,1)} %bitcast.26, ...), custom_call_target="tpu_custom_call" | custom-call | tf_op jit(solution)/shard_map/back/pallas_call | solution.py:768
  322.8 0.0 copy-start.11
  322.8 2.6 slice_convert_fusion
  325.4 1.8 slice_convert_fusion.1
  327.2 0.0 copy-done.11
  327.2 1.7 convert_element_type.44
  328.8 0.0 copy-done.10
  328.9 1.6 convert_element_type.45
  330.4 0.7 slice.27
  331.2 1.3 dynamic-slice_reduce_fusion
  332.5 0.7 dynamic_slice.18
  333.2 1.5 fusion.12
  334.7 0.0 copy-done.13
  334.7 0.7 copy.41
  335.5 0.0 copy-done.12
  335.5 0.7 copy.42
  (21 shorter events, 0.2 us)
Async XLA Ops:
  7.2 6.7 %copy-start.4 = (bf16[192,2304]{1,0:T(8,128)(2,1)S(1)}, bf16[192,2304]{1,0:T(8,128)(2,1)}, u32[]{:S(2)}) copy-start(bf16[192,2304]{1,0:T(8,128)(2,1)} %qkv.1) | copy-start | bytes 2654212
  7.2 170.6 %all-gather.3.cloned.1.call-start = ((), (), s32[]{:S(2)}) async-start(), calls=%async_computation | async-start | bytes 5898240 | tf_op jit(solution)/shard_map/all_gather | solution.py:828
  13.9 77.9 %copy-start.1 = (f32[3,256,128]{2,1,0:T(8,128)}, f32[3,256,128]{2,1,0:T(8,128)S(1)}, u32[]{:S(2)}) copy-start(f32[3,256,128]{2,1,0:T(8,128)S(1)} %pad_maximum_fusion.tables.tables_hbm) | copy-start | bytes 1179652
  13.9 1.1 copy-start.2
  15.0 1.0 copy-start.3
  16.0 1.0 copy-start.8
  86.6 2.2 copy-start
  88.8 0.9 copy-start.5
  89.7 0.7 copy-start.6
  90.4 0.7 copy-start.7
  91.1 0.6 copy-start.9
  91.8 86.0 %all-gather.5.cloned.1.call-start = ((), (), s32[]{:S(2)}) async-start(), calls=%async_computation.1 | async-start | bytes 5898240 | tf_op jit(solution)/shard_map/all_gather | solution.py:829
  322.8 4.4 %copy-start.11 = (bf16[192,3072]{1,0:T(8,128)(2,1)S(1)}, bf16[192,3072]{1,0:T(8,128)(2,1)}, u32[]{:S(2)}) copy-start(bf16[192,3072]{1,0:T(8,128)(2,1)} %get-tuple-element.45) | copy-start | bytes 3538948
  327.2 1.7 copy-start.10
  328.8 5.9 %copy-start.13 = (bf16[256,768]{1,0:T(8,128)(2,1)S(1)}, bf16[256,768]{1,0:T(8,128)(2,1)}, u32[]{:S(2)}) copy-start(bf16[256,768]{1,0:T(8,128)(2,1)} %get-tuple-element.41) | copy-start | bytes 1179652
  328.9 6.6 %copy-start.12 = (bf16[256,768]{1,0:T(8,128)(2,1)S(1)}, bf16[256,768]{1,0:T(8,128)(2,1)}, u32[]{:S(2)}) copy-start(bf16[256,768]{1,0:T(8,128)(2,1)} %get-tuple-element.42) | copy-start | bytes 1179652
Sparse Core Ops, SparseCore 0:
  91.9 38.9 all-gather.2
  132.6 40.8 all-gather.4

commit v4 on v3

--- a/solution.py
+++ b/solution.py
@@ -21,12 +21,14 @@
     lax.fori_loop(0, nblk, load, 0)
 
     def land(i, _):
-        rows = pl.ds(pl.multiple_of(i * BLK, BLK), BLK)
-        pltpu.make_async_copy(kv_hbm.at[pl.ds(0, BLK)], kv.at[rows], sem.at[i]).wait()
-        acc[rows] = jnp.zeros((BLK, G * 128), f32)
+        rows = pl.ds(pl.multiple_of(i * chunk, chunk), chunk)
+        for j in range(blocks):
+            at = pl.ds(pl.multiple_of(i * chunk + j * BLK, BLK), BLK)
+            pltpu.make_async_copy(kv_hbm.at[pl.ds(0, BLK)], kv.at[at], sem.at[i * blocks + j]).wait()
+        acc[rows] = jnp.zeros((chunk, G * 128), f32)
         kvt[:, rows] = kv[rows].T
         return 0
-    lax.fori_loop(0, nblk, land, 0)
+    lax.fori_loop(0, nblk // blocks, land, 0)
 
     upper = lax.broadcasted_iota(jnp.int32, (128, 128), 0) < 64
     left = lax.broadcasted_iota(jnp.int32, (128, 128), 1) < 64
@@ -38,11 +40,14 @@
         pairs = [qdo[qrows, h * 128:(h + 1) * 128] for h in range(G)]
         turned = [p.astype(f32).T for p in pairs]
         wide = [jnp.concatenate([jnp.where(upper, turned[h], 0.0).astype(bf), jnp.where(upper, 0.0, turned[h]).astype(bf)], 1) for h in range(G)]
-        key_i = lax.broadcasted_iota(jnp.int32, (chunk, BLK), 0)
-        row_i = lax.broadcasted_iota(jnp.int32, (chunk, BLK), 1) + (b - last * blocks) * BLK
-
-        def fwd(c, state, masked):
-            at = pl.ds(pl.multiple_of(c * chunk, chunk), chunk)
+        rest = b - last * blocks
+
+        def pick(step, state):
+            sizes = [chunk * (i + 1) // 4 for i in range(4)]
+            return lax.switch(rest // (blocks // 4), [functools.partial(step, size) for size in sizes], state)
+
+        def fwd(c, state, masked, size=chunk):
+            at = pl.ds(pl.multiple_of(c * chunk, chunk), size)
             out = []
             every = [jnp.dot(kv[at, h * 128:(h + 1) * 128], wide[h], preferred_element_type=f32) for h in range(G)]
             kept = []
@@ -51,6 +56,8 @@
                 s = every[h][:, :128]
                 grads[at, h * 128:(h + 1) * 128] = every[h][:, 128:]
                 if masked:
+                    key_i = lax.broadcasted_iota(jnp.int32, (size, BLK), 0)
+                    row_i = lax.broadcasted_iota(jnp.int32, (size, BLK), 1) + rest * BLK
                     s = jnp.where(key_i <= row_i, s, NEG)
                 new = jnp.maximum(m, jnp.max(s, 0, keepdims=True))
                 p = jnp.exp(s - new)
@@ -68,7 +75,7 @@
 
         state = tuple((jnp.full((1, BLK), NEG, f32), jnp.zeros((1, BLK), f32), jnp.zeros((64, BLK), f32)) for _ in range(G))
         state = lax.fori_loop(0, last, lambda c, s: fwd(c, s, False), state)
-        state = fwd(last, state, True)
+        state = pick(lambda size, s: fwd(last, s, True, size), state)
         lse, delta, outs = [], [], []
         for h in range(G):
             m, l, o = state[h]
@@ -78,8 +85,8 @@
             delta.append(jnp.sum(o * turned[h][64:], 0, keepdims=True))
         narrow = [jnp.concatenate([jnp.where(left, pairs[h], jnp.zeros_like(pairs[h])), jnp.where(left, jnp.zeros_like(pairs[h]), pairs[h])], 0) for h in range(G)]
 
-        def bwd(c, state):
-            at = pl.ds(pl.multiple_of(c * chunk, chunk), chunk)
+        def bwd(c, state, size=chunk):
+            at = pl.ds(pl.multiple_of(c * chunk, chunk), size)
             out, work = [], []
             for h in range(G):
                 cols = slice(h * 128, (h + 1) * 128)
@@ -93,23 +100,32 @@
             return tuple(out)
 
         dq = tuple(jnp.zeros((64, BLK), f32) for _ in range(G))
-        dq = lax.fori_loop(0, last + 1, bwd, dq)
+        dq = lax.fori_loop(0, last, bwd, dq)
+        dq = pick(lambda size, s: bwd(last, s, size), dq)
         for h in range(G):
             odq[qrows, h * 128:(h + 1) * 128] = jnp.concatenate([outs[h], dq[h]], 0).T.astype(bf)
         return 0
     lax.fori_loop(0, qpos.shape[0], q_block, 0)
 
+    def leave(slot, j):
+        return pltpu.make_async_copy(stage.at[slot, j], dkv_hbm.at[pl.ds(0, BLK)], osem.at[slot, j])
+
     def send(i, _):
-        slot = lax.rem(i, 8)
-        @pl.when(i >= 8)
+        slot = lax.rem(i, 2)
+        @pl.when(i >= 2)
         def _():
-            pltpu.make_async_copy(stage.at[slot], dkv_hbm.at[pl.ds(0, BLK)], osem.at[slot]).wait()
-        stage[slot] = acc[pl.ds(pl.multiple_of(i * BLK, BLK), BLK)].astype(bf)
-        pltpu.make_async_copy(stage.at[slot], dkv_hbm.at[pl.ds(pl.multiple_of(lay[i] * BLK, BLK), BLK)], osem.at[slot]).start()
+            for j in range(4):
+                leave(slot, j).wait()
+        for j in range(4):
+            at = i * 4 + j
+            stage[slot, j] = acc[pl.ds(pl.multiple_of(at * BLK, BLK), BLK)].astype(bf)
+            pltpu.make_async_copy(stage.at[slot, j], dkv_hbm.at[pl.ds(pl.multiple_of(lay[at] * BLK, BLK), BLK)], osem.at[slot, j]).start()
         return 0
-    lax.fori_loop(0, nblk, send, 0)
-    for slot in range(8):
-        pltpu.make_async_copy(stage.at[slot], dkv_hbm.at[pl.ds(0, BLK)], osem.at[slot]).wait()
+    lax.fori_loop(0, nblk // 4, send, 0)
+    for slot in range(2):
+        for j in range(4):
+            leave(slot, j).wait()
+
 
 def attention(qpos, lay, qdo, kv, chunk=1024):
     n = kv.shape[0]
@@ -122,8 +138,8 @@
         in_specs=[smem, smem, vmem, hbm], out_specs=(vmem, hbm),
         scratch_shapes=[pltpu.VMEM((n, G * 128), jnp.bfloat16), pltpu.VMEM((G * 128, n), jnp.bfloat16),
             pltpu.VMEM((n, G * 128), jnp.float32), pltpu.VMEM((n, G * 128), jnp.bfloat16), pltpu.VMEM((n, G * 128), jnp.float32), pltpu.VMEM((n // chunk, G, 8, BLK), jnp.float32),
-            pltpu.VMEM((8, BLK, G * 128), jnp.bfloat16),
-            pltpu.SemaphoreType.DMA((n // BLK,)), pltpu.SemaphoreType.DMA((8,))],
+            pltpu.VMEM((2, 4, BLK, G * 128), jnp.bfloat16),
+            pltpu.SemaphoreType.DMA((n // BLK,)), pltpu.SemaphoreType.DMA((2, 4))],
         compiler_params=pltpu.CompilerParams(vmem_limit_bytes=62 * 2**20),
         name="attention",
     )(qpos, lay, qdo, kv)
@@ -157,9 +173,12 @@
     pltpu.make_async_copy(ref, ref, sem).wait()
 
 
-def front_kernel(tokens, grad, tables, qkv, dense, vectors, kv_all, qdo, normed_one, normed_two, all_vectors, weights_out,
-                 weights, vec_in, kvs, qds, local_sem, send_sem, recv_sem, kv_send, kv_recv, q_send, q_recv):
+def front_kernel(tokens_hbm, grad_hbm, tables_hbm, qkv, dense, vectors_hbm, kv_all, qdo, one_hbm, two_hbm, vectors_out, weights_out,
+                 tokens, grad, tables, vectors, normed_one, normed_two, all_vectors, bring_sem, weights, vec_in, kvs, qds, local_sem, send_sem, recv_sem, kv_send, kv_recv, q_send, q_recv):
     z, yl, x, yh, core = place()
+    bring = [pltpu.make_async_copy(src, dst, bring_sem.at[i]) for i, (src, dst) in enumerate(((vectors_hbm, vectors), (tokens_hbm, tokens), (tables_hbm, tables), (grad_hbm, grad)))]
+    for copy in bring:
+        copy.start()
     f32, bf = jnp.float32, jnp.bfloat16
     me = yh * 2 + core
     far = (1 - yh) * 2 + core
@@ -192,6 +211,7 @@
     shards = [qkv.at[:, pl.ds(768, 768)], qkv.at[:, pl.ds(1536, 768)], qkv.at[:, pl.ds(0, 768)], dense]
     quarter = [x, z, x, z]
     ring = [xs, zs, xs, zs]
+    bring[0].wait()
     vec_sem = [remote(vectors, vec_in.at[i], to) for i, to in enumerate([sib] + others)]
     cross_sem = [remote(shards[i].at[pl.ds(pl.multiple_of(quarter[i] * 48, 16), 48)], rows(i, me * 192 + quarter[i] * 48, 48), cross) for i in range(4)]
     own, late = [], [[], [], [], []]
@@ -201,6 +221,8 @@
         own.append(copy)
         late[i].append((rows(i, (yh * 2 + 1 - core) * 192, 192), remote(shards[i], rows(i, me * 192, 192), sib)))
 
+    for copy in bring[1:]:
+        copy.wait()
     values = tokens[...].astype(f32)
     centered = values - jnp.mean(values, -1, keepdims=True)
     unit = centered * lax.rsqrt(jnp.mean(centered * centered, -1, keepdims=True) + 1e-05)
@@ -211,6 +233,9 @@
     normed_one[...] = (unit * vec[0:1] + vec[1:2]).astype(bf)
     normed_two[...] = (unit * vec[2:3] + vec[3:4]).astype(bf)
 
+    leave = [pltpu.make_async_copy(src, dst, bring_sem.at[4 + i]) for i, (src, dst) in enumerate(((all_vectors, vectors_out), (normed_one, one_hbm), (normed_two, two_hbm)))]
+    for copy in leave:
+        copy.start()
     cuts = ((0, 32), (32, 16))
     ring_sem, half_sem = {}, {}
 
@@ -333,6 +358,8 @@
             arrive(slot(z + 2, 1 - core, d).at[pl.ds(way * half, half)], sib_sem[3 + way, d])
         landed(qdo.at[lax.rem(x + 4 - d, 4)], q_recv.at[d])
     keep_out.wait()
+    for copy in leave:
+        copy.wait()
     for copy in sent:
         copy.wait_send()
     for d, copy in sent_kv + sent_q:
@@ -346,7 +373,6 @@
 
 def front(tokens, grad, tables, qkv, dense, vectors, collective_id=0):
     hbm = pl.BlockSpec(memory_space=pl.ANY)
-    vmem = pl.BlockSpec(memory_space=pltpu.VMEM)
     dma = pltpu.SemaphoreType.DMA
     bf, f32 = jnp.bfloat16, jnp.float32
     rows = jax.ShapeDtypeStruct((ROWS, 768), bf)
@@ -354,15 +380,16 @@
         front_kernel,
         out_shape=(jax.ShapeDtypeStruct((32, ROWS, WIDE), bf), jax.ShapeDtypeStruct((4, ROWS, WIDE), bf), rows, rows,
                    jax.ShapeDtypeStruct((16, 768), f32), jax.ShapeDtypeStruct((4, 768, 768), bf)),
-        in_specs=[vmem, vmem, vmem, hbm, hbm, vmem], out_specs=(hbm, hbm, vmem, vmem, vmem, hbm),
-        scratch_shapes=[pltpu.VMEM((4, 768, 768), bf), pltpu.VMEM((3, 16, 768), bf), pltpu.VMEM((4, ROWS, WIDE), bf), pltpu.VMEM((4, ROWS, WIDE), bf),
+        in_specs=[hbm] * 6, out_specs=(hbm,) * 6,
+        scratch_shapes=[pltpu.VMEM((ROWS, 768), bf), pltpu.VMEM((ROWS, 768), bf), pltpu.VMEM((3, ROWS, 128), f32), pltpu.VMEM((16, 768), bf),
+                        pltpu.VMEM((ROWS, 768), bf), pltpu.VMEM((ROWS, 768), bf), pltpu.VMEM((16, 768), f32), dma((7,)), pltpu.VMEM((4, 768, 768), bf), pltpu.VMEM((3, 16, 768), bf), pltpu.VMEM((4, ROWS, WIDE), bf), pltpu.VMEM((4, ROWS, WIDE), bf),
                         dma((5,)), dma((100,)), dma((100,)), dma((4,)), dma((4,)), dma((4,)), dma((4,))],
-        compiler_params=pltpu.CompilerParams(collective_id=collective_id, has_side_effects=True, vmem_limit_bytes=40 * 2**20),
+        compiler_params=pltpu.CompilerParams(collective_id=collective_id, has_side_effects=True, vmem_limit_bytes=62 * 2**20),
         name="front",
     )(tokens, grad, tables, qkv, dense, vectors)
 
 
-PARTS = ((768, False), (768, True), (384, True), (384, False))
+PARTS = ((384, False), (384, True), (768, True), (384, True), (384, False))
 TILE = 384
 
 
@@ -380,9 +407,9 @@
 
 def back_kernel(odq, dkv, tokens_hbm, grad_hbm, one_hbm, two_hbm, vectors_hbm, tables_hbm, matrices, up_hbm, down_hbm,
                 layer_output, input_grad, wide_out, upper_out, lower_out, vector_out, *refs):
-    sib_in, far_in, near_in, far_two, near_two, y_in = (refs[4 * i : 4 * i + 4] for i in range(6))
+    sib_in, far_in, near_in, far_two, near_two, y_in = (refs[5 * i : 5 * i + 5] for i in range(6))
     (tokens, grad, normed_one, normed_two, vectors, tables, up, down_w, upper, lower, mlp, back_two, up_bias, bias_grad,
-     held, held_in, held_far, held_near, odq_own, dkv_own, attended, mixed, tiny, tiny_in, send_sem, recv_sem, local_sem) = refs[24:]
+     held, held_in, held_far, held_near, odq_own, dkv_own, attended, mixed, tiny, tiny_in, send_sem, recv_sem, local_sem) = refs[30:]
     z, yl, x, yh, core = place()
     f32, bf = jnp.float32, jnp.bfloat16
     swapped_place = yl != core
@@ -507,19 +534,21 @@
     fetch = [bring(matrices.at[i], up.at[:, pl.ds(768 * i, 768)]) for i in range(4)]
 
     def piece(p, w, a):
-        if p == 0:
-            return down_w.at[pl.ds(pl.multiple_of(a * 768 + w * 192, 192), 192)]
-        if p == 1:
+        if p < 2:
+            return down_w.at[pl.ds(pl.multiple_of(a * 768 + w * 192, 192), 192), pl.ds(384 * p, 384)]
+        if p == 2:
             return upper.at[pl.ds(pl.multiple_of(w * 192, 192), 192), pl.ds(pl.multiple_of(a * 768, 768), 768)]
-        return lower.at[pl.ds(pl.multiple_of(w * 768 + a * 192, 192), 192), pl.ds(384 * (p - 2), 384)]
+        return lower.at[pl.ds(pl.multiple_of(w * 768 + a * 192, 192), 192), pl.ds(384 * (p - 3), 384)]
 
     def own(p, k, s):
         return piece(p, 2 * s + core, lax.rem(first[p] + (2, 1, 3, 0)[k], 4))
 
     def result(p, a, start, size):
         if p < 2:
-            return (wide_out, upper_out)[p].at[pl.ds(start, size), pl.ds(pl.multiple_of(a * 768, 768), 768)]
-        return lower_out.at[pl.ds(pl.multiple_of(a * 192 + start, 16), size), pl.ds(384 * (p - 2), 384)]
+            return wide_out.at[pl.ds(start, size), pl.ds(pl.multiple_of(a * 768 + 384 * p, 384), 384)]
+        if p == 2:
+            return upper_out.at[pl.ds(start, size), pl.ds(pl.multiple_of(a * 768, 768), 768)]
+        return lower_out.at[pl.ds(pl.multiple_of(a * 192 + start, 16), size), pl.ds(384 * (p - 3), 384)]
 
     first = [x if part[1] else z for part in PARTS]
     second = [z if part[1] else x for part in PARTS]
@@ -642,7 +671,7 @@
         for i, to in enumerate(groups[step]):
             sems["tiny", step, i] = remote(tiny.at[step], tiny_in.at[step, i], to)
 
-    group_one = (1, 2, 3)
+    group_one, group_two = (2, 3, 4), (0, 1)
     for p in group_one:
         swap(p)
     for way in (0, 1):
@@ -681,10 +710,12 @@
     for i in range(3):
         down_w[768 * i:768 * i + 768] = dot(one, mixed[i], 0, 0).astype(bf)
     down_w[2304:] = dot(attended[...], g, 0, 0).astype(bf)
-    swap(0)
+    for p in group_two:
+        swap(p)
     for p in group_one:
         near(p)
-    far(0)
+    for p in group_two:
+        far(p)
     for copy in fetch:
         copy.wait()
     values = tokens[...].astype(f32)
@@ -710,32 +741,41 @@
         mine(p)
     layer_output[...] = (values + mlp[...] + dot(attended[...], up[:, 2304:3072], 1, 0) + vectors[4:5]).astype(bf)
     tiny_stage(1)
-    near(0)
+    for p in group_two:
+        near(p)
     for p in group_one:
         near2(p)
     tiny_stage(2)
-    mine(0)
+    for p in group_two:
+        mine(p)
     for p in group_one:
         mine2(p)
     tiny_stage(3)
     for p in group_one:
         total(p)
-    near2(0)
+    for p in group_two:
+        near2(p)
     for p in group_one:
         relay(p)
-    mine2(0)
+    for p in group_two:
+        mine2(p)
     for p in group_one:
         last(p)
-    total(0)
+    for p in group_two:
+        total(p)
     tiny_stage(4)
-    relay(0)
+    for p in group_two:
+        relay(p)
     for p in group_one:
         end(p)
-    last(0)
+    for p in group_two:
+        last(p)
     for p in group_one:
         close(p)
-    end(0)
-    close(0)
+    for p in group_two:
+        end(p)
+    for p in group_two:
+        close(p)
     for ref, sem in pairs:
         landed(ref, send_sem.at[sem])
     for copy in sent:
@@ -763,7 +803,7 @@
         ((4, ROWS, WIDE), bf), ((4, ROWS, WIDE), bf), plain, ((3, ROWS, 768), bf), ((4, 16, 768), f32), ((4, 3, 16, 768), f32),
     ):
         scratch.append(pltpu.VMEM(shape, kind))
-    scratch += [dma((140,)), dma((140,)), dma((16,))]
+    scratch += [dma((170,)), dma((170,)), dma((16,))]
     rows = jax.ShapeDtypeStruct((ROWS, 768), bf)
     return pl.pallas_call(
         back_kernel,

time: 344 us -> 325 us (0.945)
  Pallas kernels: 298 us -> 284 us
  local copies, waits for them, and re-layouts: 18.1 us -> 10.5 us
    unnamed x37 -> x17, local copies, waits for them, and re-layouts: 11.1 us -> 2.82 us
    pallas_call x1, Pallas kernels: 145 us -> 138 us  [back(): pl.pallas_call(back_kernel, out_shape=(rows, rows, jax.ShapeDtypeStruct((...]
    pallas_call x1, Pallas kernels: 83.2 us -> 76.9 us  [attention(): pl.pallas_call(functools.partial(attn_kernel, chunk), out_shape=(jax.Shap...]
  transfers between devices with their start and end apart: 2 -> 2, of which waited for: 0 -> 1; matrix products, arithmetic and copies ran while one was open for 1% -> 1% of each run, Pallas kernels for 24% -> 24%
where the time goes in v4:
time: 325 us; the launch traced here: 324 us
  Pallas kernels  284 us (87%)
  between operations  14.2 us (4%)
  other arithmetic  12.8 us (4%)
  local copies, waits for them, and re-layouts  10.5 us (3%)
    pallas_call x1, Pallas kernels, back(): pl.pallas_call(back_kernel, out_shape=(rows, rows, jax.ShapeDtypeStruct((...  138 us
    pallas_call x1, Pallas kernels, attention(): pl.pallas_call(functools.partial(attn_kernel, chunk), out_shape=(jax.Shap...  76.9 us
    pallas_call x1, Pallas kernels, front(): pl.pallas_call(front_kernel, out_shape=(jax.ShapeDtypeStruct((32, ROWS, W...  69.5 us
  transfers between devices with their start and end apart: 2, of which 1 were waited for; matrix products, arithmetic and copies ran while one was open for 1% of the time, Pallas kernels for 24%

profile of v4, /device:TPU:0, one launch (start us, length us, event | category | flops | bytes accessed | tf_op | source)
XLA Modules:
  0.0 324.4 jit_solution(4048322980589089052)
XLA Ops:
  7.2 0.0 all-gather.3.cloned.1.call-start
  7.3 0.7 subtract_bitcast_fusion
  7.9 0.7 pad_add_fusion
  8.6 0.1 copy.29
  8.7 0.1 reshape.366
  8.8 0.8 broadcast_select_fusion.2
  9.6 0.1 select_n.147
  9.7 0.1 select_n.149
  9.8 0.1 select_n.151
  9.9 0.1 select_n.153
  10.0 0.1 select_n.155
  10.0 0.8 broadcast_select_fusion.1
  10.8 0.1 select_n.157
  10.9 0.8 broadcast_select_fusion
  11.7 0.2 dynamic-update-slice
  11.9 0.2 dynamic-update-slice.1
  12.1 0.2 dynamic-update-slice.2
  12.3 0.2 dynamic-update-slice.3
  12.5 0.2 dynamic-update-slice.4
  12.7 0.3 dynamic-update-slice.5
  13.0 0.7 reshape.368.vectors_hbm
  13.6 0.1 dynamic-slice_multiply_fusion
  13.7 0.1 convert_bitcast_fusion
  13.8 0.6 fusion.3
  14.4 0.8 pad_maximum_fusion.tables_hbm
  15.1 69.5 %front.1 = (bf16[32,256,384]{2,1,0:T(8,128)(2,1)}, bf16[4,256,384]{2,1,0:T(8,128)(2,1)}, bf16[256,768]{1,0:T(8,128)(2,1)}, bf16[256,768]{1,0:T(8,128)(2,1)}, f32...) custom-call(bf16[256,768]{1,0:T(8,128)(2,1)} %bitcast.22, bf16[256,768]{1,0:T(8,128)(2,1)} %bitcast.24, ...), custom_call_target="tpu_custom_call" | custom-call | tf_op jit(solution)/shard_map/front/pallas_call | solution.py:379
  84.6 0.0 all-gather.3.cloned.1.call-update
  84.7 0.0 all-gather.5.cloned.1.call-start
  84.7 0.7 all-gather.5.cloned.1.call-update
  85.4 0.1 reshape.367
  85.6 0.6 dynamic_slice.15.qpos
  86.1 1.3 scatter_custom_fusion.lay
  87.4 76.9 %attention.1 = (bf16[1024,384]{1,0:T(8,128)(2,1)}, bf16[8192,384]{1,0:T(8,128)(2,1)}) custom-call(s32[8]{0:T(128)} %dynamic_slice.15.qpos, s32[64]{0:T(128)} %scatter_custom_fusion.lay, bf16[1024,384]{1,0:T(8,128)(2,1)} %bitcast.27, bf16[8192,384]{1,0:T(8,128)(2,1)} %bitcast.20), custom_call_target="tpu_custom_call" | custom-call | tf_op jit(solution)/shard_map/attention/pallas_call | solution.py:135
  164.3 0.0 all-gather.3.cloned.1.call-done.up_hbm
  164.4 2.1 all-gather.5.cloned.1.call-done.down_hbm
  166.5 137.6 %back.1 = (bf16[256,768]{1,0:T(8,128)(2,1)}, bf16[256,768]{1,0:T(8,128)(2,1)}, bf16[192,3072]{1,0:T(8,128)(2,1)}, bf16[192,3072]{1,0:T(8,128)(2,1)}, bf16[768,768]{1,0:T(8,128)(2,1)}, /*index=5*/f32[16,768]{1,0:T(8,128)}) custom-call(bf16[4,256,384]{2,1,0:T(8,128)(2,1)} %bitcast.26, bf16[32,256,384]{2,1,0:T(8,128)(2,1)} %bitcast.21, ...), custom_call_target="tpu_custom_call" | custom-call | tf_op jit(solution)/shard_map/back/pallas_call | solution.py:808
  304.1 0.0 copy-start.1
  304.1 2.6 slice_convert_fusion
  306.7 1.8 slice_convert_fusion.1
  308.5 0.0 copy-done.1
  308.5 0.0 copy-start
  308.5 1.7 convert_element_type.44
  310.2 0.0 copy-done
  310.2 0.0 copy-start.3
  310.2 0.0 copy-start.2
  310.2 1.6 convert_element_type.45
  311.8 0.7 slice.27
  312.5 1.3 dynamic-slice_reduce_fusion
  313.9 0.7 dynamic_slice.18
  314.5 1.5 fusion.12
  316.1 0.0 copy-done.3
  316.1 0.7 copy.41
  316.8 0.0 copy-done.2
  316.8 0.7 copy.42
  (11 shorter events, 0.1 us)
Async XLA Ops:
  7.2 157.2 %all-gather.3.cloned.1.call-start = ((), (), s32[]{:S(2)}) async-start(), calls=%async_computation | async-start | bytes 5898240 | tf_op jit(solution)/shard_map/all_gather | solution.py:868
  84.7 81.8 %all-gather.5.cloned.1.call-start = ((), (), s32[]{:S(2)}) async-start(), calls=%async_computation.1 | async-start | bytes 5898240 | tf_op jit(solution)/shard_map/all_gather | solution.py:869
  304.1 4.4 %copy-start.1 = (bf16[192,3072]{1,0:T(8,128)(2,1)S(1)}, bf16[192,3072]{1,0:T(8,128)(2,1)}, u32[]{:S(2)}) copy-start(bf16[192,3072]{1,0:T(8,128)(2,1)} %get-tuple-element.45) | copy-start | bytes 3538948
  308.5 1.7 copy-start
  310.2 5.9 %copy-start.3 = (bf16[256,768]{1,0:T(8,128)(2,1)S(1)}, bf16[256,768]{1,0:T(8,128)(2,1)}, u32[]{:S(2)}) copy-start(bf16[256,768]{1,0:T(8,128)(2,1)} %get-tuple-element.41) | copy-start | bytes 1179652
  310.2 6.6 %copy-start.2 = (bf16[256,768]{1,0:T(8,128)(2,1)S(1)}, bf16[256,768]{1,0:T(8,128)(2,1)}, u32[]{:S(2)}) copy-start(bf16[256,768]{1,0:T(8,128)(2,1)} %get-tuple-element.42) | copy-start | bytes 1179652
Sparse Core Ops, SparseCore 0:
  84.8 39.0 all-gather.2
  125.5 40.9 all-gather.4

commit v5 on v4

--- a/solution.py
+++ b/solution.py
@@ -314,6 +314,17 @@
          lambda lanes: dot(one, weights[1, :, lanes]) + vec[7:8, lanes])
     mine = z * 8 + yl * 4 + x
     sent_kv = exchange(kvs, kv_all.at[mine], kv_send, kv_recv)
+    def slot(zz, cc, d):
+        return kv_all.at[lax.rem(zz, 4) * 8 + cc * 4 + lax.rem(x + 4 - d, 4)]
+
+    half = ROWS // 2
+    up_sem, part_sem, sib_sem = {}, {}, {}
+    for d in (0, 1, 3, 2):
+        here = slot(z, core, d)
+        landed(here, kv_recv.at[d])
+        for way in (0, 1):
+            up_sem[way, d] = remote(here, here, zs[way])
+        sib_sem[0, d] = remote(here, here, sib)
     for i in (2, 3):
         relay(i)
     for i in (2, 3):
@@ -328,17 +339,6 @@
     keep_out = pltpu.make_async_copy(weights, weights_out, local_sem.at[4])
     keep_out.start()
 
-    def slot(zz, cc, d):
-        return kv_all.at[lax.rem(zz, 4) * 8 + cc * 4 + lax.rem(x + 4 - d, 4)]
-
-    half = ROWS // 2
-    up_sem, part_sem, sib_sem = {}, {}, {}
-    for d in (0, 1, 3, 2):
-        here = slot(z, core, d)
-        landed(here, kv_recv.at[d])
-        for way in (0, 1):
-            up_sem[way, d] = remote(here, here, zs[way])
-        sib_sem[0, d] = remote(here, here, sib)
     for d in (0, 1, 3, 2):
         for way in (0, 1):
             here = slot(z + 3 - 2 * way, core, d)
@@ -389,7 +389,7 @@
     )(tokens, grad, tables, qkv, dense, vectors)
 
 
-PARTS = ((384, False), (384, True), (768, True), (384, True), (384, False))
+PARTS = ((384, False), (384, True), (768, True), (384, False), (384, False))
 TILE = 384
 
 
@@ -484,13 +484,6 @@
     inputs = [bring(src, dst) for src, dst in ((two_hbm, normed_two), (grad_hbm, grad), (vectors_hbm, vectors), (up_hbm, up), (down_hbm, down_w),
                                                (tokens_hbm, tokens), (one_hbm, normed_one), (tables_hbm, tables))]
     odq_sem = [exchange(odq, odq_own.at[x], d) for d in range(4)]
-    mlp[...] = jnp.zeros_like(mlp)
-    back_two[...] = jnp.zeros_like(back_two)
-    for copy in inputs:
-        copy.wait()
-    for i in range(4):
-        up_bias[0:1, 768 * i:768 * i + 768] = vectors[8 + i:9 + i]
-
     def feed(t, _):
         at = pl.ds(pl.multiple_of(t * TILE, TILE), TILE)
         values = dot(normed_two[...], up[:, at], 1, 0) + up_bias[0:1, at]
@@ -515,12 +508,17 @@
             return 0
         lax.fori_loop(0, 2 * (chunks[1] - chunks[0]), step, 0)
 
-    lax.fori_loop(0, 1, feed, 0)
     held_load[0].wait()
     arrive(held_in.at[0], held_sem[0])
     sum_held(0, (0, 4), [])
     held_far_sem = [remote(held.at[0, pl.ds(2 * way, 2)], held_far.at[way], zs[way]) for way in (0, 1)]
-    lax.fori_loop(1, 3, feed, 0)
+    mlp[...] = jnp.zeros_like(mlp)
+    back_two[...] = jnp.zeros_like(back_two)
+    for copy in inputs:
+        copy.wait()
+    for i in range(4):
+        up_bias[0:1, 768 * i:768 * i + 768] = vectors[8 + i:9 + i]
+    lax.fori_loop(0, 3, feed, 0)
     held_near_sem = []
     for way in (0, 1):
         k = 1 + way
@@ -712,10 +710,10 @@
     down_w[2304:] = dot(attended[...], g, 0, 0).astype(bf)
     for p in group_two:
         swap(p)
+    for p in group_two:
+        far(p)
     for p in group_one:
         near(p)
-    for p in group_two:
-        far(p)
     for copy in fetch:
         copy.wait()
     values = tokens[...].astype(f32)
@@ -737,12 +735,12 @@
     sums.extend(bias_grad[0:1, 768 * i:768 * i + 768] for i in range(4))
     tiny[0] = jnp.concatenate(sums + [jnp.zeros((4, 768), f32)], 0)
     tiny_stage(0)
+    for p in group_two:
+        near(p)
     for p in group_one:
         mine(p)
     layer_output[...] = (values + mlp[...] + dot(attended[...], up[:, 2304:3072], 1, 0) + vectors[4:5]).astype(bf)
     tiny_stage(1)
-    for p in group_two:
-        near(p)
     for p in group_one:
         near2(p)
     tiny_stage(2)

time: 325 us -> 314 us (0.966)
  Pallas kernels: 284 us -> 273 us
    pallas_call x1, Pallas kernels: 138 us -> 128 us  [back(): pl.pallas_call(back_kernel, out_shape=(rows, rows, jax.ShapeDtypeStruct((...]
  transfers between devices with their start and end apart: 2 -> 2, of which waited for: 1 -> 1; matrix products, arithmetic and copies ran while one was open for 1% -> 1% of each run, Pallas kernels for 24% -> 25%
where the time goes in v5:
time: 314 us
  Pallas kernels  273 us (87%)
  between operations  14.2 us (5%)
  other arithmetic  12.8 us (4%)
  local copies, waits for them, and re-layouts  10.5 us (3%)
    pallas_call x1, Pallas kernels, back(): pl.pallas_call(back_kernel, out_shape=(rows, rows, jax.ShapeDtypeStruct((...  128 us
    pallas_call x1, Pallas kernels, attention(): pl.pallas_call(functools.partial(attn_kernel, chunk), out_shape=(jax.Shap...  76.9 us
    pallas_call x1, Pallas kernels, front(): pl.pallas_call(front_kernel, out_shape=(jax.ShapeDtypeStruct((32, ROWS, W...  68 us
  transfers between devices with their start and end apart: 2, of which 1 were waited for; matrix products, arithmetic and copies ran while one was open for 1% of the time, Pallas kernels for 25%

profile of v5, /device:TPU:0, one launch (start us, length us, event | category | flops | bytes accessed | tf_op | source)
XLA Modules:
  0.0 313.5 jit_solution(5055059133636248235)
XLA Ops:
  7.2 0.0 all-gather.3.cloned.1.call-start
  7.3 0.7 subtract_bitcast_fusion
  7.9 0.7 pad_add_fusion
  8.6 0.1 copy.29
  8.7 0.1 reshape.366
  8.8 0.8 broadcast_select_fusion.2
  9.6 0.1 select_n.147
  9.7 0.1 select_n.149
  9.8 0.1 select_n.151
  9.9 0.1 select_n.153
  10.0 0.1 select_n.155
  10.0 0.8 broadcast_select_fusion.1
  10.8 0.1 select_n.157
  10.9 0.8 broadcast_select_fusion
  11.7 0.2 dynamic-update-slice
  11.9 0.2 dynamic-update-slice.1
  12.1 0.2 dynamic-update-slice.2
  12.3 0.2 dynamic-update-slice.3
  12.5 0.2 dynamic-update-slice.4
  12.7 0.3 dynamic-update-slice.5
  13.0 0.7 reshape.368.vectors_hbm
  13.6 0.1 dynamic-slice_multiply_fusion
  13.7 0.1 convert_bitcast_fusion
  13.8 0.6 fusion.3
  14.4 0.8 pad_maximum_fusion.tables_hbm
  15.1 68.0 %front.1 = (bf16[32,256,384]{2,1,0:T(8,128)(2,1)}, bf16[4,256,384]{2,1,0:T(8,128)(2,1)}, bf16[256,768]{1,0:T(8,128)(2,1)}, bf16[256,768]{1,0:T(8,128)(2,1)}, f32...) custom-call(bf16[256,768]{1,0:T(8,128)(2,1)} %bitcast.22, bf16[256,768]{1,0:T(8,128)(2,1)} %bitcast.24, ...), custom_call_target="tpu_custom_call" | custom-call | tf_op jit(solution)/shard_map/front/pallas_call | solution.py:379
  83.1 0.0 all-gather.3.cloned.1.call-update
  83.2 0.0 all-gather.5.cloned.1.call-start
  83.2 0.7 all-gather.5.cloned.1.call-update
  83.9 0.1 reshape.367
  84.1 0.6 dynamic_slice.15.qpos
  84.6 1.3 scatter_custom_fusion.lay
  85.9 76.9 %attention.1 = (bf16[1024,384]{1,0:T(8,128)(2,1)}, bf16[8192,384]{1,0:T(8,128)(2,1)}) custom-call(s32[8]{0:T(128)} %dynamic_slice.15.qpos, s32[64]{0:T(128)} %scatter_custom_fusion.lay, bf16[1024,384]{1,0:T(8,128)(2,1)} %bitcast.27, bf16[8192,384]{1,0:T(8,128)(2,1)} %bitcast.20), custom_call_target="tpu_custom_call" | custom-call | tf_op jit(solution)/shard_map/attention/pallas_call | solution.py:135
  162.8 0.0 all-gather.3.cloned.1.call-done.up_hbm
  162.8 2.2 all-gather.5.cloned.1.call-done.down_hbm
  165.0 128.2 %back.1 = (bf16[256,768]{1,0:T(8,128)(2,1)}, bf16[256,768]{1,0:T(8,128)(2,1)}, bf16[192,3072]{1,0:T(8,128)(2,1)}, bf16[192,3072]{1,0:T(8,128)(2,1)}, bf16[768,768]{1,0:T(8,128)(2,1)}, /*index=5*/f32[16,768]{1,0:T(8,128)}) custom-call(bf16[4,256,384]{2,1,0:T(8,128)(2,1)} %bitcast.26, bf16[32,256,384]{2,1,0:T(8,128)(2,1)} %bitcast.21, ...), custom_call_target="tpu_custom_call" | custom-call | tf_op jit(solution)/shard_map/back/pallas_call | solution.py:806
  293.2 0.0 copy-start.1
  293.2 2.6 slice_convert_fusion
  295.8 1.8 slice_convert_fusion.1
  297.6 0.0 copy-done.1
  297.6 0.0 copy-start
  297.6 1.7 convert_element_type.44
  299.3 0.0 copy-done
  299.3 0.0 copy-start.3
  299.3 0.0 copy-start.2
  299.3 1.6 convert_element_type.45
  300.9 0.7 slice.27
  301.6 1.3 dynamic-slice_reduce_fusion
  303.0 0.7 dynamic_slice.18
  303.6 1.5 fusion.12
  305.2 0.0 copy-done.3
  305.2 0.7 copy.41
  305.9 0.0 copy-done.2
  305.9 0.7 copy.42
  (11 shorter events, 0.1 us)
Async XLA Ops:
  7.2 155.6 %all-gather.3.cloned.1.call-start = ((), (), s32[]{:S(2)}) async-start(), calls=%async_computation | async-start | bytes 5898240 | tf_op jit(solution)/shard_map/all_gather | solution.py:866
  83.2 81.8 %all-gather.5.cloned.1.call-start = ((), (), s32[]{:S(2)}) async-start(), calls=%async_computation.1 | async-start | bytes 5898240 | tf_op jit(solution)/shard_map/all_gather | solution.py:867
  293.2 4.4 %copy-start.1 = (bf16[192,3072]{1,0:T(8,128)(2,1)S(1)}, bf16[192,3072]{1,0:T(8,128)(2,1)}, u32[]{:S(2)}) copy-start(bf16[192,3072]{1,0:T(8,128)(2,1)} %get-tuple-element.45) | copy-start | bytes 3538948
  297.6 1.7 copy-start
  299.3 5.9 %copy-start.3 = (bf16[256,768]{1,0:T(8,128)(2,1)S(1)}, bf16[256,768]{1,0:T(8,128)(2,1)}, u32[]{:S(2)}) copy-start(bf16[256,768]{1,0:T(8,128)(2,1)} %get-tuple-element.41) | copy-start | bytes 1179652
  299.3 6.6 %copy-start.2 = (bf16[256,768]{1,0:T(8,128)(2,1)S(1)}, bf16[256,768]{1,0:T(8,128)(2,1)}, u32[]{:S(2)}) copy-start(bf16[256,768]{1,0:T(8,128)(2,1)} %get-tuple-element.42) | copy-start | bytes 1179652
Sparse Core Ops, SparseCore 0:
  83.3 39.0 all-gather.2
  124.1 40.9 all-gather.4

commit v6 on v5

--- a/solution.py
+++ b/solution.py
@@ -672,6 +672,8 @@
     group_one, group_two = (2, 3, 4), (0, 1)
     for p in group_one:
         swap(p)
+    for p in group_one:
+        far(p)
     for way in (0, 1):
         arrive(held_near.at[way], held_near_sem[way])
     held_load[3].wait()
@@ -679,7 +681,7 @@
     sum_held(3, (0, 4), [(held_near.at[0], 0), (held_near.at[1], 0)])
     dkv_sem = [exchange(held.at[3], dkv_own.at[x], d) for d in range(4)]
     for p in group_one:
-        far(p)
+        near(p)
     for d in range(4):
         h = lax.rem(x + 4 - d, 4)
         arrive(odq_own.at[h], odq_sem[d])
@@ -712,8 +714,6 @@
         swap(p)
     for p in group_two:
         far(p)
-    for p in group_one:
-        near(p)
     for copy in fetch:
         copy.wait()
     values = tokens[...].astype(f32)
@@ -735,10 +735,10 @@
     sums.extend(bias_grad[0:1, 768 * i:768 * i + 768] for i in range(4))
     tiny[0] = jnp.concatenate(sums + [jnp.zeros((4, 768), f32)], 0)
     tiny_stage(0)
+    for p in group_one:
+        mine(p)
     for p in group_two:
         near(p)
-    for p in group_one:
-        mine(p)
     layer_output[...] = (values + mlp[...] + dot(attended[...], up[:, 2304:3072], 1, 0) + vectors[4:5]).astype(bf)
     tiny_stage(1)
     for p in group_one:

time: 314 us -> 303 us (0.965)
  Pallas kernels: 273 us -> 262 us
    pallas_call x1, Pallas kernels: 128 us -> 117 us  [back(): pl.pallas_call(back_kernel, out_shape=(rows, rows, jax.ShapeDtypeStruct((...]
where the time goes in v6:
time: 303 us; the launch traced here: 302 us
  Pallas kernels  262 us (86%)
  between operations  14.2 us (5%)
  other arithmetic  12.8 us (4%)
  local copies, waits for them, and re-layouts  10.5 us (3%)
    pallas_call x1, Pallas kernels, back(): pl.pallas_call(back_kernel, out_shape=(rows, rows, jax.ShapeDtypeStruct((...  117 us
    pallas_call x1, Pallas kernels, attention(): pl.pallas_call(functools.partial(attn_kernel, chunk), out_shape=(jax.Shap...  76.8 us
    pallas_call x1, Pallas kernels, front(): pl.pallas_call(front_kernel, out_shape=(jax.ShapeDtypeStruct((32, ROWS, W...  68 us
  transfers between devices with their start and end apart: 2, of which 1 were waited for; matrix products, arithmetic and copies ran while one was open for 1% of the time, Pallas kernels for 25%

profile of v6, /device:TPU:0, one launch (start us, length us, event | category | flops | bytes accessed | tf_op | source)
XLA Modules:
  0.0 302.3 jit_solution(5982418237111296714)
XLA Ops:
  7.2 0.0 all-gather.3.cloned.1.call-start
  7.3 0.7 subtract_bitcast_fusion
  7.9 0.7 pad_add_fusion
  8.6 0.1 copy.29
  8.7 0.1 reshape.366
  8.8 0.8 broadcast_select_fusion.2
  9.6 0.1 select_n.147
  9.7 0.1 select_n.149
  9.8 0.1 select_n.151
  9.9 0.1 select_n.153
  10.0 0.1 select_n.155
  10.0 0.8 broadcast_select_fusion.1
  10.8 0.1 select_n.157
  10.9 0.8 broadcast_select_fusion
  11.7 0.2 dynamic-update-slice
  11.9 0.2 dynamic-update-slice.1
  12.1 0.2 dynamic-update-slice.2
  12.3 0.2 dynamic-update-slice.3
  12.5 0.2 dynamic-update-slice.4
  12.7 0.3 dynamic-update-slice.5
  13.0 0.7 reshape.368.vectors_hbm
  13.6 0.1 dynamic-slice_multiply_fusion
  13.7 0.1 convert_bitcast_fusion
  13.8 0.6 fusion.3
  14.4 0.8 pad_maximum_fusion.tables_hbm
  15.1 68.0 %front.1 = (bf16[32,256,384]{2,1,0:T(8,128)(2,1)}, bf16[4,256,384]{2,1,0:T(8,128)(2,1)}, bf16[256,768]{1,0:T(8,128)(2,1)}, bf16[256,768]{1,0:T(8,128)(2,1)}, f32...) custom-call(bf16[256,768]{1,0:T(8,128)(2,1)} %bitcast.22, bf16[256,768]{1,0:T(8,128)(2,1)} %bitcast.24, ...), custom_call_target="tpu_custom_call" | custom-call | tf_op jit(solution)/shard_map/front/pallas_call | solution.py:379
  83.1 0.0 all-gather.3.cloned.1.call-update
  83.2 0.0 all-gather.5.cloned.1.call-start
  83.2 0.7 all-gather.5.cloned.1.call-update
  83.9 0.1 reshape.367
  84.1 0.6 dynamic_slice.15.qpos
  84.6 1.3 scatter_custom_fusion.lay
  85.9 76.8 %attention.1 = (bf16[1024,384]{1,0:T(8,128)(2,1)}, bf16[8192,384]{1,0:T(8,128)(2,1)}) custom-call(s32[8]{0:T(128)} %dynamic_slice.15.qpos, s32[64]{0:T(128)} %scatter_custom_fusion.lay, bf16[1024,384]{1,0:T(8,128)(2,1)} %bitcast.27, bf16[8192,384]{1,0:T(8,128)(2,1)} %bitcast.20), custom_call_target="tpu_custom_call" | custom-call | tf_op jit(solution)/shard_map/attention/pallas_call | solution.py:135
  162.8 0.0 all-gather.3.cloned.1.call-done.up_hbm
  162.8 2.2 all-gather.5.cloned.1.call-done.down_hbm
  165.0 117.0 %back.1 = (bf16[256,768]{1,0:T(8,128)(2,1)}, bf16[256,768]{1,0:T(8,128)(2,1)}, bf16[192,3072]{1,0:T(8,128)(2,1)}, bf16[192,3072]{1,0:T(8,128)(2,1)}, bf16[768,768]{1,0:T(8,128)(2,1)}, /*index=5*/f32[16,768]{1,0:T(8,128)}) custom-call(bf16[4,256,384]{2,1,0:T(8,128)(2,1)} %bitcast.26, bf16[32,256,384]{2,1,0:T(8,128)(2,1)} %bitcast.21, ...), custom_call_target="tpu_custom_call" | custom-call | tf_op jit(solution)/shard_map/back/pallas_call | solution.py:806
  282.0 0.0 copy-start.1
  282.0 2.6 slice_convert_fusion
  284.6 1.8 slice_convert_fusion.1
  286.4 0.0 copy-done.1
  286.4 0.0 copy-start
  286.4 1.7 convert_element_type.44
  288.1 0.0 copy-done
  288.1 0.0 copy-start.3
  288.1 0.0 copy-start.2
  288.1 1.6 convert_element_type.45
  289.6 0.7 slice.27
  290.4 1.3 dynamic-slice_reduce_fusion
  291.7 0.7 dynamic_slice.18
  292.4 1.5 fusion.12
  294.0 0.0 copy-done.3
  294.0 0.7 copy.41
  294.7 0.0 copy-done.2
  294.7 0.7 copy.42
  (11 shorter events, 0.1 us)
Async XLA Ops:
  7.2 155.6 %all-gather.3.cloned.1.call-start = ((), (), s32[]{:S(2)}) async-start(), calls=%async_computation | async-start | bytes 5898240 | tf_op jit(solution)/shard_map/all_gather | solution.py:866
  83.2 81.8 %all-gather.5.cloned.1.call-start = ((), (), s32[]{:S(2)}) async-start(), calls=%async_computation.1 | async-start | bytes 5898240 | tf_op jit(solution)/shard_map/all_gather | solution.py:867
  282.0 4.4 %copy-start.1 = (bf16[192,3072]{1,0:T(8,128)(2,1)S(1)}, bf16[192,3072]{1,0:T(8,128)(2,1)}, u32[]{:S(2)}) copy-start(bf16[192,3072]{1,0:T(8,128)(2,1)} %get-tuple-element.45) | copy-start | bytes 3538948
  286.4 1.7 copy-start
  288.1 5.9 %copy-start.3 = (bf16[256,768]{1,0:T(8,128)(2,1)S(1)}, bf16[256,768]{1,0:T(8,128)(2,1)}, u32[]{:S(2)}) copy-start(bf16[256,768]{1,0:T(8,128)(2,1)} %get-tuple-element.41) | copy-start | bytes 1179652
  288.1 6.6 %copy-start.2 = (bf16[256,768]{1,0:T(8,128)(2,1)S(1)}, bf16[256,768]{1,0:T(8,128)(2,1)}, u32[]{:S(2)}) copy-start(bf16[256,768]{1,0:T(8,128)(2,1)} %get-tuple-element.42) | copy-start | bytes 1179652
Sparse Core Ops, SparseCore 0:
  83.3 39.0 all-gather.2
  124.1 40.9 all-gather.4
